TPU v7x, 32 devices: a whole 2x2x4 slice. The times are simulated.
32 devices in a mesh: load: 2 (over core), brick: 16 (over z, y, x).
Axes of the slice: x: 2, y: 2, z: 4, core: 2. Of those that a mesh axis runs over, the one named last changes fastest.
Arguments:
- density: float32 [192, 64, 128], P('brick'), may hold values from 0.1 to 0.95
- passive: int32 [192, 64, 128], P('brick'), may hold values from 0 to 2, as said below
- support: int32 [192, 64, 128], P('brick'), may hold values 0 or 1
- load_nodes: int32 [4, 64], P('load'), may hold values from 0 to 1572863
- load_force: float32 [4, 64], P('load'), may hold values from -6 to 6
- self_weight: float32 [4], P('load'), may hold values from 0.3 to 3
- body_force: float32 [4, 192, 64, 128], P('load', 'brick'), may hold values from -3 to 3
Outputs:
- new_density: float32 [192, 64, 128], P('brick', 'load')
- momentum: float32 [192, 64, 128], P('brick', 'load')
- displacement: float32 [4, 192, 64, 128], P('load', 'brick')
Inputs may be any that keep to these rules, and one draw needn't show every extreme that they name: 0 marks a design voxel, 1 a passive void voxel, 2 a passive solid voxel.
All inputs are finite; a program needn't handle non-finite values. No bound on the sum of `support` on one device may be relied on, other than what follows from the above.
Results may differ from a plain program's by a relative error of at most 0.0001.
Values sent between devices are 32-bit elements; how exact they have to be, the bound alone decides.
No kernel may reach another device: no remote copies, remote signals or barrier semaphores. Data moves between devices by JAX's collectives and lax.ppermute only.
A program may use at most 64 MiB of HBM per device.

v0:
```python
import jax
import jax.numpy as jnp
from jax import lax
from jax.sharding import PartitionSpec as P

SWEEPS = 5
DESIGN_ITERS = 2


stiff_floor = 0.01
mass_shift = 0.1
spectrum_low = 0.05
spectrum_high = 2.0
moment_decay = 0.8
step_size = 0.1
volume_pull = 0.5
volume_target = 0.4
density_floor = 0.001


def padded_2(block, sides, width):
    for axis, dim in sides:
        count = lax.axis_size(axis)
        forward = [(i, i + 1) for i in range(count - 1)]
        backward = [(target, source) for source, target in forward]
        low = lax.ppermute(
            lax.slice_in_dim(block, block.shape[dim] - width, None, axis=dim), axis, forward
        )
        high = lax.ppermute(lax.slice_in_dim(block, 0, width, axis=dim), axis, backward)
        block = jnp.concatenate([low, block, high], axis=dim)
    return block


def neighbours(padded):
    return (
        padded[..., 2:, 1:-1, 1:-1],
        padded[..., :-2, 1:-1, 1:-1],
        padded[..., 1:-1, 2:, 1:-1],
        padded[..., 1:-1, :-2, 1:-1],
        padded[..., 1:-1, 1:-1, 2:],
        padded[..., 1:-1, 1:-1, :-2],
    )


def pad_sides(vector, leading):
    return jnp.pad(vector, ((0, 0),) * (leading + 1) + ((1, 1), (1, 1)))


def wide_pad(vector):
    return jnp.pad(vector, ((0, 0), (1, 1), (1, 1), (1, 1)))


def passive_apply(design, passive):
    return jnp.where(passive == 1, density_floor, jnp.where(passive == 2, 1.0, design))


def operate(vector, free_mask, stiffness, face_list, padded_free):
    freed = padded_free[..., 1:-1, 1:-1, 1:-1]
    accumulated = mass_shift * stiffness * freed
    for face_weight, beside in zip(face_list, neighbours(padded_free)):
        accumulated = accumulated + face_weight * (freed - beside)
    return free_mask * accumulated + (1.0 - free_mask) * vector


def chebyshev(source, free_mask, stiffness, face_list, diagonal, pad_fn):
    centre = 0.5 * (spectrum_high + spectrum_low)
    half_width = 0.5 * (spectrum_high - spectrum_low)
    ratio_one = centre / half_width
    previous = 1.0 / ratio_one
    solution = jnp.zeros_like(source)
    residual = source
    direction = residual / diagonal / centre
    for sweep_index in range(SWEEPS):
        solution = solution + direction
        if sweep_index < SWEEPS - 1:
            applied = operate(
                direction, free_mask, stiffness, face_list, pad_fn(free_mask * direction)
            )
            residual = residual - applied
            current = 1.0 / (2.0 * ratio_one - previous)
            direction = current * previous * direction + 2.0 * current / half_width * (
                residual / diagonal
            )
            previous = current
    return solution


def load_energy(freed, padded):
    energy = mass_shift * freed * freed
    for beside in neighbours(padded):
        energy = energy + 0.25 * (freed - beside) ** 2
    return energy


def inside_count(start_x, start_y, grid_shape, total_shape):
    along_x = start_x + lax.broadcasted_iota(jnp.int32, grid_shape, 0)
    along_y = start_y + lax.broadcasted_iota(jnp.int32, grid_shape, 1)
    along_z = lax.broadcasted_iota(jnp.int32, grid_shape, 2)
    edges = (
        (along_x == 0).astype(jnp.float32)
        + (along_x == total_shape[0] - 1).astype(jnp.float32)
        + (along_y == 0).astype(jnp.float32)
        + (along_y == total_shape[1] - 1).astype(jnp.float32)
        + (along_z == 0).astype(jnp.float32)
        + (along_z == total_shape[2] - 1).astype(jnp.float32)
    )
    return 6.0 - edges


def filter_field(sensitivity, padded, neighbour_count):
    accumulated = 2.0 * sensitivity
    for beside in neighbours(padded):
        accumulated = accumulated + beside
    return accumulated / (2.0 + neighbour_count)


def design_step(design, momentum, passive, abs_total, density_total, total_cells):
    mean_step = abs_total / total_cells + 1e-06
    mean_density = density_total / total_cells
    moved = design - step_size * momentum / mean_step - volume_pull * (mean_density - volume_target)
    return passive_apply(jnp.clip(moved, density_floor, 1.0), passive)


def place_points(load_nodes, load_force, first_x, rows_x, size_y, size_z):
    loads_here = load_nodes.shape[0]
    span_cells = rows_x * size_y * size_z
    local_ids = load_nodes - first_x * size_y * size_z
    inside = (local_ids >= 0) & (local_ids < span_cells)
    slot_ids = jnp.where(inside, local_ids, span_cells)
    row_ids = lax.broadcasted_iota(jnp.int32, load_nodes.shape, 0)
    points = (
        jnp.zeros((loads_here, span_cells + 1), jnp.float32).at[row_ids, slot_ids].add(load_force)
    )
    return points[:, :span_cells].reshape(loads_here, rows_x, size_y, size_z)


def face_terms(stiffness, padded, free_mask):
    face_list = tuple((0.5 * (stiffness + beside) for beside in neighbours(padded)))
    face_total = face_list[0]
    for face_weight in face_list[1:]:
        face_total = face_total + face_weight
    diagonal = free_mask * (face_total + mass_shift * stiffness) + (1.0 - free_mask)
    return (face_list, diagonal)


def body(density, passive, support, load_nodes, load_force, self_weight, body_force):
    cells_x, size_y, size_z = density.shape
    brick_count = lax.axis_size("brick")
    brick_index = lax.axis_index("brick")
    load_count = lax.axis_size("load")
    load_index = lax.axis_index("load")
    slab_rows = size_y // load_count
    slab_start = load_index * slab_rows
    total_cells = cells_x * brick_count * size_y * size_z
    free_mask = (1 - support).astype(jnp.float32)
    design = passive_apply(density, passive)
    widen = SWEEPS + 1
    free_wide = padded_2(free_mask, (("brick", 0),), widen)
    force_wide = padded_2(body_force, (("brick", 1),), widen)
    wide_shape = free_wide.shape
    along_x = brick_index * cells_x - widen + lax.broadcasted_iota(jnp.int32, wide_shape, 0)
    valid_wide = ((along_x >= 0) & (along_x < cells_x * brick_count)).astype(jnp.float32)
    points = place_points(
        load_nodes, load_force, brick_index * cells_x - widen, cells_x + 2 * widen, size_y, size_z
    )
    design_here = design
    start_y = 0
    momentum = jnp.zeros_like(design_here)
    neighbour_count = inside_count(
        brick_index * cells_x, start_y, design_here.shape, (cells_x * brick_count, size_y, size_z)
    )
    displacement = None
    for iteration in range(DESIGN_ITERS):
        design_wide = padded_2(design, (("brick", 0),), widen)
        stiffness = valid_wide * (stiff_floor + (1.0 - stiff_floor) * design_wide**3)
        face_list, diagonal = face_terms(stiffness, jnp.pad(stiffness, 1), free_wide)
        source = free_wide * (points + self_weight[:, None, None, None] * design_wide + force_wide)
        solution = chebyshev(source, free_wide, stiffness, face_list, diagonal, wide_pad)
        freed = free_wide * solution
        energy_wide = load_energy(freed, wide_pad(freed))
        local_energy = jnp.sum(energy_wide[:, widen : widen + cells_x], axis=0)
        displacement = solution[:, widen : widen + cells_x]
        energy = lax.psum(local_energy, "load")
        sensitivity = -3.0 * (1.0 - stiff_floor) * design_here * design_here * energy
        padded = pad_sides(padded_2(sensitivity, (("brick", 0),), 1), 0)
        filtered = filter_field(sensitivity, padded, neighbour_count)
        momentum = moment_decay * momentum + filtered
        abs_total, density_total = lax.psum(
            (jnp.sum(jnp.abs(momentum)), jnp.sum(design_here)), "brick"
        )
        design_here = design_step(
            design_here, momentum, passive, abs_total, density_total, total_cells
        )
        design = design_here
    return (
        lax.dynamic_slice_in_dim(design_here, slab_start, slab_rows, 1),
        lax.dynamic_slice_in_dim(momentum, slab_start, slab_rows, 1),
        displacement,
    )


def solution(mesh):
    placed = (
        P("brick", None, None),
        P("brick", None, None),
        P("brick", None, None),
        P("load", None),
        P("load", None),
        P("load"),
        P("load", "brick", None, None),
    )
    return jax.shard_map(
        body,
        mesh=mesh,
        in_specs=placed,
        out_specs=(
            P("brick", "load", None),
            P("brick", "load", None),
            P("load", "brick", None, None),
        ),
        check_vma=False,
    )
```

profile of v0, /device:TPU:0, one launch (start us, length us, event | category | flops | bytes accessed | tf_op | source)
XLA Modules:
  0.0 262.0 jit_solution(8944874889715102151)
XLA Ops:
  7.2 2.7 %fusion.273 = (f32[]{:T(128)}, f32[12,64,128]{2,1,0:T(8,128)S(1)}, pred[12,64,128]{2,1,0:T(8,128)(4,1)}, pred[12,64,128]{2,1,0:T(8,128)(4,1)}) fusion(f32[12,64,128]{2,1,0:T(8,128)} %param.7, s32[12,64,128]{2,1,0:T(8,128)} %param.8), kind=kLoop, calls=%fused_computation.429 | loop fusion | flops 491519 | bytes 1376260 | tf_op jit(solution)/shard_map/reduce_sum | solution.py:189
  10.7 5.5 %collective-permute-start.2 = (f32[6,64,128]{2,1,0:T(8,128)}, f32[6,64,128]{2,1,0:T(8,128)}, u32[]{:S(2)}, u32[]{:S(2)}) collective-permute-start(f32[6,64,128]{2,1,0:T(8,128)} %get-tuple-element.83), channel_id=1, source_target_pairs={{0,1},{1,2},{2,3},{3,4},{4,5},{5,6},{6,7},{7,8},{8,9},{9,10},{10,1... | collective-permute-start | bytes 589832 | tf_op jit(solution)/shard_map/ppermute | solution.py:26
  18.4 5.2 %collective-permute-start = (f32[6,64,128]{2,1,0:T(8,128)}, f32[6,64,128]{2,1,0:T(8,128)}, u32[]{:S(2)}, u32[]{:S(2)}) collective-permute-start(f32[6,64,128]{2,1,0:T(8,128)} %get-tuple-element.85), channel_id=1, source_target_pairs={{0,1},{1,2},{2,3},{3,4},{4,5},{5,6},{6,7},{7,8},{8,9},{9,10},{10,1... | collective-permute-start | bytes 589832 | tf_op jit(solution)/shard_map/ppermute | solution.py:26
  25.9 5.3 %collective-permute-start.4 = (f32[2,6,64,128]{3,2,1,0:T(8,128)}, f32[2,6,64,128]{3,2,1,0:T(8,128)}, u32[]{:S(2)}, u32[]{:S(2)}) collective-permute-start(f32[2,6,64,128]{3,2,1,0:T(8,128)} %get-tuple-element.75), channel_id=1, source_target_pairs={{0,1},{1,2},{2,3},{3,4},{4,5},{5,6},{6,7},{7,8},{8,9},{9,10},{10,1... | collective-permute-start | bytes 1179656 | tf_op jit(solution)/shard_map/ppermute | solution.py:26
  31.8 7.0 %scatter_fusion = f32[2,196609]{1,0:T(2,128)S(1)} fusion(f32[2,196609]{1,0:T(2,128)S(1)} %broadcast_in_dim.19, s32[128]{0:T(128)S(1)} %reshape.152, f32[128]{0:T(128)S(1)} %reshape.154), kind=kCustom, calls=%fused_computation | custom fusion | flops 128 | bytes 2560 | tf_op jit(solution)/shard_map/scatter-add | solution.py:132
  47.3 4.0 %collective-permute-done.5 = f32[2,6,64,128]{3,2,1,0:T(8,128)S(1)} collective-permute-done((f32[2,6,64,128]{3,2,1,0:T(8,128)S(1)}, f32[2,6,64,128]{3,2,1,0:T(8,128)S(1)}, u32[]{:S(2)}, u32[]{:S(2)}) %collective-permute-start.5) | collective-permute-done | bytes 393248 | tf_op jit(solution)/shard_map/ppermute | solution.py:29
  52.5 3.2 %broadcast_multiply_fusion.6 = (f32[2,24,64,128]{3,2,1,0:T(8,128)S(1)}, f32[2,24,64,128]{3,2,1,0:T(8,128)S(1)}) fusion(f32[24,64,128]{2,1,0:T(8,128)S(1)} %pad_maximum_fusion, f32[24,64,128]{2,1,0:T(8,128)S(1)} %get-tuple-element.51, f32[2,24,64,128]{3,2,1,0:T(8,128)S(1)} %get-tuple-element.50, f32[24,64,128]{2,1,0:T(8,128)S(1)} %get-tuple-element.72, ...), kind=kLoop, calls=%fused_computation.364 | loop fusion | flops 12582912 | bytes 18087944 | tf_op jit(solution)/shard_map/mul | solution.py:77
  55.8 2.7 %broadcast_multiply_fusion.5 = (f32[2,24,64,128]{3,2,1,0:T(8,128)S(1)}, f32[2,24,64,128]{3,2,1,0:T(8,128)S(1)}, f32[2,24,64,128]{3,2,1,0:T(8,128)S(1)}) fusion(f32[24,64,128]{2,1,0:T(8,128)S(1)} %pad_maximum_fusion, f32[2,24,64,128]{3,2,1,0:T(8,128)S(1)} %get-tuple-element.46, f32[24,64,128]{2,1,0:T(8,128)S(1)} %get-tuple-element.51, ...), kind=kLoop, calls=%fused_computation.363 | loop fusion | flops 12582912 | bytes 17301504 | tf_op jit(solution)/shard_map/mul | solution.py:77
  58.4 2.7 %fusion.182 = (f32[2,24,64,128]{3,2,1,0:T(8,128)S(1)}, f32[2,24,64,128]{3,2,1,0:T(8,128)S(1)}) fusion(f32[2,24,64,128]{3,2,1,0:T(8,128)S(1)} %get-tuple-element.43, f32[24,64,128]{2,1,0:T(8,128)S(1)} %get-tuple-element.51, f32[24,64,128]{2,1,0:T(8,128)S(1)} %pad_maximum_fusion, f32[2,24,64,128]{3,2,1,0:T(8,128)S(1)} %get-tuple-element.44, ...), kind=kLoop, calls=%fused_computation.274 | loop fusion | flops 11010048 | bytes 15728640 | tf_op jit(solution)/shard_map/mul | solution.py:77
  61.1 3.2 %multiply_multiply_fusion.1 = (f32[2,24,64,128]{3,2,1,0:T(8,128)S(1)}, f32[2,24,64,128]{3,2,1,0:T(8,128)S(1)}) fusion(f32[2,24,64,128]{3,2,1,0:T(8,128)S(1)} %get-tuple-element.41, f32[24,64,128]{2,1,0:T(8,128)S(1)} %get-tuple-element.71, f32[2,24,64,128]{3,2,1,0:T(8,128)S(1)} %get-tuple-element.40, f32[24,64,128]{2,1,0:T(8,128)S(1)} %get-tuple-element.57, ...), kind=kLoop, calls=%fused_computation.74 | loop fusion | flops 16908288 | bytes 18874368 | tf_op jit(solution)/shard_map/mul | solution.py:89
  64.3 3.4 %fusion.87 = (f32[2,24,64,128]{3,2,1,0:T(8,128)S(1)}, f32[2,24,64,128]{3,2,1,0:T(8,128)S(1)}, f32[2,24,64,128]{3,2,1,0:T(8,128)S(1)}, f32[2,24,64,128]{3,2,1,0:T...) fusion(f32[2,24,64,128]{3,2,1,0:T(8,128)S(1)} %get-tuple-element.39), kind=kLoop, calls=%fused_computation.162 | loop fusion | flops 2359296 | bytes 11010048 | tf_op jit(solution)/shard_map/mul | solution.py:91
  67.7 2.9 %fusion.233 = f32[12,64,128]{2,1,0:T(8,128)} fusion(f32[2,24,64,128]{3,2,1,0:T(8,128)} %get-tuple-element.68, f32[2,24,64,128]{3,2,1,0:T(8,128)S(1)} %get-tuple-element.67, f32[2,24,64,128]{3,2,1,0:T(8,128)} %get-tuple-element.69, f32[2,24,64,128]{3,2,1,0:T(8,128)S(1)} %get-tuple-element.39, f32[2,24,64,128]{3,2,1,0:T(8,128)S(1)} %get-tuple-element.65, ...), kind=kLoop, calls=%fused_computation.336 | loop fusion | flops 3637248 | bytes 6684672 | tf_op jit(solution)/shard_map/reduce_sum | solution.py:181
  71.3 21.5 %all-reduce.19.cloned.1.call-done = f32[12,64,128]{2,1,0:T(8,128)} async-done(((f32[12,64,128]{2,1,0:T(8,128)}), f32[12,64,128]{2,1,0:T(8,128)}) %all-reduce.19.cloned.1.call-update) | async-done | bytes 393232 | tf_op jit(solution)/shard_map/psum | solution.py:183
  95.3 4.7 %collective-permute-start.7 = (f32[1,64,128]{2,1,0:T(8,128)S(1)}, f32[1,64,128]{2,1,0:T(8,128)S(1)}, u32[]{:S(2)}, u32[]{:S(2)}) collective-permute-start(f32[1,64,128]{2,1,0:T(8,128)S(1)} %get-tuple-element.81), channel_id=1, source_target_pairs={{0,1},{1,2},{2,3},{3,4},{4,5},{5,6},{6,7},{7,8},{8,9},{9,10},{10,1... | collective-permute-start | bytes 98312 | tf_op jit(solution)/shard_map/ppermute | solution.py:26
  103.6 43.6 %all-reduce.15 = (f32[]{:T(128)}, f32[]{:T(128)}) all-reduce(f32[]{:T(128)} %get-tuple-element.34, f32[]{:T(128)} %get-tuple-element.32), channel_id=1, replica_groups=mesh['load'=2,'brick'=16] {'brick'}, use_global_device_ids=true, to_apply=%region_6.7 | all-reduce | flops 2 | bytes 16 | tf_op jit(solution)/shard_map/psum | solution.py:188
  153.1 4.0 %collective-permute-done.8 = f32[6,64,128]{2,1,0:T(8,128)S(1)} collective-permute-done((f32[6,64,128]{2,1,0:T(8,128)S(1)}, f32[6,64,128]{2,1,0:T(8,128)S(1)}, u32[]{:S(2)}, u32[]{:S(2)}) %collective-permute-start.8) | collective-permute-done | bytes 196640 | tf_op jit(solution)/shard_map/ppermute | solution.py:26
  163.6 3.2 %broadcast_multiply_fusion.3 = (f32[2,24,64,128]{3,2,1,0:T(8,128)S(1)}, f32[2,24,64,128]{3,2,1,0:T(8,128)S(1)}) fusion(f32[24,64,128]{2,1,0:T(8,128)S(1)} %pad_maximum_fusion, f32[24,64,128]{2,1,0:T(8,128)S(1)} %get-tuple-element.25, f32[2,24,64,128]{3,2,1,0:T(8,128)S(1)} %get-tuple-element.24, f32[24,64,128]{2,1,0:T(8,128)S(1)} %copy-done.8, ...), kind=kLoop, calls=%fused_computation.361 | loop fusion | flops 12582912 | bytes 18087944 | tf_op jit(solution)/shard_map/mul | solution.py:77
  166.8 2.7 %broadcast_multiply_fusion.2 = (f32[2,24,64,128]{3,2,1,0:T(8,128)S(1)}, f32[2,24,64,128]{3,2,1,0:T(8,128)S(1)}, f32[2,24,64,128]{3,2,1,0:T(8,128)S(1)}) fusion(f32[24,64,128]{2,1,0:T(8,128)S(1)} %pad_maximum_fusion, f32[2,24,64,128]{3,2,1,0:T(8,128)S(1)} %get-tuple-element.20, f32[24,64,128]{2,1,0:T(8,128)S(1)} %get-tuple-element.25, ...), kind=kLoop, calls=%fused_computation.360 | loop fusion | flops 12582912 | bytes 17301504 | tf_op jit(solution)/shard_map/mul | solution.py:77
  172.2 4.0 %multiply_multiply_fusion = (f32[2,24,64,128]{3,2,1,0:T(8,128)S(1)}, f32[2,24,64,128]{3,2,1,0:T(8,128)S(1)}, f32[2,24,64,128]{3,2,1,0:T(8,128)}) fusion(f32[24,64,128]{2,1,0:T(8,128)S(1)} %pad_maximum_fusion, f32[2,24,64,128]{3,2,1,0:T(8,128)S(1)} %get-tuple-element.15, f32[24,64,128]{2,1,0:T(8,128)S(1)} %get-tuple-element.71, ...), kind=kLoop, calls=%fused_computation.73 | loop fusion | flops 16908288 | bytes 20447232 | tf_op jit(solution)/shard_map/mul | solution.py:89
  176.2 3.1 %fusion.178 = (f32[2,24,64,128]{3,2,1,0:T(8,128)S(1)}, f32[2,24,64,128]{3,2,1,0:T(8,128)S(1)}, f32[2,24,64,128]{3,2,1,0:T(8,128)S(1)}, f32[2,24,64,128]{3,2,1,0:...) fusion(f32[2,24,64,128]{3,2,1,0:T(8,128)S(1)} %get-tuple-element.12), kind=kLoop, calls=%fused_computation.253 | loop fusion | flops 2359296 | bytes 11010048 | tf_op jit(solution)/shard_map/mul | solution.py:91
  179.3 2.7 %fusion.220 = f32[12,64,128]{2,1,0:T(8,128)} fusion(f32[2,24,64,128]{3,2,1,0:T(8,128)S(1)} %get-tuple-element.62, f32[2,24,64,128]{3,2,1,0:T(8,128)S(1)} %get-tuple-element.61, f32[2,24,64,128]{3,2,1,0:T(8,128)} %get-tuple-element.63, f32[2,24,64,128]{3,2,1,0:T(8,128)S(1)} %get-tuple-element.12, f32[2,24,64,128]{3,2,1,0:T(8,128)S(1)} %get-tuple-element.59, ...), kind=kLoop, calls=%fused_computation.317 | loop fusion | flops 3637248 | bytes 6684672 | tf_op jit(solution)/shard_map/reduce_sum | solution.py:181
  182.0 15.2 %all-reduce.21.cloned.1.call-done = f32[12,64,128]{2,1,0:T(8,128)} async-done(((f32[12,64,128]{2,1,0:T(8,128)}), f32[12,64,128]{2,1,0:T(8,128)}) %all-reduce.21.cloned.1.call-update) | async-done | bytes 393232 | tf_op jit(solution)/shard_map/psum | solution.py:183
  199.7 4.5 %collective-permute-start.11 = (f32[1,64,128]{2,1,0:T(8,128)S(1)}, f32[1,64,128]{2,1,0:T(8,128)S(1)}, u32[]{:S(2)}, u32[]{:S(2)}) collective-permute-start(f32[1,64,128]{2,1,0:T(8,128)S(1)} %get-tuple-element.77), channel_id=1, source_target_pairs={{0,1},{1,2},{2,3},{3,4},{4,5},{5,6},{6,7},{7,8},{8,9},{9,10},{10,1... | collective-permute-start | bytes 98312 | tf_op jit(solution)/shard_map/ppermute | solution.py:26
  208.9 43.4 %all-reduce.14 = (f32[]{:T(128)}, f32[]{:T(128)}) all-reduce(f32[]{:T(128)} %get-tuple-element.9, f32[]{:T(128)} %get-tuple-element.7), channel_id=1, replica_groups=mesh['load'=2,'brick'=16] {'brick'}, use_global_device_ids=true, to_apply=%region_12.13 | all-reduce | flops 2 | bytes 16 | tf_op jit(solution)/shard_map/psum | solution.py:188
  (110 shorter events, 44.1 us)
Async XLA Ops:
  7.2 10.4 %copy-start.14 = (s32[12,64,128]{2,1,0:T(8,128)S(1)}, s32[12,64,128]{2,1,0:T(8,128)}, u32[]{:S(2)}) copy-start(s32[12,64,128]{2,1,0:T(8,128)} %param.9) | copy-start | bytes 1179652
  7.2 17.8 %copy-start.10 = (f32[2,12,64,128]{3,2,1,0:T(8,128)S(1)}, f32[2,12,64,128]{3,2,1,0:T(8,128)}, u32[]{:S(2)}) copy-start(f32[2,12,64,128]{3,2,1,0:T(8,128)} %param.13) | copy-start | bytes 2359300
  7.2 85.6 %all-reduce.19.cloned.1.call-start = ((), (), s32[]{:S(2)}) async-start(), calls=%async_computation | async-start | bytes 786432 | tf_op jit(solution)/shard_map/psum | solution.py:183
  9.9 31.3 %copy-start.2 = (f32[12,64,128]{2,1,0:T(8,128)}, f32[12,64,128]{2,1,0:T(8,128)S(1)}, u32[]{:S(2)}) copy-start(f32[12,64,128]{2,1,0:T(8,128)S(1)} %get-tuple-element.35) | copy-start | bytes 1179652
  10.7 28.5 %collective-permute-start.2 = (f32[6,64,128]{2,1,0:T(8,128)}, f32[6,64,128]{2,1,0:T(8,128)}, u32[]{:S(2)}, u32[]{:S(2)}) collective-permute-start(f32[6,64,128]{2,1,0:T(8,128)} %get-tuple-element.83), channel_id=1, source_target_pairs={{0,1},{1,2},{2,3},{3,4},{4,5},{5,6},{6,7},{7,8},{8,9},{9,10},{10,1... | collective-permute-start | bytes 589832 | tf_op jit(solution)/shard_map/ppermute | solution.py:26
  16.2 15.0 %copy-start.23 = (s32[2,64]{1,0:T(2,128)S(1)}, s32[2,64]{1,0:T(2,128)}, u32[]{:S(2)}) copy-start(s32[2,64]{1,0:T(2,128)} %param.10) | copy-start | bytes 1540
  16.2 15.1 %copy-start.24 = (f32[2,64]{1,0:T(2,128)S(1)}, f32[2,64]{1,0:T(2,128)}, u32[]{:S(2)}) copy-start(f32[2,64]{1,0:T(2,128)} %param.11) | copy-start | bytes 1540
  16.2 25.1 %collective-permute-start.3 = (f32[6,64,128]{2,1,0:T(8,128)S(1)}, f32[6,64,128]{2,1,0:T(8,128)}, u32[]{:S(2)}, u32[]{:S(2)}) collective-permute-start(f32[6,64,128]{2,1,0:T(8,128)S(1)} %get-tuple-element.84), channel_id=1, source_target_pairs={{1,0},{2,1},{3,2},{4,3},{5,4},{6,5},{7,6},{8,7},{9,8},{10,9},{11,1... | collective-permute-start | bytes 589832 | tf_op jit(solution)/shard_map/ppermute | solution.py:29
  18.4 24.1 %collective-permute-start = (f32[6,64,128]{2,1,0:T(8,128)}, f32[6,64,128]{2,1,0:T(8,128)}, u32[]{:S(2)}, u32[]{:S(2)}) collective-permute-start(f32[6,64,128]{2,1,0:T(8,128)} %get-tuple-element.85), channel_id=1, source_target_pairs={{0,1},{1,2},{2,3},{3,4},{4,5},{5,6},{6,7},{7,8},{8,9},{9,10},{10,1... | collective-permute-start | bytes 589832 | tf_op jit(solution)/shard_map/ppermute | solution.py:26
  23.7 18.9 %collective-permute-start.1 = (f32[6,64,128]{2,1,0:T(8,128)}, f32[6,64,128]{2,1,0:T(8,128)}, u32[]{:S(2)}, u32[]{:S(2)}) collective-permute-start(f32[6,64,128]{2,1,0:T(8,128)} %get-tuple-element.86), channel_id=1, source_target_pairs={{1,0},{2,1},{3,2},{4,3},{5,4},{6,5},{7,6},{8,7},{9,8},{10,9},{11,1... | collective-permute-start | bytes 589832 | tf_op jit(solution)/shard_map/ppermute | solution.py:29
  25.9 20.3 %collective-permute-start.4 = (f32[2,6,64,128]{3,2,1,0:T(8,128)}, f32[2,6,64,128]{3,2,1,0:T(8,128)}, u32[]{:S(2)}, u32[]{:S(2)}) collective-permute-start(f32[2,6,64,128]{3,2,1,0:T(8,128)} %get-tuple-element.75), channel_id=1, source_target_pairs={{0,1},{1,2},{2,3},{3,4},{4,5},{5,6},{6,7},{7,8},{8,9},{9,10},{10,1... | collective-permute-start | bytes 1179656 | tf_op jit(solution)/shard_map/ppermute | solution.py:26
  40.0 11.3 %collective-permute-start.5 = (f32[2,6,64,128]{3,2,1,0:T(8,128)S(1)}, f32[2,6,64,128]{3,2,1,0:T(8,128)S(1)}, u32[]{:S(2)}, u32[]{:S(2)}) collective-permute-start(f32[2,6,64,128]{3,2,1,0:T(8,128)S(1)} %copy-done.15), channel_id=1, source_target_pairs={{1,0},{2,1},{3,2},{4,3},{5,4},{6,5},{7,6},{8,7},{9,8},{10,9},{11,1... | collective-permute-start | bytes 1179656 | tf_op jit(solution)/shard_map/ppermute | solution.py:29
  70.7 126.6 %all-reduce.21.cloned.1.call-start = ((), (), s32[]{:S(2)}) async-start(), calls=%async_computation.1 | async-start | bytes 786432 | tf_op jit(solution)/shard_map/psum | solution.py:183
  94.0 6.1 %collective-permute-start.6 = (f32[1,64,128]{2,1,0:T(8,128)S(1)}, f32[1,64,128]{2,1,0:T(8,128)S(1)}, u32[]{:S(2)}, u32[]{:S(2)}) collective-permute-start(f32[1,64,128]{2,1,0:T(8,128)S(1)} %get-tuple-element.82), channel_id=1, source_target_pairs={{1,0},{2,1},{3,2},{4,3},{5,4},{6,5},{7,6},{8,7},{9,8},{10,9},{11,1... | collective-permute-start | bytes 98312 | tf_op jit(solution)/shard_map/ppermute | solution.py:29
  95.3 6.1 %collective-permute-start.7 = (f32[1,64,128]{2,1,0:T(8,128)S(1)}, f32[1,64,128]{2,1,0:T(8,128)S(1)}, u32[]{:S(2)}, u32[]{:S(2)}) collective-permute-start(f32[1,64,128]{2,1,0:T(8,128)S(1)} %get-tuple-element.81), channel_id=1, source_target_pairs={{0,1},{1,2},{2,3},{3,4},{4,5},{5,6},{6,7},{7,8},{8,9},{9,10},{10,1... | collective-permute-start | bytes 98312 | tf_op jit(solution)/shard_map/ppermute | solution.py:26
  150.5 9.8 %copy-start.3 = (f32[12,64,128]{2,1,0:T(8,128)}, f32[12,64,128]{2,1,0:T(8,128)S(1)}, u32[]{:S(2)}) copy-start(f32[12,64,128]{2,1,0:T(8,128)S(1)} %get-tuple-element.10) | copy-start | bytes 1179652
  150.5 6.6 %collective-permute-start.8 = (f32[6,64,128]{2,1,0:T(8,128)S(1)}, f32[6,64,128]{2,1,0:T(8,128)S(1)}, u32[]{:S(2)}, u32[]{:S(2)}) collective-permute-start(f32[6,64,128]{2,1,0:T(8,128)S(1)} %get-tuple-element.79), channel_id=1, source_target_pairs={{0,1},{1,2},{2,3},{3,4},{4,5},{5,6},{6,7},{7,8},{8,9},{9,10},{10,1... | collective-permute-start | bytes 589832 | tf_op jit(solution)/shard_map/ppermute | solution.py:26
  151.8 7.6 %collective-permute-start.9 = (f32[6,64,128]{2,1,0:T(8,128)S(1)}, f32[6,64,128]{2,1,0:T(8,128)S(1)}, u32[]{:S(2)}, u32[]{:S(2)}) collective-permute-start(f32[6,64,128]{2,1,0:T(8,128)S(1)} %get-tuple-element.80), channel_id=1, source_target_pairs={{1,0},{2,1},{3,2},{4,3},{5,4},{6,5},{7,6},{8,7},{9,8},{10,9},{11,1... | collective-permute-start | bytes 589832 | tf_op jit(solution)/shard_map/ppermute | solution.py:29
  179.3 18.0 %copy-start.4 = (f32[12,64,128]{2,1,0:T(8,128)S(1)}, f32[12,64,128]{2,1,0:T(8,128)}, u32[]{:S(2)}) copy-start(f32[12,64,128]{2,1,0:T(8,128)} %copy-done.3) | copy-start | bytes 1179652
  182.0 22.2 %copy-start.9 = (f32[2,24,64,128]{3,2,1,0:T(8,128)S(1)}, f32[2,24,64,128]{3,2,1,0:T(8,128)}, u32[]{:S(2)}) copy-start(f32[2,24,64,128]{3,2,1,0:T(8,128)} %get-tuple-element.13) | copy-start | bytes 4718596
  198.4 6.8 %collective-permute-start.10 = (f32[1,64,128]{2,1,0:T(8,128)S(1)}, f32[1,64,128]{2,1,0:T(8,128)S(1)}, u32[]{:S(2)}, u32[]{:S(2)}) collective-permute-start(f32[1,64,128]{2,1,0:T(8,128)S(1)} %get-tuple-element.78), channel_id=1, source_target_pairs={{1,0},{2,1},{3,2},{4,3},{5,4},{6,5},{7,6},{8,7},{9,8},{10,9},{11,1... | collective-permute-start | bytes 98312 | tf_op jit(solution)/shard_map/ppermute | solution.py:29
  199.7 6.1 %collective-permute-start.11 = (f32[1,64,128]{2,1,0:T(8,128)S(1)}, f32[1,64,128]{2,1,0:T(8,128)S(1)}, u32[]{:S(2)}, u32[]{:S(2)}) collective-permute-start(f32[1,64,128]{2,1,0:T(8,128)S(1)} %get-tuple-element.77), channel_id=1, source_target_pairs={{0,1},{1,2},{2,3},{3,4},{4,5},{5,6},{6,7},{7,8},{8,9},{9,10},{10,1... | collective-permute-start | bytes 98312 | tf_op jit(solution)/shard_map/ppermute | solution.py:26
  206.8 47.6 %copy-start.12 = (pred[12,64,128]{2,1,0:T(8,128)(4,1)S(1)}, pred[12,64,128]{2,1,0:T(8,128)(4,1)}, u32[]{:S(2)}) copy-start(pred[12,64,128]{2,1,0:T(8,128)(4,1)} %get-tuple-element.36) | copy-start | bytes 294916
  206.8 47.6 %copy-start.13 = (pred[12,64,128]{2,1,0:T(8,128)(4,1)S(1)}, pred[12,64,128]{2,1,0:T(8,128)(4,1)}, u32[]{:S(2)}) copy-start(pred[12,64,128]{2,1,0:T(8,128)(4,1)} %get-tuple-element.37) | copy-start | bytes 294916
  (15 other events, 63.3 us)
Sparse Core Ops, SparseCore 0:
  70.8 21.9 all-reduce.18
  182.2 15.0 all-reduce.20
where the time goes:
time: 263 us; the launch traced here: 262 us
  blocking collectives  87.1 us (33%)
  other arithmetic  65.8 us (25%)
  waiting for transfers between devices  49 us (19%)
  starting transfers between devices  34.6 us (13%)
  between operations  17.2 us (7%)
  local copies, waits for them, and re-layouts  8.34 us (3%)
    psum x2, blocking collectives, body(): lax.psum((jnp.sum(jnp.abs(momentum)), jnp.sum(design_here)), 'brick')  87.1 us
    psum x2, waiting for transfers between devices, body(): energy = lax.psum(local_energy, 'load')  36.7 us
    ppermute x6, starting transfers between devices, padded_2(): lax.ppermute(lax.slice_in_dim(block, block.shape[dim] - width, None, axis...  26.6 us
    mul x8, other arithmetic, chebyshev(): free_mask * direction  18.8 us
    ppermute x6, starting transfers between devices, padded_2(): lax.ppermute(lax.slice_in_dim(block, 0, width, axis=dim), axis, backward)  7.85 us
    mul x2, other arithmetic, load_energy(): energy = mass_shift * freed * freed  7.21 us
    scatter-add x1, other arithmetic, place_points(): jnp.zeros((loads_here, span_cells + 1), jnp.float32).at[row_ids, slot_ids]  6.96 us
    mul x2, other arithmetic, load_energy(): energy = energy + 0.25 * (freed - beside) ** 2  6.48 us
  transfers between devices with their start and end apart: 14, of which 7 were waited for; matrix products, arithmetic and copies ran while one was open for 6% of the time, Pallas kernels for 0%

commit v1 on v0

v1 whole, which is shorter than its diff:
```python
import functools

import jax
import jax.numpy as jnp
from jax import lax
from jax.experimental import pallas as pl
from jax.experimental.pallas import tpu as pltpu
from jax.sharding import PartitionSpec as P

SWEEPS = 5

stiff_floor = 0.01
mass_shift = 0.1
spectrum_low = 0.05
spectrum_high = 2.0
moment_decay = 0.8
step_size = 0.1
volume_pull = 0.5
volume_target = 0.4
density_floor = 0.001

SOURCE = SWEEPS
DESIGN = SWEEPS + 1
SENSE = SWEEPS + 2


def chebyshev_factors():
    centre = 0.5 * (spectrum_high + spectrum_low)
    half_width = 0.5 * (spectrum_high - spectrum_low)
    ratio_one = centre / half_width
    previous = 1.0 / ratio_one
    factors = []
    for _ in range(SWEEPS - 1):
        current = 1.0 / (2.0 * ratio_one - previous)
        factors.append((current * previous, 2.0 * current / half_width))
        previous = current
    return 1.0 / centre, factors


def shifted(plane):
    size_y, size_z = plane.shape
    return (
        pltpu.roll(plane, 1, 0),
        pltpu.roll(plane, size_y - 1, 0),
        pltpu.roll(plane, 1, 1),
        pltpu.roll(plane, size_z - 1, 1),
    )


def inner_masks(shape):
    along_y = lax.broadcasted_iota(jnp.int32, shape, 0)
    along_z = lax.broadcasted_iota(jnp.int32, shape, 1)
    return (along_y > 0, along_y < shape[0] - 1, along_z > 0, along_z < shape[1] - 1)


def beside_planes(plane, masks):
    return tuple(jnp.where(mask, moved, 0.0) for mask, moved in zip(masks, shifted(plane)))


def edge_planes(masks):
    edges = sum((1.0 - mask.astype(jnp.float32)) for mask in masks)
    return 1.0 / (8.0 - edges), 1.0 / (7.0 - edges)


def stiffness_of(design):
    return stiff_floor + (1.0 - stiff_floor) * (design * design * design)


def weights_stage(rows, free_of, stiff, weight, inverse, masks):
    def one_row(q, carry):
        here, below, above = stiff[q + 1], stiff[q], stiff[q + 2]
        around = (below, above) + beside_planes(here, masks)
        total = around[0]
        for plane in around[1:]:
            total = total + plane
        diagonal = (3.0 + mass_shift) * here + 0.5 * total
        scale = jnp.where(free_of(q), 1.0 / diagonal, 0.0)
        inverse[q] = scale
        half = 0.5 * scale
        weight[0, q] = half * (here + below)
        weight[1, q] = half * (here + above)
        for j in range(4):
            weight[2 + j, q] = jnp.where(masks[j], half * (here + around[2 + j]), 0.0)
        return carry

    lax.fori_loop(0, rows, one_row, 0)


def sweep_stage(rows, loads, weight, resid, steps, shown):
    _, factors = chebyshev_factors()
    for k, (keep, gain) in enumerate(factors):
        last = k == len(factors) - 1

        def one_row(q, carry, k=k, keep=keep, gain=gain, last=last):
            faces = [weight[j, q] for j in range(6)]
            for l in range(loads):
                here = steps[k, l, q]
                total = faces[0] * steps[k, l, q - 1] + faces[1] * steps[k, l, q + 1]
                for face, moved in zip(faces[2:], shifted(here)):
                    total = total + face * moved
                left = resid[l, q] - here + total
                step = keep * here + gain * left
                if last:
                    for earlier in range(k + 1):
                        step = step + steps[earlier, l, q]
                    shown[l, q - (SWEEPS - 1)] = step
                else:
                    resid[l, q] = left
                    steps[k + 1, l, q] = step
            return carry

        lax.fori_loop(k + 1, rows - k - 1, one_row, 0)


def energy_stage(cells, loads, design_of, shown, sense, masks):
    def one_row(i, carry):
        energy = None
        for l in range(loads):
            here = shown[l, i + 1]
            around = (shown[l, i], shown[l, i + 2]) + beside_planes(here, masks)
            spread = None
            for plane in around:
                gap = here - plane
                spread = gap * gap if spread is None else spread + gap * gap
            part = mass_shift * (here * here) + 0.25 * spread
            energy = part if energy is None else energy + part
        design = design_of(i)
        sense[i] = (-3.0 * (1.0 - stiff_floor)) * (design * design) * energy
        return carry

    lax.fori_loop(0, cells, one_row, 0)


def fold(plane):
    return jnp.sum(plane.reshape(plane.shape[0] // 8, 8, plane.shape[1]), axis=0)


def filter_total(cells, sense, is_first, is_last, masks):
    inside, outer = edge_planes(masks)
    beside_inside = sum(beside_planes(inside, masks))
    beside_outer = sum(beside_planes(outer, masks))
    usual = 4.0 * inside + beside_inside
    at_end = 2.0 * outer + inside + beside_outer
    zero = jnp.zeros_like(inside)
    total = lax.fori_loop(0, cells, lambda i, acc: acc + sense[i], zero)
    ends = jnp.where(is_first, sense[0], zero) + jnp.where(is_last, sense[cells - 1], zero)
    nexts = jnp.where(is_first, sense[1], zero) + jnp.where(is_last, sense[cells - 2], zero)
    return -fold(total * usual + ends * (at_end - usual) + nexts * (outer - inside))


def first_kernel(cells, loads, place, self_weight, design_ref, free_ref, force_ref, force_lo, force_hi, points_ref,
                 pair_a, pair_b, sense_ref, tile_ref, design_wide, free_wide, base_wide,
                 stiff, weight, inverse, resid, steps, shown):
    even, is_first, is_last = place[0] == 1, place[1] == 1, place[2] == 1
    shape = design_ref.shape[1:]
    masks = inner_masks(shape)
    wide = cells + 2 * DESIGN
    rows = cells + 2 * SOURCE
    zero = jnp.zeros(shape, jnp.float32)

    for i in range(DESIGN):
        low = jnp.where(even, pair_a[i], pair_b[i])
        high = jnp.where(even, pair_b[i], pair_a[i])
        design_wide[i] = low
        design_wide[DESIGN + cells + i] = high
        stiff[i] = jnp.where(is_first, zero, stiffness_of(low))
        stiff[DESIGN + cells + i] = jnp.where(is_last, zero, stiffness_of(high))
    for i in range(SOURCE):
        low = jnp.where(even, pair_a[DESIGN + i], pair_b[DESIGN + i])
        high = jnp.where(even, pair_b[DESIGN + i], pair_a[DESIGN + i])
        free_wide[i] = jnp.where(is_first, zero, low)
        free_wide[SOURCE + cells + i] = jnp.where(is_last, zero, high)

    def own(i, carry):
        design = design_ref[i]
        design_wide[DESIGN + i] = design
        stiff[DESIGN + i] = stiffness_of(design)
        free_wide[SOURCE + i] = free_ref[i]
        return carry

    lax.fori_loop(0, cells, own, 0)

    weights_stage(rows, lambda q: free_wide[q] > 0.5, stiff, weight, inverse, masks)

    first_scale, _ = chebyshev_factors()
    for l in range(loads):
        for start, count, force in ((0, SOURCE, force_lo), (SOURCE, cells, force_ref), (SOURCE + cells, SOURCE, force_hi)):

            def one_row(i, carry, l=l, start=start, force=force):
                q = start + i
                base = points_ref[l, q] + force[l, i]
                base_wide[l, q] = base
                left = inverse[q] * (base + self_weight[l] * design_wide[q + 1])
                resid[l, q] = left
                steps[0, l, q] = first_scale * left
                return carry

            lax.fori_loop(0, count, one_row, 0)

    sweep_stage(rows, loads, weight, resid, steps, shown)
    energy_stage(cells, loads, lambda i: design_ref[i], shown, sense_ref, masks)
    tile_ref[0] = filter_total(cells, sense_ref, is_first, is_last, masks)
    tile_ref[1] = fold(lax.fori_loop(0, cells, lambda i, acc: acc + design_ref[i], zero))


def second_kernel(cells, loads, total_cells, share, place, self_weight, tile_in, sense_a, sense_b, pair_a, pair_b,
                  design_wide, free_wide, base_wide,
                  shown_ref, sense_ref, tile_ref, design_out, momentum_out,
                  sense_wide, stiff, weight, inverse, resid, steps, shown, design_new):
    even, is_first, is_last = place[0] == 1, place[1] == 1, place[2] == 1
    shape = sense_a.shape[1:]
    masks = inner_masks(shape)
    wide = cells + 2 * DESIGN
    rows = cells + 2 * SOURCE
    zero = jnp.zeros(shape, jnp.float32)
    for i in range(SENSE):
        low = jnp.where(even, pair_a[i], pair_b[i])
        high = jnp.where(even, pair_b[i], pair_a[i])
        sense_wide[i] = jnp.where(is_first, zero, low)
        sense_wide[SENSE + cells + i] = jnp.where(is_last, zero, high)

    def own(i, carry):
        sense_wide[SENSE + i] = sense_a[i] + sense_b[i]
        return carry

    lax.fori_loop(0, cells, own, 0)

    abs_total = jnp.sum(tile_in[0], keepdims=True)
    density_total = jnp.sum(tile_in[1], keepdims=True) * share
    mean_step = abs_total / total_cells + 1e-6
    pull = volume_pull * (density_total / total_cells - volume_target)
    rate = step_size / mean_step
    inside, outer = edge_planes(masks)

    def one_row(r, carry):
        here = sense_wide[r + 1]
        total = 2.0 * here + sense_wide[r] + sense_wide[r + 2]
        for plane in beside_planes(here, masks):
            total = total + plane
        at_end = (is_first & (r == DESIGN)) | (is_last & (r == DESIGN + cells - 1))
        momentum = total * jnp.where(at_end, outer, inside)
        before = design_wide[r]
        moved = jnp.clip(before - rate * momentum - pull, density_floor, 1.0)
        fixed = (before == density_floor) | (before == 1.0)
        design = jnp.where(fixed, before, moved)
        design_new[r] = design
        outside = (is_first & (r < DESIGN)) | (is_last & (r >= DESIGN + cells))
        stiff[r] = jnp.where(outside, zero, stiffness_of(design))

        @pl.when((r >= DESIGN) & (r < DESIGN + cells))
        def _():
            momentum_out[r - DESIGN] = momentum
            design_out[r - DESIGN] = design

        return carry

    lax.fori_loop(0, wide, one_row, 0)

    weights_stage(rows, lambda q: free_wide[q] > 0.5, stiff, weight, inverse, masks)
    first_scale, _ = chebyshev_factors()

    def start_row(q, carry):
        scale, design = inverse[q], design_new[q + 1]
        for l in range(loads):
            left = scale * (base_wide[l, q] + self_weight[l] * design)
            resid[l, q] = left
            steps[0, l, q] = first_scale * left
        return carry

    lax.fori_loop(0, rows, start_row, 0)
    sweep_stage(rows, loads, weight, resid, steps, shown)
    for l in range(loads):

        def copy_row(i, carry, l=l):
            shown_ref[l, i] = shown[l, i + 1]
            return carry

        lax.fori_loop(0, cells, copy_row, 0)
    energy_stage(cells, loads, lambda i: design_out[i], shown, sense_ref, masks)
    tile_ref[0] = filter_total(cells, sense_ref, is_first, is_last, masks)
    tile_ref[1] = fold(lax.fori_loop(0, cells, lambda i, acc: acc + design_out[i], zero))


def last_kernel(cells, slab, total_cells, share, place, tile_before, tile_in, sense_a, sense_b, row_lo, row_hi,
                momentum_in, design_in, passive_ref, design_ref, momentum_ref, sense_wide, design_all, momentum_all):
    is_first, is_last, start = place[1] == 1, place[2] == 1, place[3]
    shape = sense_a.shape[1:]
    masks = inner_masks(shape)
    zero = jnp.zeros(shape, jnp.float32)
    sense_wide[0] = jnp.where(is_first, zero, row_lo[0])
    sense_wide[cells + 1] = jnp.where(is_last, zero, row_hi[0])

    def own(i, carry):
        sense_wide[i + 1] = sense_a[i] + sense_b[i]
        return carry

    lax.fori_loop(0, cells, own, 0)
    abs_total = jnp.sum(moment_decay * tile_before[0] + tile_in[0], keepdims=True)
    density_total = jnp.sum(tile_in[1], keepdims=True) * share
    mean_step = abs_total / total_cells + 1e-6
    pull = volume_pull * (density_total / total_cells - volume_target)
    rate = step_size / mean_step
    inside, outer = edge_planes(masks)

    def one_row(i, carry):
        here = sense_wide[i + 1]
        total = 2.0 * here + sense_wide[i] + sense_wide[i + 2]
        for plane in beside_planes(here, masks):
            total = total + plane
        at_end = (is_first & (i == 0)) | (is_last & (i == cells - 1))
        momentum = moment_decay * momentum_in[i] + total * jnp.where(at_end, outer, inside)
        moved = jnp.clip(design_in[i] - rate * momentum - pull, density_floor, 1.0)
        kind = passive_ref[i]
        design_all[i] = jnp.where(kind == 1, density_floor, jnp.where(kind == 2, 1.0, moved))
        momentum_all[i] = momentum
        return carry

    lax.fori_loop(0, cells, one_row, 0)
    window = pl.ds(pl.multiple_of(start, 8), slab)
    design_ref[...] = design_all[:, window, :]
    momentum_ref[...] = momentum_all[:, window, :]


VMEM = pl.BlockSpec(memory_space=pltpu.VMEM)
SMEM = pl.BlockSpec(memory_space=pltpu.SMEM)


def on_core(kernel, operands, scalars, outs, scratch):
    return pl.pallas_call(
        kernel,
        out_shape=[jax.ShapeDtypeStruct(shape, jnp.float32) for shape in outs],
        in_specs=[SMEM] * scalars + [VMEM] * (len(operands) - scalars),
        out_specs=[VMEM] * len(outs),
        scratch_shapes=[pltpu.VMEM(shape, jnp.float32) for shape in scratch],
        compiler_params=pltpu.CompilerParams(vmem_limit_bytes=48 * 1024 * 1024),
    )(*operands)


def swap(value, axis, bit):
    count = lax.axis_size(axis)
    return lax.ppermute(value, axis, [(i, i ^ bit) for i in range(count)])


def along(value, step):
    count = lax.axis_size("brick")
    pairs = [(i, i + step) for i in range(count) if 0 <= i + step < count]
    return lax.ppermute(value, "brick", pairs)


def both_ways(value):
    count, loads = lax.axis_size("brick"), lax.axis_size("load")
    pairs = []
    for l in range(loads):
        step = 1 if l % 2 == 0 else -1
        pairs += [(l * count + i, l * count + i + step) for i in range(count) if 0 <= i + step < count]
    return lax.ppermute(value, ("load", "brick"), pairs)


def bits_of(count):
    return [1 << k for k in range(count.bit_length() - 1)]


def sum_over(value, axis):
    for bit in bits_of(lax.axis_size(axis)):
        value = value + swap(value, axis, bit)
    return value


def load_terms(value):
    bits = bits_of(lax.axis_size("load"))
    for bit in bits[:-1]:
        value = value + swap(value, "load", bit)
    return value, swap(value, "load", bits[-1])


def place_points(load_nodes, load_force, first_x, rows_x, size_y, size_z):
    loads_here = load_nodes.shape[0]
    span_cells = rows_x * size_y * size_z
    local_ids = load_nodes - first_x * size_y * size_z
    inside = (local_ids >= 0) & (local_ids < span_cells)
    slot_ids = jnp.where(inside, local_ids, span_cells)
    row_ids = lax.broadcasted_iota(jnp.int32, load_nodes.shape, 0)
    points = (
        jnp.zeros((loads_here, span_cells + 1), jnp.float32).at[row_ids, slot_ids].add(load_force)
    )
    return points[:, :span_cells].reshape(loads_here, rows_x, size_y, size_z)


def body(density, passive, support, load_nodes, load_force, self_weight, body_force):
    cells, size_y, size_z = density.shape
    loads = body_force.shape[0]
    bricks, brick = lax.axis_size("brick"), lax.axis_index("brick")
    load_count, load_index = lax.axis_size("load"), lax.axis_index("load")
    slab = size_y // load_count
    total_cells = float(cells * bricks * size_y * size_z)
    share = 1.0 / load_count
    even = load_index % 2 == 0
    place = jnp.stack([even, brick == 0, brick == bricks - 1, load_index * slab]).astype(jnp.int32)
    plane = (size_y, size_z)
    wide, rows = cells + 2 * DESIGN, cells + 2 * SOURCE

    free = (1 - support).astype(jnp.float32)
    design = jnp.where(passive == 1, density_floor, jnp.where(passive == 2, 1.0, density))
    upward = jnp.concatenate([design[cells - DESIGN:], free[cells - SOURCE:]])
    downward = jnp.concatenate([design[:DESIGN], free[:SOURCE]])
    pair_a = both_ways(jnp.where(even, upward, downward))
    pair_b = swap(pair_a, "load", 1)
    force_lo = along(body_force[:, cells - SOURCE:], 1)
    force_hi = along(body_force[:, :SOURCE], -1)
    points = place_points(load_nodes, load_force, brick * cells - SOURCE, rows, size_y, size_z)

    solve_scratch = [
        (wide,) + plane,
        (6, rows) + plane,
        (rows,) + plane,
        (loads, rows) + plane,
        (SWEEPS - 1, loads, rows) + plane,
        (loads, cells + 2) + plane,
    ]
    tile = (2, 8, size_z)
    sense, tiles, design_wide, free_wide, base_wide = on_core(
        functools.partial(first_kernel, cells, loads),
        (place, self_weight, design, free, body_force, force_lo, force_hi, points, pair_a, pair_b),
        2,
        [(cells,) + plane, tile, (wide,) + plane, (rows,) + plane, (loads, rows) + plane],
        solve_scratch,
    )
    tiles_first = sum_over(sum_over(tiles, "load"), "brick")
    sense_a, sense_b = load_terms(sense)
    start = jnp.where(even, cells - SENSE, 0)
    edge = lax.dynamic_slice_in_dim(sense_a, start, SENSE, 0) + lax.dynamic_slice_in_dim(sense_b, start, SENSE, 0)
    pair_a = both_ways(edge)
    pair_b = swap(pair_a, "load", 1)

    shown, sense, tiles, design, momentum = on_core(
        functools.partial(second_kernel, cells, loads, total_cells, share),
        (place, self_weight, tiles_first, sense_a, sense_b, pair_a, pair_b, design_wide, free_wide, base_wide),
        2,
        [(loads, cells) + plane, (cells,) + plane, tile, (cells,) + plane, (cells,) + plane],
        [(cells + 2 * SENSE,) + plane] + solve_scratch + [(wide,) + plane],
    )
    tiles_last = sum_over(sum_over(tiles, "load"), "brick")
    sense_a, sense_b = load_terms(sense)
    row_lo = along(sense_a[cells - 1:] + sense_b[cells - 1:], 1)
    row_hi = along(sense_a[:1] + sense_b[:1], -1)
    design, momentum = on_core(
        functools.partial(last_kernel, cells, slab, total_cells, share),
        (place, tiles_first, tiles_last, sense_a, sense_b, row_lo, row_hi, momentum, design, passive),
        1,
        [(cells, slab, size_z)] * 2,
        [(cells + 2,) + plane, (cells,) + plane, (cells,) + plane],
    )
    return design, momentum, shown


def solution(mesh):
    placed = (
        P("brick", None, None),
        P("brick", None, None),
        P("brick", None, None),
        P("load", None),
        P("load", None),
        P("load"),
        P("load", "brick", None, None),
    )
    return jax.shard_map(
        body,
        mesh=mesh,
        in_specs=placed,
        out_specs=(
            P("brick", "load", None),
            P("brick", "load", None),
            P("load", "brick", None, None),
        ),
        check_vma=False,
    )
```

time: 263 us -> 129 us (0.49)
  blocking collectives: 87.1 us -> 0 us
  other arithmetic: 65.8 us -> 20.6 us
  Pallas kernels: 0 us -> 33.1 us
  waiting for transfers between devices: 49 us -> 26.2 us
  between operations: 17.2 us -> 0.88 us
  local copies, waits for them, and re-layouts: 8.34 us -> 11.9 us
    psum x2 -> x0, blocking collectives: 87.1 us -> none  [body(): lax.psum((jnp.sum(jnp.abs(momentum)), jnp.sum(design_here)), 'brick')]
    mul x17 -> x0, other arithmetic: 36.9 us -> none  [the longest x8 18.8 us: chebyshev(): free_mask * direction]
    psum x2 -> x0, waiting for transfers between devices: 36.7 us -> none  [body(): energy = lax.psum(local_energy, 'load')]
    pallas_call x0 -> x3, Pallas kernels: none -> 33.1 us  [on_core(): pl.pallas_call(kernel, out_shape=[jax.ShapeDtypeStruct(shape, jnp.float32...]
    reduce_sum x6 -> x0, other arithmetic: 14.4 us -> none  [the longest x2 5.68 us: body(): local_energy = jnp.sum(energy_wide[:, widen:widen + cells_x], axis=0)]
    ppermute x12 -> x20, waiting for transfers between devices: 12.3 us -> 26.2 us  [the longest x14 20.2 us: swap(): return lax.ppermute(value, axis, [(i, i ^ bit) for i in range(count)])]
    scatter-add x1, other arithmetic: 6.96 us -> 19.3 us  [place_points(): jnp.zeros((loads_here, span_cells + 1), jnp.float32).at[row_ids, slot_ids]]
    unnamed x55 -> x29, local copies, waits for them, and re-layouts: 3.63 us -> 9.53 us
  transfers between devices with their start and end apart: 14 -> 20, of which waited for: 7 -> 11; matrix products, arithmetic and copies ran while one was open for 6% -> 19% of each run, Pallas kernels for 0% -> 0%
where the time goes in v1:
time: 129 us; the launch traced here: 128 us
  starting transfers between devices  35.7 us (28%)
  Pallas kernels  33.1 us (26%)
  waiting for transfers between devices  26.2 us (20%)
  other arithmetic  20.6 us (16%)
  local copies, waits for them, and re-layouts  11.9 us (9%)
    pallas_call x3, Pallas kernels, on_core(): pl.pallas_call(kernel, out_shape=[jax.ShapeDtypeStruct(shape, jnp.float32...  33.1 us
    ppermute x14, waiting for transfers between devices, swap(): return lax.ppermute(value, axis, [(i, i ^ bit) for i in range(count)])  20.2 us
    scatter-add x1, other arithmetic, place_points(): jnp.zeros((loads_here, span_cells + 1), jnp.float32).at[row_ids, slot_ids]  19.3 us
    ppermute x14, starting transfers between devices, swap(): return lax.ppermute(value, axis, [(i, i ^ bit) for i in range(count)])  14.8 us
    ppermute x4, starting transfers between devices, along(): return lax.ppermute(value, 'brick', pairs)  11.7 us
    unnamed x29, local copies, waits for them, and re-layouts  9.53 us
    ppermute x2, starting transfers between devices, both_ways(): return lax.ppermute(value, ('load', 'brick'), pairs)  9.22 us
    ppermute x2, waiting for transfers between devices, both_ways(): return lax.ppermute(value, ('load', 'brick'), pairs)  6 us
  transfers between devices with their start and end apart: 20, of which 11 were waited for; matrix products, arithmetic and copies ran while one was open for 19% of the time, Pallas kernels for 0%

profile of v1, /device:TPU:0, one launch (start us, length us, event | category | flops | bytes accessed | tf_op | source)
XLA Modules:
  0.0 128.4 jit_solution(11065326903495964307)
XLA Ops:
  2.1 5.0 %collective-permute-start.2 = (f32[11,64,128]{2,1,0:T(8,128)S(1)}, f32[11,64,128]{2,1,0:T(8,128)S(1)}, u32[]{:S(2)}, u32[]{:S(2)}) collective-permute-start(f32[11,64,128]{2,1,0:T(8,128)S(1)} %maximum_select_fusion), channel_id=1, source_target_pairs={{0,1},{1,2},{2,3},{3,4},{4,5},{5,6},{6,7},{7,8},{8,9},{9,10},{10,1... | collective-permute-start | bytes 1081352 | tf_op jit(solution)/shard_map/ppermute | solution.py:356
  9.3 4.6 %collective-permute-start = (f32[2,5,64,128]{3,2,1,0:T(8,128)}, f32[2,5,64,128]{3,2,1,0:T(8,128)S(1)}, u32[]{:S(2)}, u32[]{:S(2)}) collective-permute-start(f32[2,5,64,128]{3,2,1,0:T(8,128)} %get-tuple-element.30), channel_id=1, source_target_pairs={{0,1},{1,2},{2,3},{3,4},{4,5},{5,6},{6,7},{7,8},{8,9},{9,10},{10,1... | collective-permute-start | bytes 983048 | tf_op jit(solution)/shard_map/ppermute | solution.py:347
  15.4 19.3 %scatter_fusion = f32[2,180225]{1,0:T(2,128)} fusion(f32[2,180225]{1,0:T(2,128)} %broadcast_in_dim.18, s32[128]{0:T(128)S(1)} %reshape.25, f32[128]{0:T(128)S(1)} %reshape.27), kind=kCustom, calls=%fused_computation | custom fusion | flops 128 | bytes 2560 | tf_op jit(solution)/shard_map/scatter-add | solution.py:384
  34.7 1.4 %slice_bitcast_fusion = f32[1,2,1408,128]{3,1,2,0:T(2,128)S(1)} fusion(f32[2,180225]{1,0:T(2,128)} %scatter_fusion), kind=kLoop, calls=%fused_computation.1 | loop fusion | bytes 2883584
  40.8 14.5 %shard_map.94 = (f32[12,64,128]{2,1,0:T(8,128)S(1)}, f32[2,8,128]{2,1,0:T(8,128)S(1)}, f32[24,64,128]{2,1,0:T(8,128)S(1)}, f32[22,64,128]{2,1,0:T(8,128)S(1)}, f32[2,22,64,128]{3,2,1,0:T(8,128)}) custom-call(s32[4]{0:T(128)S(1)} %pad_add_fusion.place, f32[2]{0:T(128)S(1)} %copy-done.9, f32[12,64,128]{2,1,0:T(8,128)S(1)} %select_select_fusion.design_ref, ...), custom_call_target="tpu_custom_call" | custom-call | tf_op jit(solution)/shard_map/pallas_call | solution.py:329
  58.0 4.2 %collective-permute-start.10 = (f32[7,64,128]{2,1,0:T(8,128)S(1)}, f32[7,64,128]{2,1,0:T(8,128)S(1)}, u32[]{:S(2)}, u32[]{:S(2)}) collective-permute-start(f32[7,64,128]{2,1,0:T(8,128)S(1)} %dynamic-slice_add_fusion), channel_id=1, source_target_pairs={{0,1},{1,2},{2,3},{3,4},{4,5},{5,6},{6,7},{7,8},{8,9},{9,10},{10,1... | collective-permute-start | bytes 688136 | tf_op jit(solution)/shard_map/ppermute | solution.py:356
  62.3 6.0 %collective-permute-done.10.pair_a = f32[7,64,128]{2,1,0:T(8,128)S(1)} collective-permute-done((f32[7,64,128]{2,1,0:T(8,128)S(1)}, f32[7,64,128]{2,1,0:T(8,128)S(1)}, u32[]{:S(2)}, u32[]{:S(2)}) %collective-permute-start.10) | collective-permute-done | bytes 229408 | tf_op jit(solution)/shard_map/ppermute | solution.py:356
  69.8 2.4 %collective-permute-start.5 = (f32[2,8,128]{2,1,0:T(8,128)S(1)}, f32[2,8,128]{2,1,0:T(8,128)S(1)}, u32[]{:S(2)}, u32[]{:S(2)}) collective-permute-start(f32[2,8,128]{2,1,0:T(8,128)S(1)} %add.60), channel_id=1, source_target_pairs={{0,1},{1,0},{2,3},{3,2},{4,5},{5,4},{6,7},{7,6},{8,9},{9,8},{10,11... | collective-permute-start | bytes 24584 | tf_op jit(solution)/shard_map/ppermute | solution.py:341
  72.2 1.6 %collective-permute-done.5 = f32[2,8,128]{2,1,0:T(8,128)S(1)} collective-permute-done((f32[2,8,128]{2,1,0:T(8,128)S(1)}, f32[2,8,128]{2,1,0:T(8,128)S(1)}, u32[]{:S(2)}, u32[]{:S(2)}) %collective-permute-start.5) | collective-permute-done | bytes 8224 | tf_op jit(solution)/shard_map/ppermute | solution.py:341
  75.0 2.5 %collective-permute-done.6 = f32[2,8,128]{2,1,0:T(8,128)S(1)} collective-permute-done((f32[2,8,128]{2,1,0:T(8,128)S(1)}, f32[2,8,128]{2,1,0:T(8,128)S(1)}, u32[]{:S(2)}, u32[]{:S(2)}) %collective-permute-start.6) | collective-permute-done | bytes 8224 | tf_op jit(solution)/shard_map/ppermute | solution.py:341
  77.5 1.5 %collective-permute-start.7 = (f32[2,8,128]{2,1,0:T(8,128)S(1)}, f32[2,8,128]{2,1,0:T(8,128)S(1)}, u32[]{:S(2)}, u32[]{:S(2)}) collective-permute-start(f32[2,8,128]{2,1,0:T(8,128)S(1)} %add.62), channel_id=1, source_target_pairs={{0,4},{1,5},{2,6},{3,7},{4,0},{5,1},{6,2},{7,3},{8,12},{9,13},{10,... | collective-permute-start | bytes 24584 | tf_op jit(solution)/shard_map/ppermute | solution.py:341
  79.0 2.1 %collective-permute-done.7 = f32[2,8,128]{2,1,0:T(8,128)S(1)} collective-permute-done((f32[2,8,128]{2,1,0:T(8,128)S(1)}, f32[2,8,128]{2,1,0:T(8,128)S(1)}, u32[]{:S(2)}, u32[]{:S(2)}) %collective-permute-start.7) | collective-permute-done | bytes 8224 | tf_op jit(solution)/shard_map/ppermute | solution.py:341
  81.2 2.2 %collective-permute-start.8 = (f32[2,8,128]{2,1,0:T(8,128)S(1)}, f32[2,8,128]{2,1,0:T(8,128)S(1)}, u32[]{:S(2)}, u32[]{:S(2)}) collective-permute-start(f32[2,8,128]{2,1,0:T(8,128)S(1)} %add.63), channel_id=1, source_target_pairs={{0,8},{1,9},{2,10},{3,11},{4,12},{5,13},{6,14},{7,15},{8,0},{9,1},... | collective-permute-start | bytes 24584 | tf_op jit(solution)/shard_map/ppermute | solution.py:341
  83.4 2.3 %collective-permute-done.8 = f32[2,8,128]{2,1,0:T(8,128)S(1)} collective-permute-done((f32[2,8,128]{2,1,0:T(8,128)S(1)}, f32[2,8,128]{2,1,0:T(8,128)S(1)}, u32[]{:S(2)}, u32[]{:S(2)}) %collective-permute-start.8) | collective-permute-done | bytes 8224 | tf_op jit(solution)/shard_map/ppermute | solution.py:341
  85.7 1.4 %copy-done.2 = f32[2,22,64,128]{3,2,1,0:T(8,128)S(1)} copy-done((f32[2,22,64,128]{3,2,1,0:T(8,128)S(1)}, f32[2,22,64,128]{3,2,1,0:T(8,128)}, u32[]{:S(2)}) %copy-start.2) | copy-done | bytes 1441816
  88.2 16.0 %shard_map.95 = (f32[2,12,64,128]{3,2,1,0:T(8,128)}, f32[12,64,128]{2,1,0:T(8,128)S(1)}, f32[2,8,128]{2,1,0:T(8,128)S(1)}, f32[12,64,128]{2,1,0:T(8,128)S(1)}, f32[12,64,128]{2,1,0:T(8,128)S(1)}) custom-call(s32[4]{0:T(128)S(1)} %pad_add_fusion.place, f32[2]{0:T(128)S(1)} %copy-done.9, f32[2,8,128]{2,1,0:T(8,128)S(1)} %add.64.tile_in.tile_before, ...), custom_call_target="tpu_custom_call" | custom-call | tf_op jit(solution)/shard_map/pallas_call | solution.py:329
  105.9 2.0 %collective-permute-start.13 = (f32[2,8,128]{2,1,0:T(8,128)S(1)}, f32[2,8,128]{2,1,0:T(8,128)S(1)}, u32[]{:S(2)}, u32[]{:S(2)}) collective-permute-start(f32[2,8,128]{2,1,0:T(8,128)S(1)} %add.66), channel_id=1, source_target_pairs={{0,1},{1,0},{2,3},{3,2},{4,5},{5,4},{6,7},{7,6},{8,9},{9,8},{10,11... | collective-permute-start | bytes 24584 | tf_op jit(solution)/shard_map/ppermute | solution.py:341
  109.3 4.5 %collective-permute-start.18 = (f32[1,64,128]{2,1,0:T(8,128)S(1)}, f32[1,64,128]{2,1,0:T(8,128)S(1)}, u32[]{:S(2)}, u32[]{:S(2)}) collective-permute-start(f32[1,64,128]{2,1,0:T(8,128)S(1)} %get-tuple-element.28), channel_id=1, source_target_pairs={{0,1},{1,2},{2,3},{3,4},{4,5},{5,6},{6,7},{7,8},{8,9},{9,10},{10,1... | collective-permute-start | bytes 98312 | tf_op jit(solution)/shard_map/ppermute | solution.py:347
  114.8 2.8 %collective-permute-done.14 = f32[2,8,128]{2,1,0:T(8,128)S(1)} collective-permute-done((f32[2,8,128]{2,1,0:T(8,128)S(1)}, f32[2,8,128]{2,1,0:T(8,128)S(1)}, u32[]{:S(2)}, u32[]{:S(2)}) %collective-permute-start.14) | collective-permute-done | bytes 8224 | tf_op jit(solution)/shard_map/ppermute | solution.py:341
  117.6 1.5 %collective-permute-start.15 = (f32[2,8,128]{2,1,0:T(8,128)S(1)}, f32[2,8,128]{2,1,0:T(8,128)S(1)}, u32[]{:S(2)}, u32[]{:S(2)}) collective-permute-start(f32[2,8,128]{2,1,0:T(8,128)S(1)} %add.68), channel_id=1, source_target_pairs={{0,4},{1,5},{2,6},{3,7},{4,0},{5,1},{6,2},{7,3},{8,12},{9,13},{10,... | collective-permute-start | bytes 24584 | tf_op jit(solution)/shard_map/ppermute | solution.py:341
  119.1 2.1 %collective-permute-done.15 = f32[2,8,128]{2,1,0:T(8,128)S(1)} collective-permute-done((f32[2,8,128]{2,1,0:T(8,128)S(1)}, f32[2,8,128]{2,1,0:T(8,128)S(1)}, u32[]{:S(2)}, u32[]{:S(2)}) %collective-permute-start.15) | collective-permute-done | bytes 8224 | tf_op jit(solution)/shard_map/ppermute | solution.py:341
  121.2 1.5 %collective-permute-start.16 = (f32[2,8,128]{2,1,0:T(8,128)S(1)}, f32[2,8,128]{2,1,0:T(8,128)S(1)}, u32[]{:S(2)}, u32[]{:S(2)}) collective-permute-start(f32[2,8,128]{2,1,0:T(8,128)S(1)} %add.69), channel_id=1, source_target_pairs={{0,8},{1,9},{2,10},{3,11},{4,12},{5,13},{6,14},{7,15},{8,0},{9,1},... | collective-permute-start | bytes 24584 | tf_op jit(solution)/shard_map/ppermute | solution.py:341
  122.7 3.1 %collective-permute-done.16 = f32[2,8,128]{2,1,0:T(8,128)S(1)} collective-permute-done((f32[2,8,128]{2,1,0:T(8,128)S(1)}, f32[2,8,128]{2,1,0:T(8,128)S(1)}, u32[]{:S(2)}, u32[]{:S(2)}) %collective-permute-start.16) | collective-permute-done | bytes 8224 | tf_op jit(solution)/shard_map/ppermute | solution.py:341
  125.8 2.7 %shard_map.96 = (f32[12,32,128]{2,1,0:T(8,128)}, f32[12,32,128]{2,1,0:T(8,128)}) custom-call(s32[4]{0:T(128)S(1)} %pad_add_fusion.place, f32[2,8,128]{2,1,0:T(8,128)S(1)} %add.64.tile_in.tile_before, f32[2,8,128]{2,1,0:T(8,128)S(1)} %add.70.tile_in, f32[12,64,128]{2,1,0:T(8,128)S(1)} %get-tuple-element.21.sense_a, ...), custom_call_target="tpu_custom_call" | custom-call | tf_op jit(solution)/shard_map/pallas_call | solution.py:329
  (71 shorter events, 20.3 us)
Async XLA Ops:
  1.9 5.2 %copy-start = (f32[2,12,64,128]{3,2,1,0:T(8,128)S(1)}, f32[2,12,64,128]{3,2,1,0:T(8,128)}, u32[]{:S(2)}) copy-start(f32[2,12,64,128]{3,2,1,0:T(8,128)} %force_ref.1) | copy-start | bytes 2359300
  1.9 11.9 %copy-start.11 = (s32[2,64]{1,0:T(2,128)S(1)}, s32[2,64]{1,0:T(2,128)}, u32[]{:S(2)}) copy-start(s32[2,64]{1,0:T(2,128)} %param.10) | copy-start | bytes 1540
  2.0 12.0 %copy-start.12 = (f32[2,64]{1,0:T(2,128)S(1)}, f32[2,64]{1,0:T(2,128)}, u32[]{:S(2)}) copy-start(f32[2,64]{1,0:T(2,128)} %param.11) | copy-start | bytes 1540
  2.1 32.6 %collective-permute-start.2 = (f32[11,64,128]{2,1,0:T(8,128)S(1)}, f32[11,64,128]{2,1,0:T(8,128)S(1)}, u32[]{:S(2)}, u32[]{:S(2)}) collective-permute-start(f32[11,64,128]{2,1,0:T(8,128)S(1)} %maximum_select_fusion), channel_id=1, source_target_pairs={{0,1},{1,2},{2,3},{3,4},{4,5},{5,6},{6,7},{7,8},{8,9},{9,10},{10,1... | collective-permute-start | bytes 1081352 | tf_op jit(solution)/shard_map/ppermute | solution.py:356
  8.0 29.4 %collective-permute-start.1 = (f32[2,5,64,128]{3,2,1,0:T(8,128)}, f32[2,5,64,128]{3,2,1,0:T(8,128)S(1)}, u32[]{:S(2)}, u32[]{:S(2)}) collective-permute-start(f32[2,5,64,128]{3,2,1,0:T(8,128)} %get-tuple-element.29), channel_id=1, source_target_pairs={{1,0},{2,1},{3,2},{4,3},{5,4},{6,5},{7,6},{8,7},{9,8},{10,9},{11,1... | collective-permute-start | bytes 983048 | tf_op jit(solution)/shard_map/ppermute | solution.py:347
  9.3 28.9 %collective-permute-start = (f32[2,5,64,128]{3,2,1,0:T(8,128)}, f32[2,5,64,128]{3,2,1,0:T(8,128)S(1)}, u32[]{:S(2)}, u32[]{:S(2)}) collective-permute-start(f32[2,5,64,128]{3,2,1,0:T(8,128)} %get-tuple-element.30), channel_id=1, source_target_pairs={{0,1},{1,2},{2,3},{3,4},{4,5},{5,6},{6,7},{7,8},{8,9},{9,10},{10,1... | collective-permute-start | bytes 983048 | tf_op jit(solution)/shard_map/ppermute | solution.py:347
  34.7 4.2 %collective-permute-start.3 = (f32[11,64,128]{2,1,0:T(8,128)S(1)}, f32[11,64,128]{2,1,0:T(8,128)S(1)}, u32[]{:S(2)}, u32[]{:S(2)}) collective-permute-start(f32[11,64,128]{2,1,0:T(8,128)S(1)} %collective-permute-done.2.pair_a), channel_id=1, source_target_pairs={{0,16},{16,0},{1,17},{17,1},{2,18},{18,2},{3,19},{19,3},{4,20},{20... | collective-permute-start | bytes 1081352 | tf_op jit(solution)/shard_map/ppermute | solution.py:341
  36.1 2.8 %copy-start.9 = (f32[2]{0:T(128)S(1)}, f32[2]{0:T(128)}, u32[]{:S(2)}) copy-start(f32[2]{0:T(128)} %self_weight.3) | copy-start | bytes 28
  56.2 1.9 %collective-permute-start.9 = (f32[12,64,128]{2,1,0:T(8,128)S(1)}, f32[12,64,128]{2,1,0:T(8,128)S(1)}, u32[]{:S(2)}, u32[]{:S(2)}) collective-permute-start(f32[12,64,128]{2,1,0:T(8,128)S(1)} %get-tuple-element.16.sense_a), channel_id=1, source_target_pairs={{0,16},{16,0},{1,17},{17,1},{2,18},{18,2},{3,19},{19,3},{4,20},{20... | collective-permute-start | bytes 1179656 | tf_op jit(solution)/shard_map/ppermute | solution.py:341
  58.0 10.2 %collective-permute-start.10 = (f32[7,64,128]{2,1,0:T(8,128)S(1)}, f32[7,64,128]{2,1,0:T(8,128)S(1)}, u32[]{:S(2)}, u32[]{:S(2)}) collective-permute-start(f32[7,64,128]{2,1,0:T(8,128)S(1)} %dynamic-slice_add_fusion), channel_id=1, source_target_pairs={{0,1},{1,2},{2,3},{3,4},{4,5},{5,6},{6,7},{7,8},{8,9},{9,10},{10,1... | collective-permute-start | bytes 688136 | tf_op jit(solution)/shard_map/ppermute | solution.py:356
  68.3 17.5 %collective-permute-start.11 = (f32[7,64,128]{2,1,0:T(8,128)S(1)}, f32[7,64,128]{2,1,0:T(8,128)S(1)}, u32[]{:S(2)}, u32[]{:S(2)}) collective-permute-start(f32[7,64,128]{2,1,0:T(8,128)S(1)} %collective-permute-done.10.pair_a), channel_id=1, source_target_pairs={{0,16},{16,0},{1,17},{17,1},{2,18},{18,2},{3,19},{19,3},{4,20},{20... | collective-permute-start | bytes 688136 | tf_op jit(solution)/shard_map/ppermute | solution.py:341
  68.3 1.5 %collective-permute-start.4 = (f32[2,8,128]{2,1,0:T(8,128)S(1)}, f32[2,8,128]{2,1,0:T(8,128)S(1)}, u32[]{:S(2)}, u32[]{:S(2)}) collective-permute-start(f32[2,8,128]{2,1,0:T(8,128)S(1)} %get-tuple-element.15), channel_id=1, source_target_pairs={{0,16},{16,0},{1,17},{17,1},{2,18},{18,2},{3,19},{19,3},{4,20},{20... | collective-permute-start | bytes 24584 | tf_op jit(solution)/shard_map/ppermute | solution.py:341
  69.8 4.1 %collective-permute-start.5 = (f32[2,8,128]{2,1,0:T(8,128)S(1)}, f32[2,8,128]{2,1,0:T(8,128)S(1)}, u32[]{:S(2)}, u32[]{:S(2)}) collective-permute-start(f32[2,8,128]{2,1,0:T(8,128)S(1)} %add.60), channel_id=1, source_target_pairs={{0,1},{1,0},{2,3},{3,2},{4,5},{5,4},{6,7},{7,6},{8,9},{9,8},{10,11... | collective-permute-start | bytes 24584 | tf_op jit(solution)/shard_map/ppermute | solution.py:341
  73.9 3.7 %collective-permute-start.6 = (f32[2,8,128]{2,1,0:T(8,128)S(1)}, f32[2,8,128]{2,1,0:T(8,128)S(1)}, u32[]{:S(2)}, u32[]{:S(2)}) collective-permute-start(f32[2,8,128]{2,1,0:T(8,128)S(1)} %add.61), channel_id=1, source_target_pairs={{0,2},{1,3},{2,0},{3,1},{4,6},{5,7},{6,4},{7,5},{8,10},{9,11},{10,... | collective-permute-start | bytes 24584 | tf_op jit(solution)/shard_map/ppermute | solution.py:341
  77.5 3.7 %collective-permute-start.7 = (f32[2,8,128]{2,1,0:T(8,128)S(1)}, f32[2,8,128]{2,1,0:T(8,128)S(1)}, u32[]{:S(2)}, u32[]{:S(2)}) collective-permute-start(f32[2,8,128]{2,1,0:T(8,128)S(1)} %add.62), channel_id=1, source_target_pairs={{0,4},{1,5},{2,6},{3,7},{4,0},{5,1},{6,2},{7,3},{8,12},{9,13},{10,... | collective-permute-start | bytes 24584 | tf_op jit(solution)/shard_map/ppermute | solution.py:341
  81.2 4.5 %collective-permute-start.8 = (f32[2,8,128]{2,1,0:T(8,128)S(1)}, f32[2,8,128]{2,1,0:T(8,128)S(1)}, u32[]{:S(2)}, u32[]{:S(2)}) collective-permute-start(f32[2,8,128]{2,1,0:T(8,128)S(1)} %add.63), channel_id=1, source_target_pairs={{0,8},{1,9},{2,10},{3,11},{4,12},{5,13},{6,14},{7,15},{8,0},{9,1},... | collective-permute-start | bytes 24584 | tf_op jit(solution)/shard_map/ppermute | solution.py:341
  104.2 3.8 %collective-permute-start.17 = (f32[12,64,128]{2,1,0:T(8,128)S(1)}, f32[12,64,128]{2,1,0:T(8,128)S(1)}, u32[]{:S(2)}, u32[]{:S(2)}) collective-permute-start(f32[12,64,128]{2,1,0:T(8,128)S(1)} %get-tuple-element.21.sense_a), channel_id=1, source_target_pairs={{0,16},{16,0},{1,17},{17,1},{2,18},{18,2},{3,19},{19,3},{4,20},{20... | collective-permute-start | bytes 1179656 | tf_op jit(solution)/shard_map/ppermute | solution.py:341
  104.2 1.7 %collective-permute-start.12 = (f32[2,8,128]{2,1,0:T(8,128)S(1)}, f32[2,8,128]{2,1,0:T(8,128)S(1)}, u32[]{:S(2)}, u32[]{:S(2)}) collective-permute-start(f32[2,8,128]{2,1,0:T(8,128)S(1)} %get-tuple-element.20), channel_id=1, source_target_pairs={{0,16},{16,0},{1,17},{17,1},{2,18},{18,2},{3,19},{19,3},{4,20},{20... | collective-permute-start | bytes 24584 | tf_op jit(solution)/shard_map/ppermute | solution.py:341
  105.9 7.9 %collective-permute-start.13 = (f32[2,8,128]{2,1,0:T(8,128)S(1)}, f32[2,8,128]{2,1,0:T(8,128)S(1)}, u32[]{:S(2)}, u32[]{:S(2)}) collective-permute-start(f32[2,8,128]{2,1,0:T(8,128)S(1)} %add.66), channel_id=1, source_target_pairs={{0,1},{1,0},{2,3},{3,2},{4,5},{5,4},{6,7},{7,6},{8,9},{9,8},{10,11... | collective-permute-start | bytes 24584 | tf_op jit(solution)/shard_map/ppermute | solution.py:341
  108.0 17.8 %collective-permute-start.19 = (f32[1,64,128]{2,1,0:T(8,128)S(1)}, f32[1,64,128]{2,1,0:T(8,128)S(1)}, u32[]{:S(2)}, u32[]{:S(2)}) collective-permute-start(f32[1,64,128]{2,1,0:T(8,128)S(1)} %get-tuple-element.27), channel_id=1, source_target_pairs={{1,0},{2,1},{3,2},{4,3},{5,4},{6,5},{7,6},{8,7},{9,8},{10,9},{11,1... | collective-permute-start | bytes 98312 | tf_op jit(solution)/shard_map/ppermute | solution.py:347
  109.3 16.5 %collective-permute-start.18 = (f32[1,64,128]{2,1,0:T(8,128)S(1)}, f32[1,64,128]{2,1,0:T(8,128)S(1)}, u32[]{:S(2)}, u32[]{:S(2)}) collective-permute-start(f32[1,64,128]{2,1,0:T(8,128)S(1)} %get-tuple-element.28), channel_id=1, source_target_pairs={{0,1},{1,2},{2,3},{3,4},{4,5},{5,6},{6,7},{7,8},{8,9},{9,10},{10,1... | collective-permute-start | bytes 98312 | tf_op jit(solution)/shard_map/ppermute | solution.py:347
  113.8 3.7 %collective-permute-start.14 = (f32[2,8,128]{2,1,0:T(8,128)S(1)}, f32[2,8,128]{2,1,0:T(8,128)S(1)}, u32[]{:S(2)}, u32[]{:S(2)}) collective-permute-start(f32[2,8,128]{2,1,0:T(8,128)S(1)} %add.67), channel_id=1, source_target_pairs={{0,2},{1,3},{2,0},{3,1},{4,6},{5,7},{6,4},{7,5},{8,10},{9,11},{10,... | collective-permute-start | bytes 24584 | tf_op jit(solution)/shard_map/ppermute | solution.py:341
  117.6 3.7 %collective-permute-start.15 = (f32[2,8,128]{2,1,0:T(8,128)S(1)}, f32[2,8,128]{2,1,0:T(8,128)S(1)}, u32[]{:S(2)}, u32[]{:S(2)}) collective-permute-start(f32[2,8,128]{2,1,0:T(8,128)S(1)} %add.68), channel_id=1, source_target_pairs={{0,4},{1,5},{2,6},{3,7},{4,0},{5,1},{6,2},{7,3},{8,12},{9,13},{10,... | collective-permute-start | bytes 24584 | tf_op jit(solution)/shard_map/ppermute | solution.py:341
  121.2 4.5 %collective-permute-start.16 = (f32[2,8,128]{2,1,0:T(8,128)S(1)}, f32[2,8,128]{2,1,0:T(8,128)S(1)}, u32[]{:S(2)}, u32[]{:S(2)}) collective-permute-start(f32[2,8,128]{2,1,0:T(8,128)S(1)} %add.69), channel_id=1, source_target_pairs={{0,8},{1,9},{2,10},{3,11},{4,12},{5,13},{6,14},{7,15},{8,0},{9,1},... | collective-permute-start | bytes 24584 | tf_op jit(solution)/shard_map/ppermute | solution.py:341
  (9 other events, 9.1 us)

commit v2 on v1

v2 whole, which is shorter than its diff:
```python
import functools

import jax
import jax.numpy as jnp
from jax import lax
from jax.experimental import pallas as pl
from jax.experimental.pallas import tpu as pltpu
from jax.sharding import PartitionSpec as P

SWEEPS = 5

stiff_floor = 0.01
mass_shift = 0.1
spectrum_low = 0.05
spectrum_high = 2.0
moment_decay = 0.8
step_size = 0.1
volume_pull = 0.5
volume_target = 0.4
density_floor = 0.001

SOURCE = SWEEPS
DESIGN = SWEEPS + 1
SENSE = SWEEPS + 2


def chebyshev_factors():
    centre = 0.5 * (spectrum_high + spectrum_low)
    half_width = 0.5 * (spectrum_high - spectrum_low)
    ratio_one = centre / half_width
    previous = 1.0 / ratio_one
    factors = []
    for _ in range(SWEEPS - 1):
        current = 1.0 / (2.0 * ratio_one - previous)
        factors.append((current * previous, 2.0 * current / half_width))
        previous = current
    return 1.0 / centre, factors


def shifted(plane):
    size_y, size_z = plane.shape
    return (
        pltpu.roll(plane, 1, 0),
        pltpu.roll(plane, size_y - 1, 0),
        pltpu.roll(plane, 1, 1),
        pltpu.roll(plane, size_z - 1, 1),
    )


def inner_masks(shape):
    along_y = lax.broadcasted_iota(jnp.int32, shape, 0)
    along_z = lax.broadcasted_iota(jnp.int32, shape, 1)
    return (along_y > 0, along_y < shape[0] - 1, along_z > 0, along_z < shape[1] - 1)


def beside_planes(plane, masks):
    return tuple(jnp.where(mask, moved, 0.0) for mask, moved in zip(masks, shifted(plane)))


def edge_planes(masks):
    edges = sum((1.0 - mask.astype(jnp.float32)) for mask in masks)
    return 1.0 / (8.0 - edges), 1.0 / (7.0 - edges)


def stiffness_of(design):
    return stiff_floor + (1.0 - stiff_floor) * (design * design * design)


def weight_row(q, is_free, stiff, weight, inverse, masks):
    here, below, above = stiff[q + 1], stiff[q], stiff[q + 2]
    around = (below, above) + beside_planes(here, masks)
    total = around[0]
    for plane in around[1:]:
        total = total + plane
    diagonal = (3.0 + mass_shift) * here + 0.5 * total
    scale = jnp.where(is_free, 1.0 / diagonal, 0.0)
    inverse[q] = scale
    half = 0.5 * scale
    weight[0, q] = half * (here + below)
    weight[1, q] = half * (here + above)
    for j in range(4):
        weight[2 + j, q] = jnp.where(masks[j], half * (here + around[2 + j]), 0.0)


class Kept:
    def __init__(self):
        self.places = {}

    def put(self, key, ref, index, value):
        ref[index] = value
        self.places[key] = (ref, index)

    def get(self, key):
        ref, index = self.places[key]
        return ref[index]


def sweep_row(k, q, loads, weight, resid, steps, resid_to, steps_to, shown_to, shown):
    _, factors = chebyshev_factors()
    keep, gain = factors[k]
    last = k == len(factors) - 1
    faces = [weight[j, q] for j in range(6)]
    for l in range(loads):
        here = steps.get((k, l, q))
        total = faces[0] * steps.get((k, l, q - 1)) + faces[1] * steps.get((k, l, q + 1))
        for face, moved in zip(faces[2:], shifted(here)):
            total = total + face * moved
        left = resid.get((l, q)) - here + total
        step = keep * here + gain * left
        if last:
            for earlier in range(k + 1):
                step = step + steps.get((earlier, l, q))
            shown.put((l, q), shown_to, (l, q - (SWEEPS - 1)), step)
        else:
            resid.put((l, q), resid_to, (l, q), left)
            steps.put((k + 1, l, q), steps_to, (k + 1, l, q), step)


def energy_row(i, loads, design, shown, masks):
    q = i + SOURCE
    energy = None
    for l in range(loads):
        here = shown.get((l, q))
        around = (shown.get((l, q - 1)), shown.get((l, q + 1))) + beside_planes(here, masks)
        spread = None
        for plane in around:
            gap = here - plane
            spread = gap * gap if spread is None else spread + gap * gap
        part = mass_shift * (here * here) + 0.25 * spread
        energy = part if energy is None else energy + part
    return (-3.0 * (1.0 - stiff_floor)) * (design * design) * energy


def fold(plane):
    return jnp.sum(plane.reshape(plane.shape[0] // 8, 8, plane.shape[1]), axis=0)


def filter_total(cells, sense, is_first, is_last, masks):
    inside, outer = edge_planes(masks)
    usual = 4.0 * inside + sum(beside_planes(inside, masks))
    at_end = 2.0 * outer + inside + sum(beside_planes(outer, masks))
    zero = jnp.zeros_like(inside)
    total = sense[0]
    for i in range(1, cells):
        total = total + sense[i]
    ends = jnp.where(is_first, sense[0], zero) + jnp.where(is_last, sense[cells - 1], zero)
    nexts = jnp.where(is_first, sense[1], zero) + jnp.where(is_last, sense[cells - 2], zero)
    return -fold(total * usual + ends * (at_end - usual) + nexts * (outer - inside))


def fold_rows(cells, ref):
    total = ref[0]
    for i in range(1, cells):
        total = total + ref[i]
    return fold(total)


def points_kernel(cells, loads, place, nodes, forces, force_ref, base_ref):
    rows = cells + 2 * SOURCE
    size_y, size_z = base_ref.shape[2:]
    zero = jnp.zeros((size_y, size_z), jnp.float32)
    for l in range(loads):
        for q in range(rows):
            own = SOURCE <= q < SOURCE + cells
            base_ref[l, q] = force_ref[l, q - SOURCE] if own else zero
    first = place[4]
    along_z = lax.broadcasted_iota(jnp.int32, (1, size_z), 1)
    for l in range(loads):

        def one_point(p, carry, l=l):
            cell = nodes[l, p] - first

            @pl.when((cell >= 0) & (cell < rows * size_y * size_z))
            def _():
                line, z = cell // size_z, cell % size_z
                q, y = line // size_y, line % size_y
                spot = (l, q, pl.ds(y, 1), slice(None))
                base_ref[spot] = base_ref[spot] + jnp.where(along_z == z, forces[l, p], 0.0)

            return carry

        lax.fori_loop(0, nodes.shape[1], one_point, 0)


def inner_steps(cells, rows):
    return [range(SOURCE + k, SOURCE + cells - k) for k in range(SWEEPS)]


def early_kernel(cells, loads, place, self_weight, design_ref, free_ref, base_ref, pair_a, pair_b,
                 design_wide, free_wide, weight, inverse, resid_ref, steps_ref, shown_ref, stiff):
    even, is_first, is_last = place[0] == 1, place[1] == 1, place[2] == 1
    shape = design_ref.shape[1:]
    masks = inner_masks(shape)
    rows = cells + 2 * SOURCE
    zero = jnp.zeros(shape, jnp.float32)
    for i in range(DESIGN):
        low = jnp.where(even, pair_a[i], pair_b[i])
        high = jnp.where(even, pair_b[i], pair_a[i])
        design_wide[i] = low
        design_wide[DESIGN + cells + i] = high
        stiff[i] = jnp.where(is_first, zero, stiffness_of(low))
        stiff[DESIGN + cells + i] = jnp.where(is_last, zero, stiffness_of(high))
    for i in range(SOURCE):
        low = jnp.where(even, pair_a[DESIGN + i], pair_b[DESIGN + i])
        high = jnp.where(even, pair_b[DESIGN + i], pair_a[DESIGN + i])
        free_wide[i] = jnp.where(is_first, zero, low)
        free_wide[SOURCE + cells + i] = jnp.where(is_last, zero, high)
    for i in range(cells):
        design_wide[DESIGN + i] = design_ref[i]
        stiff[DESIGN + i] = stiffness_of(design_ref[i])
        free_wide[SOURCE + i] = free_ref[i]
    for q in range(rows):
        weight_row(q, free_wide[q] > 0.5, stiff, weight, inverse, masks)
    first_scale, _ = chebyshev_factors()
    resid, steps, shown = Kept(), Kept(), Kept()
    inner = inner_steps(cells, rows)
    for q in inner[0]:
        for l in range(loads):
            left = inverse[q] * (base_ref[l, q] + self_weight[l] * design_wide[q + 1])
            resid.put((l, q), resid_ref, (l, q), left)
            steps.put((0, l, q), steps_ref, (0, l, q), first_scale * left)
    for k in range(SWEEPS - 1):
        for q in inner[k + 1]:
            sweep_row(k, q, loads, weight, resid, steps, resid_ref, steps_ref, shown_ref, shown)


def first_kernel(cells, loads, place, self_weight, force_lo, force_hi, base_in, design_wide, weight, inverse,
                 resid_in, steps_in, shown_in, sense_ref, tile_ref, base_ref, resid_ref, steps_ref, shown_ref):
    is_first, is_last = place[1] == 1, place[2] == 1
    shape = design_wide.shape[1:]
    masks = inner_masks(shape)
    rows = cells + 2 * SOURCE
    first_scale, _ = chebyshev_factors()
    resid, steps, shown = Kept(), Kept(), Kept()
    inner = inner_steps(cells, rows)
    for l in range(loads):
        for k in range(SWEEPS - 1):
            for q in inner[k]:
                steps.places[(k, l, q)] = (steps_in, (k, l, q))
        for q in inner[0]:
            resid.places[(l, q)] = (resid_in, (l, q))
        for q in inner[SWEEPS - 1]:
            shown.places[(l, q)] = (shown_in, (l, q - (SWEEPS - 1)))
    for l in range(loads):
        for q in range(rows):
            base = base_in[l, q]
            if q in inner[0]:
                base_ref[l, q] = base
                continue
            base = base + (force_lo[l, q] if q < SOURCE else force_hi[l, q - SOURCE - cells])
            base_ref[l, q] = base
            left = inverse[q] * (base + self_weight[l] * design_wide[q + 1])
            resid.put((l, q), resid_ref, (l, q), left)
            steps.put((0, l, q), steps_ref, (0, l, q), first_scale * left)
    for k in range(SWEEPS - 1):
        for q in range(k + 1, rows - k - 1):
            if q not in inner[k + 1]:
                sweep_row(k, q, loads, weight, resid, steps, resid_ref, steps_ref, shown_ref, shown)
    for i in range(cells):
        sense_ref[i] = energy_row(i, loads, design_wide[DESIGN + i], shown, masks)
    tile_ref[0] = filter_total(cells, sense_ref, is_first, is_last, masks)
    tile_ref[1] = fold_rows(cells, design_wide.at[pl.ds(DESIGN, cells)])


def moment_kernel(cells, place, sense_a, sense_b, pair_a, pair_b, moment_ref, sense_wide):
    even, is_first, is_last = place[0] == 1, place[1] == 1, place[2] == 1
    shape = sense_a.shape[1:]
    masks = inner_masks(shape)
    zero = jnp.zeros(shape, jnp.float32)
    for i in range(SENSE):
        low = jnp.where(even, pair_a[i], pair_b[i])
        high = jnp.where(even, pair_b[i], pair_a[i])
        sense_wide[i] = jnp.where(is_first, zero, low)
        sense_wide[SENSE + cells + i] = jnp.where(is_last, zero, high)
    for i in range(cells):
        sense_wide[SENSE + i] = sense_a[i] + sense_b[i]
    inside, outer = edge_planes(masks)
    for r in range(cells + 2 * DESIGN):
        at_end = (is_first & (r == DESIGN)) | (is_last & (r == DESIGN + cells - 1))
        moment_ref[r] = filtered_row(r, sense_wide, masks) * jnp.where(at_end, outer, inside)


def filtered_row(r, sense_wide, masks):
    here = sense_wide[r + 1]
    total = 2.0 * here + sense_wide[r] + sense_wide[r + 2]
    for plane in beside_planes(here, masks):
        total = total + plane
    return total


def rate_and_pull(abs_tile, density_tile, total_cells, share):
    abs_total = jnp.sum(abs_tile, keepdims=True)
    density_total = jnp.sum(density_tile, keepdims=True) * share
    mean_step = abs_total / total_cells + 1e-6
    return step_size / mean_step, volume_pull * (density_total / total_cells - volume_target)


def second_kernel(cells, loads, total_cells, share, place, self_weight, tile_in, moment_wide,
                  design_wide, free_wide, base_wide,
                  shown_ref, sense_ref, tile_ref, design_out,
                  stiff, weight, inverse, resid_ref, steps_ref, shown_to, design_new):
    is_first, is_last = place[1] == 1, place[2] == 1
    shape = moment_wide.shape[1:]
    masks = inner_masks(shape)
    wide = cells + 2 * DESIGN
    rows = cells + 2 * SOURCE
    zero = jnp.zeros(shape, jnp.float32)
    rate, pull = rate_and_pull(tile_in[0], tile_in[1], total_cells, share)
    for r in range(wide):
        before = design_wide[r]
        moved = jnp.clip(before - rate * moment_wide[r] - pull, density_floor, 1.0)
        fixed = (before == density_floor) | (before == 1.0)
        design = jnp.where(fixed, before, moved)
        design_new[r] = design
        stiffness = stiffness_of(design)
        if r < DESIGN:
            stiff[r] = jnp.where(is_first, zero, stiffness)
        elif r >= DESIGN + cells:
            stiff[r] = jnp.where(is_last, zero, stiffness)
        else:
            stiff[r] = stiffness
            design_out[r - DESIGN] = design
    resid, steps, shown = Kept(), Kept(), Kept()
    first_scale, _ = chebyshev_factors()
    for q in range(rows):
        weight_row(q, free_wide[q] > 0.5, stiff, weight, inverse, masks)
        scale, design = inverse[q], design_new[q + 1]
        for l in range(loads):
            left = scale * (base_wide[l, q] + self_weight[l] * design)
            resid.put((l, q), resid_ref, (l, q), left)
            steps.put((0, l, q), steps_ref, (0, l, q), first_scale * left)
    for k in range(SWEEPS - 1):
        for q in range(k + 1, rows - k - 1):
            sweep_row(k, q, loads, weight, resid, steps, resid_ref, steps_ref, shown_to, shown)
    for i in range(cells):
        for l in range(loads):
            shown_ref[l, i] = shown.get((l, i + SOURCE))
        sense_ref[i] = energy_row(i, loads, design_out[i], shown, masks)
    tile_ref[0] = filter_total(cells, sense_ref, is_first, is_last, masks)
    tile_ref[1] = fold_rows(cells, design_out)


def last_moment_kernel(cells, slab, place, sense_a, sense_b, pair_a, pair_b, moment_wide,
                       momentum_ref, sense_wide, momentum_all):
    even, is_first, is_last, start = place[0] == 1, place[1] == 1, place[2] == 1, place[3]
    shape = sense_a.shape[1:]
    masks = inner_masks(shape)
    zero = jnp.zeros(shape, jnp.float32)
    sense_wide[0] = jnp.where(is_first, zero, jnp.where(even, pair_a[0], pair_b[0]))
    sense_wide[cells + 1] = jnp.where(is_last, zero, jnp.where(even, pair_b[0], pair_a[0]))
    for i in range(cells):
        sense_wide[i + 1] = sense_a[i] + sense_b[i]
    inside, outer = edge_planes(masks)
    for i in range(cells):
        scale = inside
        if i == 0:
            scale = jnp.where(is_first, outer, inside)
        elif i == cells - 1:
            scale = jnp.where(is_last, outer, inside)
        momentum_all[i] = moment_decay * moment_wide[DESIGN + i] + filtered_row(i, sense_wide, masks) * scale
    momentum_ref[...] = momentum_all[:, pl.ds(pl.multiple_of(start, 8), slab), :]


def last_kernel(cells, slab, total_cells, share, place, tile_before, tile_in, momentum_ref, design_in, passive_ref,
                design_ref):
    window = pl.ds(pl.multiple_of(place[3], 8), slab)
    rate, pull = rate_and_pull(moment_decay * tile_before[0] + tile_in[0], tile_in[1], total_cells, share)
    for i in range(cells):
        moved = jnp.clip(design_in[i, window, :] - rate * momentum_ref[i] - pull, density_floor, 1.0)
        kind = passive_ref[i, window, :]
        design_ref[i] = jnp.where(kind == 1, density_floor, jnp.where(kind == 2, 1.0, moved))


VMEM = pl.BlockSpec(memory_space=pltpu.VMEM)
SMEM = pl.BlockSpec(memory_space=pltpu.SMEM)


def on_core(kernel, operands, scalars, outs, scratch, limit=24):
    return pl.pallas_call(
        kernel,
        out_shape=[jax.ShapeDtypeStruct(shape, jnp.float32) for shape in outs],
        in_specs=[SMEM] * scalars + [VMEM] * (len(operands) - scalars),
        out_specs=[VMEM] * len(outs),
        scratch_shapes=[pltpu.VMEM(shape, jnp.float32) for shape in scratch],
        compiler_params=pltpu.CompilerParams(vmem_limit_bytes=limit * 1024 * 1024),
    )(*operands)


def swap(value, axis, bit):
    count = lax.axis_size(axis)
    return lax.ppermute(value, axis, [(i, i ^ bit) for i in range(count)])


def along(value, step):
    count = lax.axis_size("brick")
    pairs = [(i, i + step) for i in range(count) if 0 <= i + step < count]
    return lax.ppermute(value, "brick", pairs)


def both_ways(value):
    count, loads = lax.axis_size("brick"), lax.axis_size("load")
    pairs = []
    for l in range(loads):
        step = 1 if l % 2 == 0 else -1
        pairs += [(l * count + i, l * count + i + step) for i in range(count) if 0 <= i + step < count]
    return lax.ppermute(value, ("load", "brick"), pairs)


def bits_of(count):
    return [1 << k for k in range(count.bit_length() - 1)]


def sum_over(value, axis):
    for bit in bits_of(lax.axis_size(axis)):
        value = value + swap(value, axis, bit)
    return value


def load_terms(value):
    bits = bits_of(lax.axis_size("load"))
    for bit in bits[:-1]:
        value = value + swap(value, "load", bit)
    return value, swap(value, "load", bits[-1])


def after(value, other):
    return lax.optimization_barrier((value, other))[0]


def meet(sense, tiles, width, even):
    cells = sense.shape[0]
    tiles = sum_over(tiles, "load")
    sense_a, sense_b = load_terms(after(sense, tiles))
    bits = bits_of(lax.axis_size("brick"))
    tiles = tiles + swap(tiles, "brick", bits[0])
    start = jnp.where(even, cells - width, 0)
    sense_a, sense_b = after((sense_a, sense_b), tiles)
    edge = lax.dynamic_slice_in_dim(sense_a, start, width, 0) + lax.dynamic_slice_in_dim(sense_b, start, width, 0)
    pair_a = both_ways(edge)
    for bit in bits[1:-1]:
        tiles = tiles + swap(tiles, "brick", bit)
    pair_b = swap(after(pair_a, tiles), "load", 1)
    tiles = tiles + swap(tiles, "brick", bits[-1])
    return sense_a, sense_b, pair_a, pair_b, tiles


def body(density, passive, support, load_nodes, load_force, self_weight, body_force):
    cells, size_y, size_z = density.shape
    loads = body_force.shape[0]
    bricks, brick = lax.axis_size("brick"), lax.axis_index("brick")
    load_count, load_index = lax.axis_size("load"), lax.axis_index("load")
    slab = size_y // load_count
    total_cells = float(cells * bricks * size_y * size_z)
    share = 1.0 / load_count
    even = load_index % 2 == 0
    first_cell = (brick * cells - SOURCE) * size_y * size_z
    place = jnp.stack([even, brick == 0, brick == bricks - 1, load_index * slab, first_cell]).astype(jnp.int32)
    plane = (size_y, size_z)
    wide, rows = cells + 2 * DESIGN, cells + 2 * SOURCE
    tile = (2, 8, size_z)
    shown_shape = (loads, cells + 2) + plane
    resid_shape = (loads, rows) + plane
    steps_shape = (SWEEPS - 1, loads, rows) + plane

    free = (1 - support).astype(jnp.float32)
    design = jnp.where(passive == 1, density_floor, jnp.where(passive == 2, 1.0, density))
    upward = jnp.concatenate([design[cells - DESIGN:], free[cells - SOURCE:]])
    downward = jnp.concatenate([design[:DESIGN], free[:SOURCE]])
    pair_a = both_ways(jnp.where(even, upward, downward))
    pair_b = swap(pair_a, "load", 1)
    force_lo = along(body_force[:, cells - SOURCE:], 1)
    force_hi = along(body_force[:, :SOURCE], -1)
    (base,) = on_core(
        functools.partial(points_kernel, cells, loads),
        (place, load_nodes, load_force, body_force),
        3,
        [resid_shape],
        [],
    )
    design_wide, free_wide, weight, inverse, resid, steps, shown = on_core(
        functools.partial(early_kernel, cells, loads),
        (place, self_weight, design, free, base, pair_a, pair_b),
        2,
        [(wide,) + plane, (rows,) + plane, (6, rows) + plane, (rows,) + plane, resid_shape, steps_shape, shown_shape],
        [(wide,) + plane],
    )
    sense, tiles, base_wide = on_core(
        functools.partial(first_kernel, cells, loads),
        (place, self_weight, force_lo, force_hi, base, design_wide, weight, inverse, resid, steps, shown),
        2,
        [(cells,) + plane, tile, resid_shape],
        [resid_shape, steps_shape, shown_shape],
    )
    sense_a, sense_b, pair_a, pair_b, tiles_first = meet(sense, tiles, SENSE, even)
    (moment_wide,) = on_core(
        functools.partial(moment_kernel, cells),
        (place, sense_a, sense_b, pair_a, pair_b),
        1,
        [(wide,) + plane],
        [(cells + 2 * SENSE,) + plane],
    )
    shown, sense, tiles, design = on_core(
        functools.partial(second_kernel, cells, loads, total_cells, share),
        (place, self_weight, tiles_first, moment_wide, design_wide, free_wide, base_wide),
        2,
        [(loads, cells) + plane, (cells,) + plane, tile, (cells,) + plane],
        [(wide,) + plane, (6, rows) + plane, (rows,) + plane, resid_shape, steps_shape, shown_shape, (wide,) + plane],
    )
    sense_a, sense_b, pair_a, pair_b, tiles_last = meet(sense, tiles, 1, even)
    (momentum,) = on_core(
        functools.partial(last_moment_kernel, cells, slab),
        (place, sense_a, sense_b, pair_a, pair_b, moment_wide),
        1,
        [(cells, slab, size_z)],
        [(cells + 2,) + plane, (cells,) + plane],
    )
    (design,) = on_core(
        functools.partial(last_kernel, cells, slab, total_cells, share),
        (place, tiles_first, tiles_last, momentum, design, passive),
        1,
        [(cells, slab, size_z)],
        [],
    )
    return design, momentum, shown


def solution(mesh):
    placed = (
        P("brick", None, None),
        P("brick", None, None),
        P("brick", None, None),
        P("load", None),
        P("load", None),
        P("load"),
        P("load", "brick", None, None),
    )
    return jax.shard_map(
        body,
        mesh=mesh,
        in_specs=placed,
        out_specs=(
            P("brick", "load", None),
            P("brick", "load", None),
            P("load", "brick", None, None),
        ),
        check_vma=False,
    )
```

time: 129 us -> 99.3 us (0.77)
  other arithmetic: 20.6 us -> 1.38 us
  Pallas kernels: 33.1 us -> 20.7 us
  waiting for transfers between devices: 26.2 us -> 37.5 us
  local copies, waits for them, and re-layouts: 11.9 us -> 7.06 us
  starting transfers between devices: 35.7 us -> 31.4 us
    scatter-add x1 -> x0, other arithmetic: 19.3 us -> none  [place_points(): jnp.zeros((loads_here, span_cells + 1), jnp.float32).at[row_ids, slot_ids]]
    pallas_call x3 -> x7, Pallas kernels: 33.1 us -> 20.7 us  [on_core(): pl.pallas_call(kernel, out_shape=[jax.ShapeDtypeStruct(shape, jnp.float32...]
    ppermute x4 -> x2, waiting for transfers between devices: 0.01 us -> 7.6 us  [along(): return lax.ppermute(value, 'brick', pairs)]
    ppermute x4 -> x2, starting transfers between devices: 11.7 us -> 5.82 us  [along(): return lax.ppermute(value, 'brick', pairs)]
    unnamed x29 -> x34, local copies, waits for them, and re-layouts: 9.53 us -> 6.13 us
    ppermute x2 -> x3, waiting for transfers between devices: 6 us -> 8.77 us  [both_ways(): return lax.ppermute(value, ('load', 'brick'), pairs)]
    ppermute x2 -> x3, starting transfers between devices: 9.22 us -> 11.8 us  [both_ways(): return lax.ppermute(value, ('load', 'brick'), pairs)]
    broadcast_in_dim x1 -> x0, local copies, waits for them, and re-layouts: 1.34 us -> none  [place_points(): jnp.zeros((loads_here, span_cells + 1), jnp.float32).at[row_ids, slot_ids]]
  transfers between devices with their start and end apart: 20 -> 20, of which waited for: 11 -> 12; matrix products, arithmetic and copies ran while one was open for 19% -> 1% of each run, Pallas kernels for 0% -> 6%
where the time goes in v2:
time: 99.3 us; the launch traced here: 98.9 us
  waiting for transfers between devices  37.5 us (38%)
  starting transfers between devices  31.4 us (32%)
  Pallas kernels  20.7 us (21%)
  local copies, waits for them, and re-layouts  7.06 us (7%)
  other arithmetic  1.38 us (1%)
    ppermute x15, waiting for transfers between devices, swap(): return lax.ppermute(value, axis, [(i, i ^ bit) for i in range(count)])  21.1 us
    pallas_call x7, Pallas kernels, on_core(): pl.pallas_call(kernel, out_shape=[jax.ShapeDtypeStruct(shape, jnp.float32...  20.7 us
    ppermute x15, starting transfers between devices, swap(): return lax.ppermute(value, axis, [(i, i ^ bit) for i in range(count)])  13.7 us
    ppermute x3, starting transfers between devices, both_ways(): return lax.ppermute(value, ('load', 'brick'), pairs)  11.8 us
    ppermute x3, waiting for transfers between devices, both_ways(): return lax.ppermute(value, ('load', 'brick'), pairs)  8.77 us
    ppermute x2, waiting for transfers between devices, along(): return lax.ppermute(value, 'brick', pairs)  7.6 us
    unnamed x34, local copies, waits for them, and re-layouts  6.13 us
    ppermute x2, starting transfers between devices, along(): return lax.ppermute(value, 'brick', pairs)  5.82 us
  transfers between devices with their start and end apart: 20, of which 12 were waited for; matrix products, arithmetic and copies ran while one was open for 1% of the time, Pallas kernels for 6%

profile of v2, /device:TPU:0, one launch (start us, length us, event | category | flops | bytes accessed | tf_op | source)
XLA Modules:
  0.0 98.9 jit_solution(14099033580483915514)
XLA Ops:
  2.1 5.0 %collective-permute-start.2 = (f32[11,64,128]{2,1,0:T(8,128)S(1)}, f32[11,64,128]{2,1,0:T(8,128)S(1)}, u32[]{:S(2)}, u32[]{:S(2)}) collective-permute-start(f32[11,64,128]{2,1,0:T(8,128)S(1)} %maximum_select_fusion), channel_id=1, source_target_pairs={{0,1},{1,2},{2,3},{3,4},{4,5},{5,6},{6,7},{7,8},{8,9},{9,10},{10,1... | collective-permute-start | bytes 1081352 | tf_op jit(solution)/shard_map/ppermute | solution.py:406
  7.1 8.8 %collective-permute-done.2.pair_a = f32[11,64,128]{2,1,0:T(8,128)S(1)} collective-permute-done((f32[11,64,128]{2,1,0:T(8,128)S(1)}, f32[11,64,128]{2,1,0:T(8,128)S(1)}, u32[]{:S(2)}, u32[]{:S(2)}) %collective-permute-start.2) | collective-permute-done | bytes 360480 | tf_op jit(solution)/shard_map/ppermute | solution.py:406
  16.7 4.5 %collective-permute-start = (f32[2,5,64,128]{3,2,1,0:T(8,128)}, f32[2,5,64,128]{3,2,1,0:T(8,128)S(1)}, u32[]{:S(2)}, u32[]{:S(2)}) collective-permute-start(f32[2,5,64,128]{3,2,1,0:T(8,128)} %get-tuple-element.48), channel_id=1, source_target_pairs={{0,1},{1,2},{2,3},{3,4},{4,5},{5,6},{6,7},{7,8},{8,9},{9,10},{10,1... | collective-permute-start | bytes 983048 | tf_op jit(solution)/shard_map/ppermute | solution.py:397
  22.6 2.8 %shard_map.94.base_ref.base_in = f32[2,22,64,128]{3,2,1,0:T(8,128)S(1)} custom-call(s32[5]{0:T(128)S(1)} %stack.35.place, s32[2,64]{1,0:T(2,128)S(1)} %copy-done.14, f32[2,64]{1,0:T(2,128)S(1)} %copy-done.15, f32[2,12,64,128]{3,2,1,0:T(8,128)S(1)} %copy-done), custom_call_target="tpu_custom_call" | custom-call | tf_op jit(solution)/shard_map/pallas_call | solution.py:379
  25.4 3.1 %shard_map.95 = (f32[24,64,128]{2,1,0:T(8,128)S(1)}, f32[22,64,128]{2,1,0:T(8,128)S(1)}, f32[6,22,64,128]{3,2,1,0:T(8,128)S(1)}, f32[22,64,128]{2,1,0:T(8,128)S(...) custom-call(s32[5]{0:T(128)S(1)} %stack.35.place, ...), custom_call_target="tpu_custom_call" | custom-call | tf_op jit(solution)/shard_map/pallas_call | solution.py:379
  28.5 7.6 %collective-permute-done.force_lo = f32[2,5,64,128]{3,2,1,0:T(8,128)S(1)} collective-permute-done((f32[2,5,64,128]{3,2,1,0:T(8,128)}, f32[2,5,64,128]{3,2,1,0:T(8,128)S(1)}, u32[]{:S(2)}, u32[]{:S(2)}) %collective-permute-start) | collective-permute-done | bytes 327712 | tf_op jit(solution)/shard_map/ppermute | solution.py:397
  39.6 3.6 %shard_map.96 = (f32[12,64,128]{2,1,0:T(8,128)S(1)}, f32[2,8,128]{2,1,0:T(8,128)S(1)}, f32[2,22,64,128]{3,2,1,0:T(8,128)S(1)}) custom-call(s32[5]{0:T(128)S(1)} %stack.35.place, f32[2]{0:T(128)S(1)} %copy-done.13, f32[2,5,64,128]{3,2,1,0:T(8,128)S(1)} %copy-done.10, f32[2,5,64,128]{3,2,1,0:T(8,128)S(1)} %copy-done.12, ...), custom_call_target="tpu_custom_call" | custom-call | tf_op jit(solution)/shard_map/pallas_call | solution.py:379
  44.6 2.4 %collective-permute-start.5 = (f32[2,8,128]{2,1,0:T(8,128)S(1)}, f32[2,8,128]{2,1,0:T(8,128)S(1)}, u32[]{:S(2)}, u32[]{:S(2)}) collective-permute-start(f32[2,8,128]{2,1,0:T(8,128)S(1)} %add.46), channel_id=1, source_target_pairs={{0,1},{1,0},{2,3},{3,2},{4,5},{5,4},{6,7},{7,6},{8,9},{9,8},{10,11... | collective-permute-start | bytes 24584 | tf_op jit(solution)/shard_map/ppermute | solution.py:391
  47.0 1.6 %collective-permute-done.5 = f32[2,8,128]{2,1,0:T(8,128)S(1)} collective-permute-done((f32[2,8,128]{2,1,0:T(8,128)S(1)}, f32[2,8,128]{2,1,0:T(8,128)S(1)}, u32[]{:S(2)}, u32[]{:S(2)}) %collective-permute-start.5) | collective-permute-done | bytes 8224 | tf_op jit(solution)/shard_map/ppermute | solution.py:391
  48.7 4.1 %collective-permute-start.10 = (f32[7,64,128]{2,1,0:T(8,128)S(1)}, f32[7,64,128]{2,1,0:T(8,128)S(1)}, u32[]{:S(2)}, u32[]{:S(2)}) collective-permute-start(f32[7,64,128]{2,1,0:T(8,128)S(1)} %dynamic-slice_add_fusion), channel_id=1, source_target_pairs={{0,1},{1,2},{2,3},{3,4},{4,5},{5,6},{6,7},{7,8},{8,9},{9,10},{10,1... | collective-permute-start | bytes 688136 | tf_op jit(solution)/shard_map/ppermute | solution.py:406
  52.9 3.6 %collective-permute-done.6 = f32[2,8,128]{2,1,0:T(8,128)S(1)} collective-permute-done((f32[2,8,128]{2,1,0:T(8,128)S(1)}, f32[2,8,128]{2,1,0:T(8,128)S(1)}, u32[]{:S(2)}, u32[]{:S(2)}) %collective-permute-start.6) | collective-permute-done | bytes 8224 | tf_op jit(solution)/shard_map/ppermute | solution.py:391
  56.5 2.4 %collective-permute-start.7 = (f32[2,8,128]{2,1,0:T(8,128)S(1)}, f32[2,8,128]{2,1,0:T(8,128)S(1)}, u32[]{:S(2)}, u32[]{:S(2)}) collective-permute-start(f32[2,8,128]{2,1,0:T(8,128)S(1)} %add.48), channel_id=1, source_target_pairs={{0,4},{1,5},{2,6},{3,7},{4,0},{5,1},{6,2},{7,3},{8,12},{9,13},{10,... | collective-permute-start | bytes 24584 | tf_op jit(solution)/shard_map/ppermute | solution.py:391
  58.9 1.6 %collective-permute-done.7 = f32[2,8,128]{2,1,0:T(8,128)S(1)} collective-permute-done((f32[2,8,128]{2,1,0:T(8,128)S(1)}, f32[2,8,128]{2,1,0:T(8,128)S(1)}, u32[]{:S(2)}, u32[]{:S(2)}) %collective-permute-start.7) | collective-permute-done | bytes 8224 | tf_op jit(solution)/shard_map/ppermute | solution.py:391
  60.5 3.1 %collective-permute-start.8 = (f32[2,8,128]{2,1,0:T(8,128)S(1)}, f32[2,8,128]{2,1,0:T(8,128)S(1)}, u32[]{:S(2)}, u32[]{:S(2)}) collective-permute-start(f32[2,8,128]{2,1,0:T(8,128)S(1)} %add.49), channel_id=1, source_target_pairs={{0,8},{1,9},{2,10},{3,11},{4,12},{5,13},{6,14},{7,15},{8,0},{9,1},... | collective-permute-start | bytes 24584 | tf_op jit(solution)/shard_map/ppermute | solution.py:391
  63.6 1.6 %collective-permute-done.8 = f32[2,8,128]{2,1,0:T(8,128)S(1)} collective-permute-done((f32[2,8,128]{2,1,0:T(8,128)S(1)}, f32[2,8,128]{2,1,0:T(8,128)S(1)}, u32[]{:S(2)}, u32[]{:S(2)}) %collective-permute-start.8) | collective-permute-done | bytes 8224 | tf_op jit(solution)/shard_map/ppermute | solution.py:391
  67.3 7.3 %shard_map.98 = (f32[2,12,64,128]{3,2,1,0:T(8,128)}, f32[12,64,128]{2,1,0:T(8,128)S(1)}, f32[2,8,128]{2,1,0:T(8,128)S(1)}, f32[12,64,128]{2,1,0:T(8,128)S(1)}) custom-call(s32[5]{0:T(128)S(1)} %stack.35.place, f32[2]{0:T(128)S(1)} %copy-done.13, f32[2,8,128]{2,1,0:T(8,128)S(1)} %add.50.tile_in.tile_before, f32[24,64,128]{2,1,0:T(8,128)S(1)} %shard_map.97.moment_wide, ...), custom_call_target="tpu_custom_call" | custom-call | tf_op jit(solution)/shard_map/pallas_call | solution.py:379
  77.5 2.9 %collective-permute-done.13 = f32[2,8,128]{2,1,0:T(8,128)S(1)} collective-permute-done((f32[2,8,128]{2,1,0:T(8,128)S(1)}, f32[2,8,128]{2,1,0:T(8,128)S(1)}, u32[]{:S(2)}, u32[]{:S(2)}) %collective-permute-start.13) | collective-permute-done | bytes 8224 | tf_op jit(solution)/shard_map/ppermute | solution.py:391
  80.4 2.7 %collective-permute-start.18 = (f32[1,64,128]{2,1,0:T(8,128)S(1)}, f32[1,64,128]{2,1,0:T(8,128)S(1)}, u32[]{:S(2)}, u32[]{:S(2)}) collective-permute-start(f32[1,64,128]{2,1,0:T(8,128)S(1)} %dynamic-slice_add_fusion.1), channel_id=1, source_target_pairs={{0,1},{1,2},{2,3},{3,4},{4,5},{5,6},{6,7},{7,8},{8,9},{9,10},{10,1... | collective-permute-start | bytes 98312 | tf_op jit(solution)/shard_map/ppermute | solution.py:406
  84.4 2.4 %collective-permute-done.14 = f32[2,8,128]{2,1,0:T(8,128)S(1)} collective-permute-done((f32[2,8,128]{2,1,0:T(8,128)S(1)}, f32[2,8,128]{2,1,0:T(8,128)S(1)}, u32[]{:S(2)}, u32[]{:S(2)}) %collective-permute-start.14) | collective-permute-done | bytes 8224 | tf_op jit(solution)/shard_map/ppermute | solution.py:391
  87.9 2.5 %collective-permute-done.15 = f32[2,8,128]{2,1,0:T(8,128)S(1)} collective-permute-done((f32[2,8,128]{2,1,0:T(8,128)S(1)}, f32[2,8,128]{2,1,0:T(8,128)S(1)}, u32[]{:S(2)}, u32[]{:S(2)}) %collective-permute-start.15) | collective-permute-done | bytes 8224 | tf_op jit(solution)/shard_map/ppermute | solution.py:391
  90.4 2.2 %collective-permute-start.16 = (f32[2,8,128]{2,1,0:T(8,128)S(1)}, f32[2,8,128]{2,1,0:T(8,128)S(1)}, u32[]{:S(2)}, u32[]{:S(2)}) collective-permute-start(f32[2,8,128]{2,1,0:T(8,128)S(1)} %add.55), channel_id=1, source_target_pairs={{0,8},{1,9},{2,10},{3,11},{4,12},{5,13},{6,14},{7,15},{8,0},{9,1},... | collective-permute-start | bytes 24584 | tf_op jit(solution)/shard_map/ppermute | solution.py:391
  92.7 2.4 %collective-permute-done.16 = f32[2,8,128]{2,1,0:T(8,128)S(1)} collective-permute-done((f32[2,8,128]{2,1,0:T(8,128)S(1)}, f32[2,8,128]{2,1,0:T(8,128)S(1)}, u32[]{:S(2)}, u32[]{:S(2)}) %collective-permute-start.16) | collective-permute-done | bytes 8224 | tf_op jit(solution)/shard_map/ppermute | solution.py:391
  95.1 1.5 %shard_map.99.momentum_ref = f32[12,32,128]{2,1,0:T(8,128)} custom-call(s32[5]{0:T(128)S(1)} %stack.35.place, f32[12,64,128]{2,1,0:T(8,128)S(1)} %get-tuple-element.42.sense_a, f32[12,64,128]{2,1,0:T(8,128)S(1)} %collective-permute-done.17.sense_b, f32[1,64,128]{2,1,0:T(8,128)S(1)} %collective-permute-done.18.pair_a, ...), custom_call_target="tpu_custom_call" | custom-call | tf_op jit(solution)/shard_map/pallas_call | solution.py:379
  97.5 1.4 %shard_map.100 = f32[12,32,128]{2,1,0:T(8,128)} custom-call(s32[5]{0:T(128)S(1)} %stack.35.place, f32[2,8,128]{2,1,0:T(8,128)S(1)} %add.50.tile_in.tile_before, f32[2,8,128]{2,1,0:T(8,128)S(1)} %add.56.tile_in, f32[12,32,128]{2,1,0:T(8,128)S(1)} %copy-done.4, f32[12,64,128]{2,1,0:T(8,128)S(1)} %copy-done.8, s32[12,64,128]{2,1,0:T(8,128)S(1)} %copy-done.1), custom_call_target="tpu_custom_call" | custom-call | tf_op jit(solution)/shard_map/pallas_call | solution.py:379
  (76 shorter events, 16.8 us)
Async XLA Ops:
  2.0 20.6 %copy-start.14 = (s32[2,64]{1,0:T(2,128)S(1)}, s32[2,64]{1,0:T(2,128)}, u32[]{:S(2)}) copy-start(s32[2,64]{1,0:T(2,128)} %nodes.1) | copy-start | bytes 1540
  2.0 20.6 %copy-start.15 = (f32[2,64]{1,0:T(2,128)S(1)}, f32[2,64]{1,0:T(2,128)}, u32[]{:S(2)}) copy-start(f32[2,64]{1,0:T(2,128)} %forces.1) | copy-start | bytes 1540
  2.1 13.8 %collective-permute-start.2 = (f32[11,64,128]{2,1,0:T(8,128)S(1)}, f32[11,64,128]{2,1,0:T(8,128)S(1)}, u32[]{:S(2)}, u32[]{:S(2)}) collective-permute-start(f32[11,64,128]{2,1,0:T(8,128)S(1)} %maximum_select_fusion), channel_id=1, source_target_pairs={{0,1},{1,2},{2,3},{3,4},{4,5},{5,6},{6,7},{7,8},{8,9},{9,10},{10,1... | collective-permute-start | bytes 1081352 | tf_op jit(solution)/shard_map/ppermute | solution.py:406
  15.9 9.5 %collective-permute-start.3 = (f32[11,64,128]{2,1,0:T(8,128)S(1)}, f32[11,64,128]{2,1,0:T(8,128)S(1)}, u32[]{:S(2)}, u32[]{:S(2)}) collective-permute-start(f32[11,64,128]{2,1,0:T(8,128)S(1)} %collective-permute-done.2.pair_a), channel_id=1, source_target_pairs={{0,16},{16,0},{1,17},{17,1},{2,18},{18,2},{3,19},{19,3},{4,20},{20... | collective-permute-start | bytes 1081352 | tf_op jit(solution)/shard_map/ppermute | solution.py:391
  16.7 19.5 %collective-permute-start = (f32[2,5,64,128]{3,2,1,0:T(8,128)}, f32[2,5,64,128]{3,2,1,0:T(8,128)S(1)}, u32[]{:S(2)}, u32[]{:S(2)}) collective-permute-start(f32[2,5,64,128]{3,2,1,0:T(8,128)} %get-tuple-element.48), channel_id=1, source_target_pairs={{0,1},{1,2},{2,3},{3,4},{4,5},{5,6},{6,7},{7,8},{8,9},{9,10},{10,1... | collective-permute-start | bytes 983048 | tf_op jit(solution)/shard_map/ppermute | solution.py:397
  21.2 15.7 %collective-permute-start.1 = (f32[2,5,64,128]{3,2,1,0:T(8,128)S(1)}, f32[2,5,64,128]{3,2,1,0:T(8,128)S(1)}, u32[]{:S(2)}, u32[]{:S(2)}) collective-permute-start(f32[2,5,64,128]{3,2,1,0:T(8,128)S(1)} %get-tuple-element.47), channel_id=1, source_target_pairs={{1,0},{2,1},{3,2},{4,3},{5,4},{6,5},{7,6},{8,7},{9,8},{10,9},{11,1... | collective-permute-start | bytes 983048 | tf_op jit(solution)/shard_map/ppermute | solution.py:397
  43.2 1.2 %collective-permute-start.4 = (f32[2,8,128]{2,1,0:T(8,128)S(1)}, f32[2,8,128]{2,1,0:T(8,128)S(1)}, u32[]{:S(2)}, u32[]{:S(2)}) collective-permute-start(f32[2,8,128]{2,1,0:T(8,128)S(1)} %get-tuple-element.31), channel_id=1, source_target_pairs={{0,16},{16,0},{1,17},{17,1},{2,18},{18,2},{3,19},{19,3},{4,20},{20... | collective-permute-start | bytes 24584 | tf_op jit(solution)/shard_map/ppermute | solution.py:391
  44.4 4.2 %collective-permute-start.9 = (f32[12,64,128]{2,1,0:T(8,128)S(1)}, f32[12,64,128]{2,1,0:T(8,128)S(1)}, u32[]{:S(2)}, u32[]{:S(2)}) collective-permute-start(f32[12,64,128]{2,1,0:T(8,128)S(1)} %get-tuple-element.34.sense_a), channel_id=1, source_target_pairs={{0,16},{16,0},{1,17},{17,1},{2,18},{18,2},{3,19},{19,3},{4,20},{20... | collective-permute-start | bytes 1179656 | tf_op jit(solution)/shard_map/ppermute | solution.py:391
  44.6 4.0 %collective-permute-start.5 = (f32[2,8,128]{2,1,0:T(8,128)S(1)}, f32[2,8,128]{2,1,0:T(8,128)S(1)}, u32[]{:S(2)}, u32[]{:S(2)}) collective-permute-start(f32[2,8,128]{2,1,0:T(8,128)S(1)} %add.46), channel_id=1, source_target_pairs={{0,1},{1,0},{2,3},{3,2},{4,5},{5,4},{6,7},{7,6},{8,9},{9,8},{10,11... | collective-permute-start | bytes 24584 | tf_op jit(solution)/shard_map/ppermute | solution.py:391
  48.7 11.8 %collective-permute-start.10 = (f32[7,64,128]{2,1,0:T(8,128)S(1)}, f32[7,64,128]{2,1,0:T(8,128)S(1)}, u32[]{:S(2)}, u32[]{:S(2)}) collective-permute-start(f32[7,64,128]{2,1,0:T(8,128)S(1)} %dynamic-slice_add_fusion), channel_id=1, source_target_pairs={{0,1},{1,2},{2,3},{3,4},{4,5},{5,6},{6,7},{7,8},{8,9},{9,10},{10,1... | collective-permute-start | bytes 688136 | tf_op jit(solution)/shard_map/ppermute | solution.py:406
  52.8 3.7 %collective-permute-start.6 = (f32[2,8,128]{2,1,0:T(8,128)S(1)}, f32[2,8,128]{2,1,0:T(8,128)S(1)}, u32[]{:S(2)}, u32[]{:S(2)}) collective-permute-start(f32[2,8,128]{2,1,0:T(8,128)S(1)} %add.47), channel_id=1, source_target_pairs={{0,2},{1,3},{2,0},{3,1},{4,6},{5,7},{6,4},{7,5},{8,10},{9,11},{10,... | collective-permute-start | bytes 24584 | tf_op jit(solution)/shard_map/ppermute | solution.py:391
  56.5 4.0 %collective-permute-start.7 = (f32[2,8,128]{2,1,0:T(8,128)S(1)}, f32[2,8,128]{2,1,0:T(8,128)S(1)}, u32[]{:S(2)}, u32[]{:S(2)}) collective-permute-start(f32[2,8,128]{2,1,0:T(8,128)S(1)} %add.48), channel_id=1, source_target_pairs={{0,4},{1,5},{2,6},{3,7},{4,0},{5,1},{6,2},{7,3},{8,12},{9,13},{10,... | collective-permute-start | bytes 24584 | tf_op jit(solution)/shard_map/ppermute | solution.py:391
  60.5 4.8 %collective-permute-start.11 = (f32[7,64,128]{2,1,0:T(8,128)S(1)}, f32[7,64,128]{2,1,0:T(8,128)S(1)}, u32[]{:S(2)}, u32[]{:S(2)}) collective-permute-start(f32[7,64,128]{2,1,0:T(8,128)S(1)} %collective-permute-done.10.pair_a), channel_id=1, source_target_pairs={{0,16},{16,0},{1,17},{17,1},{2,18},{18,2},{3,19},{19,3},{4,20},{20... | collective-permute-start | bytes 688136 | tf_op jit(solution)/shard_map/ppermute | solution.py:391
  60.5 4.7 %collective-permute-start.8 = (f32[2,8,128]{2,1,0:T(8,128)S(1)}, f32[2,8,128]{2,1,0:T(8,128)S(1)}, u32[]{:S(2)}, u32[]{:S(2)}) collective-permute-start(f32[2,8,128]{2,1,0:T(8,128)S(1)} %add.49), channel_id=1, source_target_pairs={{0,8},{1,9},{2,10},{3,11},{4,12},{5,13},{6,14},{7,15},{8,0},{9,1},... | collective-permute-start | bytes 24584 | tf_op jit(solution)/shard_map/ppermute | solution.py:391
  75.3 21.3 %copy-start.1 = (s32[12,64,128]{2,1,0:T(8,128)S(1)}, s32[12,64,128]{2,1,0:T(8,128)}, u32[]{:S(2)}) copy-start(s32[12,64,128]{2,1,0:T(8,128)} %passive_ref.1) | copy-start | bytes 1179652
  75.3 21.3 %copy-start.8 = (f32[12,64,128]{2,1,0:T(8,128)S(1)}, f32[12,64,128]{2,1,0:T(8,128)}, u32[]{:S(2)}) copy-start(f32[12,64,128]{2,1,0:T(8,128)} %copy-done.7) | copy-start | bytes 1179652
  75.3 1.2 %collective-permute-start.12 = (f32[2,8,128]{2,1,0:T(8,128)S(1)}, f32[2,8,128]{2,1,0:T(8,128)S(1)}, u32[]{:S(2)}, u32[]{:S(2)}) collective-permute-start(f32[2,8,128]{2,1,0:T(8,128)S(1)} %get-tuple-element.39), channel_id=1, source_target_pairs={{0,16},{16,0},{1,17},{17,1},{2,18},{18,2},{3,19},{19,3},{4,20},{20... | collective-permute-start | bytes 24584 | tf_op jit(solution)/shard_map/ppermute | solution.py:391
  76.5 3.8 %collective-permute-start.17 = (f32[12,64,128]{2,1,0:T(8,128)S(1)}, f32[12,64,128]{2,1,0:T(8,128)S(1)}, u32[]{:S(2)}, u32[]{:S(2)}) collective-permute-start(f32[12,64,128]{2,1,0:T(8,128)S(1)} %get-tuple-element.42.sense_a), channel_id=1, source_target_pairs={{0,16},{16,0},{1,17},{17,1},{2,18},{18,2},{3,19},{19,3},{4,20},{20... | collective-permute-start | bytes 1179656 | tf_op jit(solution)/shard_map/ppermute | solution.py:391
  76.7 3.7 %collective-permute-start.13 = (f32[2,8,128]{2,1,0:T(8,128)S(1)}, f32[2,8,128]{2,1,0:T(8,128)S(1)}, u32[]{:S(2)}, u32[]{:S(2)}) collective-permute-start(f32[2,8,128]{2,1,0:T(8,128)S(1)} %add.52), channel_id=1, source_target_pairs={{0,1},{1,0},{2,3},{3,2},{4,5},{5,4},{6,7},{7,6},{8,9},{9,8},{10,11... | collective-permute-start | bytes 24584 | tf_op jit(solution)/shard_map/ppermute | solution.py:391
  80.4 10.1 %collective-permute-start.18 = (f32[1,64,128]{2,1,0:T(8,128)S(1)}, f32[1,64,128]{2,1,0:T(8,128)S(1)}, u32[]{:S(2)}, u32[]{:S(2)}) collective-permute-start(f32[1,64,128]{2,1,0:T(8,128)S(1)} %dynamic-slice_add_fusion.1), channel_id=1, source_target_pairs={{0,1},{1,2},{2,3},{3,4},{4,5},{5,6},{6,7},{7,8},{8,9},{9,10},{10,1... | collective-permute-start | bytes 98312 | tf_op jit(solution)/shard_map/ppermute | solution.py:406
  83.1 3.7 %collective-permute-start.14 = (f32[2,8,128]{2,1,0:T(8,128)S(1)}, f32[2,8,128]{2,1,0:T(8,128)S(1)}, u32[]{:S(2)}, u32[]{:S(2)}) collective-permute-start(f32[2,8,128]{2,1,0:T(8,128)S(1)} %add.53), channel_id=1, source_target_pairs={{0,2},{1,3},{2,0},{3,1},{4,6},{5,7},{6,4},{7,5},{8,10},{9,11},{10,... | collective-permute-start | bytes 24584 | tf_op jit(solution)/shard_map/ppermute | solution.py:391
  86.8 3.7 %collective-permute-start.15 = (f32[2,8,128]{2,1,0:T(8,128)S(1)}, f32[2,8,128]{2,1,0:T(8,128)S(1)}, u32[]{:S(2)}, u32[]{:S(2)}) collective-permute-start(f32[2,8,128]{2,1,0:T(8,128)S(1)} %add.54), channel_id=1, source_target_pairs={{0,4},{1,5},{2,6},{3,7},{4,0},{5,1},{6,2},{7,3},{8,12},{9,13},{10,... | collective-permute-start | bytes 24584 | tf_op jit(solution)/shard_map/ppermute | solution.py:391
  90.4 4.6 %collective-permute-start.19 = (f32[1,64,128]{2,1,0:T(8,128)S(1)}, f32[1,64,128]{2,1,0:T(8,128)S(1)}, u32[]{:S(2)}, u32[]{:S(2)}) collective-permute-start(f32[1,64,128]{2,1,0:T(8,128)S(1)} %collective-permute-done.18.pair_a), channel_id=1, source_target_pairs={{0,16},{16,0},{1,17},{17,1},{2,18},{18,2},{3,19},{19,3},{4,20},{20... | collective-permute-start | bytes 98312 | tf_op jit(solution)/shard_map/ppermute | solution.py:391
  90.4 4.6 %collective-permute-start.16 = (f32[2,8,128]{2,1,0:T(8,128)S(1)}, f32[2,8,128]{2,1,0:T(8,128)S(1)}, u32[]{:S(2)}, u32[]{:S(2)}) collective-permute-start(f32[2,8,128]{2,1,0:T(8,128)S(1)} %add.55), channel_id=1, source_target_pairs={{0,8},{1,9},{2,10},{3,11},{4,12},{5,13},{6,14},{7,15},{8,0},{9,1},... | collective-permute-start | bytes 24584 | tf_op jit(solution)/shard_map/ppermute | solution.py:391
  (13 other events, 81.7 us)

commit v3 on v2

v3 whole, which is shorter than its diff:
```python
import functools

import jax
import jax.numpy as jnp
from jax import lax
from jax.experimental import pallas as pl
from jax.experimental.pallas import tpu as pltpu
from jax.sharding import PartitionSpec as P

SWEEPS = 5

stiff_floor = 0.01
mass_shift = 0.1
spectrum_low = 0.05
spectrum_high = 2.0
moment_decay = 0.8
step_size = 0.1
volume_pull = 0.5
volume_target = 0.4
density_floor = 0.001

SOURCE = SWEEPS
DESIGN = SWEEPS + 1
SENSE = SWEEPS + 2


def chebyshev_factors():
    centre = 0.5 * (spectrum_high + spectrum_low)
    half_width = 0.5 * (spectrum_high - spectrum_low)
    ratio_one = centre / half_width
    previous = 1.0 / ratio_one
    factors = []
    for _ in range(SWEEPS - 1):
        current = 1.0 / (2.0 * ratio_one - previous)
        factors.append((current * previous, 2.0 * current / half_width))
        previous = current
    return 1.0 / centre, factors


def shifted(plane):
    size_y, size_z = plane.shape
    return (
        pltpu.roll(plane, 1, 0),
        pltpu.roll(plane, size_y - 1, 0),
        pltpu.roll(plane, 1, 1),
        pltpu.roll(plane, size_z - 1, 1),
    )


def inner_masks(shape):
    along_y = lax.broadcasted_iota(jnp.int32, shape, 0)
    along_z = lax.broadcasted_iota(jnp.int32, shape, 1)
    return (along_y > 0, along_y < shape[0] - 1, along_z > 0, along_z < shape[1] - 1)


def beside_planes(plane, masks):
    return tuple(jnp.where(mask, moved, 0.0) for mask, moved in zip(masks, shifted(plane)))


def edge_planes(masks):
    edges = sum((1.0 - mask.astype(jnp.float32)) for mask in masks)
    return 1.0 / (8.0 - edges), 1.0 / (7.0 - edges)


def stiffness_of(design):
    return stiff_floor + (1.0 - stiff_floor) * (design * design * design)


def weight_row(q, is_free, stiff, weight, inverse, masks):
    here, below, above = stiff[q + 1], stiff[q], stiff[q + 2]
    around = (below, above) + beside_planes(here, masks)
    total = around[0]
    for plane in around[1:]:
        total = total + plane
    diagonal = (3.0 + mass_shift) * here + 0.5 * total
    scale = jnp.where(is_free, 1.0 / diagonal, 0.0)
    inverse[q] = scale
    half = 0.5 * scale
    weight[0, q] = half * (here + below)
    weight[1, q] = half * (here + above)
    for j in range(4):
        weight[2 + j, q] = jnp.where(masks[j], half * (here + around[2 + j]), 0.0)


class Kept:
    def __init__(self):
        self.places = {}

    def put(self, key, ref, index, value):
        ref[index] = value
        self.places[key] = (ref, index)

    def get(self, key):
        ref, index = self.places[key]
        return ref[index]


def sweep_row(k, q, loads, weight, resid, steps, resid_to, steps_to, shown_to, shown, first=0, first_shown=SWEEPS - 1):
    _, factors = chebyshev_factors()
    keep, gain = factors[k]
    last = k == len(factors) - 1
    faces = [weight[j, q] for j in range(6)]
    for l in range(loads):
        here = steps.get((k, l, q))
        total = faces[0] * steps.get((k, l, q - 1)) + faces[1] * steps.get((k, l, q + 1))
        for face, moved in zip(faces[2:], shifted(here)):
            total = total + face * moved
        left = resid.get((l, q)) - here + total
        step = keep * here + gain * left
        if last:
            for earlier in range(k + 1):
                step = step + steps.get((earlier, l, q))
            shown.put((l, q), shown_to, (l, q - first_shown), step)
        else:
            resid.put((l, q), resid_to, (l, q - first), left)
            steps.put((k + 1, l, q), steps_to, (k + 1, l, q - first), step)


def energy_row(i, loads, design, shown, masks):
    q = i + SOURCE
    energy = None
    for l in range(loads):
        here = shown.get((l, q))
        around = (shown.get((l, q - 1)), shown.get((l, q + 1))) + beside_planes(here, masks)
        spread = None
        for plane in around:
            gap = here - plane
            spread = gap * gap if spread is None else spread + gap * gap
        part = mass_shift * (here * here) + 0.25 * spread
        energy = part if energy is None else energy + part
    return (-3.0 * (1.0 - stiff_floor)) * (design * design) * energy


def fold(plane):
    return jnp.sum(plane.reshape(plane.shape[0] // 8, 8, plane.shape[1]), axis=0)


def filter_total(cells, sense, is_first, is_last, masks):
    inside, outer = edge_planes(masks)
    usual = 4.0 * inside + sum(beside_planes(inside, masks))
    at_end = 2.0 * outer + inside + sum(beside_planes(outer, masks))
    zero = jnp.zeros_like(inside)
    total = sense[0]
    for i in range(1, cells):
        total = total + sense[i]
    ends = jnp.where(is_first, sense[0], zero) + jnp.where(is_last, sense[cells - 1], zero)
    nexts = jnp.where(is_first, sense[1], zero) + jnp.where(is_last, sense[cells - 2], zero)
    return -fold(total * usual + ends * (at_end - usual) + nexts * (outer - inside))


def fold_rows(cells, ref):
    total = jnp.abs(ref[0])
    for i in range(1, cells):
        total = total + jnp.abs(ref[i])
    return fold(total)


def place_of():
    brick = lax.axis_index("brick")
    return lax.axis_index("load") % 2 == 0, brick == 0, brick == lax.axis_size("brick") - 1


def prepare_kernel(cells, density, passive, support, force, payload_ref, upper_ref, lower_ref,
                   design_rows, kind_rows, hold_rows, sems):
    even, _, _ = place_of()
    start = jnp.where(even, cells - DESIGN, 0)
    start_mask = jnp.where(even, cells - SOURCE, 0)
    copies = [
        pltpu.make_async_copy(source, target, sems.at[i])
        for i, (source, target) in enumerate((
            (density.at[pl.ds(start, DESIGN)], design_rows),
            (passive.at[pl.ds(start, DESIGN)], kind_rows),
            (support.at[pl.ds(start_mask, SOURCE)], hold_rows),
            (force.at[:, pl.ds(cells - SOURCE, SOURCE)], upper_ref),
            (force.at[:, pl.ds(0, SOURCE)], lower_ref),
        ))
    ]
    for copy in copies:
        copy.start()
    for copy in copies[:3]:
        copy.wait()
    for i in range(DESIGN):
        payload_ref[i] = passive_apply(design_rows[i], kind_rows[i])
    for i in range(SOURCE):
        payload_ref[DESIGN + i] = (1 - hold_rows[i]).astype(jnp.float32)
    for copy in copies[3:]:
        copy.wait()


def points_kernel(cells, loads, nodes, forces, force_ref, base_ref):
    rows = cells + 2 * SOURCE
    size_y, size_z = base_ref.shape[2:]
    zero = jnp.zeros((size_y, size_z), jnp.float32)
    for l in range(loads):
        for q in range(rows):
            own = SOURCE <= q < SOURCE + cells
            base_ref[l, q] = force_ref[l, q - SOURCE] if own else zero
    first = (lax.axis_index("brick") * cells - SOURCE) * size_y * size_z
    along_z = lax.broadcasted_iota(jnp.int32, (1, size_z), 1)
    for l in range(loads):

        def one_point(p, carry, l=l):
            cell = nodes[l, p] - first

            @pl.when((cell >= 0) & (cell < rows * size_y * size_z))
            def _():
                line, z = cell // size_z, cell % size_z
                q, y = line // size_y, line % size_y
                spot = (l, q, pl.ds(y, 1), slice(None))
                base_ref[spot] = base_ref[spot] + jnp.where(along_z == z, forces[l, p], 0.0)

            return carry

        lax.fori_loop(0, nodes.shape[1], one_point, 0)


def base_row(l, q, cells, base_in, force_lo, force_hi):
    if q < SOURCE:
        return base_in[l, q] + force_lo[l, q]
    if q >= SOURCE + cells:
        return base_in[l, q] + force_hi[l, q - SOURCE - cells]
    return base_in[l, q]


def inner_steps(cells):
    return [range(SOURCE + k, SOURCE + cells - k) for k in range(SWEEPS)]


def early_kernel(cells, loads, self_weight, density, passive, support, base_ref, pair_a, pair_b,
                 design_wide, weight, inverse, resid_ref, steps_ref, shown_ref, stiff,
                 free_wide, design_low, design_high):
    even, is_first, is_last = place_of()
    shape = density.shape[1:]
    masks = inner_masks(shape)
    rows = cells + 2 * SOURCE
    zero = jnp.zeros(shape, jnp.float32)
    for i in range(DESIGN):
        low = jnp.where(even, pair_a[i], pair_b[i])
        high = jnp.where(even, pair_b[i], pair_a[i])
        design_low[i] = low
        design_high[i] = high
        stiff[i] = jnp.where(is_first, zero, stiffness_of(low))
        stiff[DESIGN + cells + i] = jnp.where(is_last, zero, stiffness_of(high))
    for i in range(SOURCE):
        low = jnp.where(even, pair_a[DESIGN + i], pair_b[DESIGN + i])
        high = jnp.where(even, pair_b[DESIGN + i], pair_a[DESIGN + i])
        free_wide[i] = jnp.where(is_first, zero, low)
        free_wide[SOURCE + cells + i] = jnp.where(is_last, zero, high)
    for i in range(cells):
        design = passive_apply(density[i], passive[i])
        stiff[DESIGN + i] = stiffness_of(design)
        free_wide[SOURCE + i] = (1 - support[i]).astype(jnp.float32)
        design_wide[DESIGN + i] = jnp.where(support[i] == 0, design, -design)
    for r in range(DESIGN):
        free = free_wide[r - 1] > 0.5 if r > 0 else zero > 0.5
        design_wide[r] = jnp.where(free, design_low[r], -design_low[r])
        q = SOURCE + cells + r
        free = free_wide[q] > 0.5 if q < rows else zero > 0.5
        design_wide[DESIGN + cells + r] = jnp.where(free, design_high[r], -design_high[r])
    for q in range(rows):
        weight_row(q, free_wide[q] > 0.5, stiff, weight, inverse, masks)
    first_scale, _ = chebyshev_factors()
    resid, steps, shown = Kept(), Kept(), Kept()
    inner = inner_steps(cells)
    for q in inner[0]:
        for l in range(loads):
            left = inverse[q] * (base_ref[l, q] + self_weight[l] * jnp.abs(design_wide[q + 1]))
            resid.put((l, q), resid_ref, (l, q - SOURCE), left)
            steps.put((0, l, q), steps_ref, (0, l, q - SOURCE), first_scale * left)
    for k in range(SWEEPS - 1):
        for q in inner[k + 1]:
            sweep_row(
                k, q, loads, weight, resid, steps, resid_ref, steps_ref, shown_ref, shown,
                SOURCE, SOURCE + SWEEPS - 1,
            )


def first_kernel(cells, loads, self_weight, force_lo, force_hi, base_in, design_wide, weight, inverse,
                 resid_in, steps_in, shown_in, sense_ref, tile_ref, resid_ref, steps_ref, shown_ref):
    _, is_first, is_last = place_of()
    shape = design_wide.shape[1:]
    masks = inner_masks(shape)
    rows = cells + 2 * SOURCE
    first_scale, _ = chebyshev_factors()
    resid, steps, shown = Kept(), Kept(), Kept()
    inner = inner_steps(cells)
    for l in range(loads):
        for k in range(SWEEPS - 1):
            for q in inner[k]:
                steps.places[(k, l, q)] = (steps_in, (k, l, q - SOURCE))
        for q in inner[0]:
            resid.places[(l, q)] = (resid_in, (l, q - SOURCE))
        for q in inner[SWEEPS - 1]:
            shown.places[(l, q)] = (shown_in, (l, q - SOURCE - (SWEEPS - 1)))
    for l in range(loads):
        for q in range(rows):
            if q in inner[0]:
                continue
            base = base_row(l, q, cells, base_in, force_lo, force_hi)
            left = inverse[q] * (base + self_weight[l] * jnp.abs(design_wide[q + 1]))
            resid.put((l, q), resid_ref, (l, q), left)
            steps.put((0, l, q), steps_ref, (0, l, q), first_scale * left)
    for k in range(SWEEPS - 1):
        for q in range(k + 1, rows - k - 1):
            if q not in inner[k + 1]:
                sweep_row(k, q, loads, weight, resid, steps, resid_ref, steps_ref, shown_ref, shown)
    for i in range(cells):
        sense_ref[i] = energy_row(i, loads, design_wide[DESIGN + i], shown, masks)
    own = design_wide.at[pl.ds(DESIGN, cells)]
    spread_totals(tile_ref, filter_total(cells, sense_ref, is_first, is_last, masks), fold_rows(cells, own))


def moment_kernel(cells, sense, pair_a, pair_b, moment_ref, sense_wide):
    even, is_first, is_last = place_of()
    shape = sense.shape[1:]
    masks = inner_masks(shape)
    zero = jnp.zeros(shape, jnp.float32)
    for i in range(SENSE):
        low = jnp.where(even, pair_a[i], pair_b[i])
        high = jnp.where(even, pair_b[i], pair_a[i])
        sense_wide[i] = jnp.where(is_first, zero, low)
        sense_wide[SENSE + cells + i] = jnp.where(is_last, zero, high)
    for i in range(cells):
        sense_wide[SENSE + i] = sense[i]
    inside, outer = edge_planes(masks)
    for r in range(cells + 2 * DESIGN):
        at_end = (is_first & (r == DESIGN)) | (is_last & (r == DESIGN + cells - 1))
        moment_ref[r] = filtered_row(r, sense_wide, masks) * jnp.where(at_end, outer, inside)


def filtered_row(r, sense_wide, masks):
    here = sense_wide[r + 1]
    total = 2.0 * here + sense_wide[r] + sense_wide[r + 2]
    for plane in beside_planes(here, masks):
        total = total + plane
    return total


def spread_totals(tile_ref, abs_tile, density_tile):
    count, width = tile_ref.shape
    row = jnp.concatenate([jnp.sum(tile, axis=0, keepdims=True) for tile in (abs_tile, density_tile)], axis=1)
    tile_ref[...] = jnp.broadcast_to(row, (count, width))


def rate_and_pull(totals, total_cells, share):
    half = totals.shape[1] // 2
    abs_total = jnp.sum(totals[:, :half], keepdims=True)
    density_total = jnp.sum(totals[:, half:], keepdims=True) * share
    mean_step = abs_total / total_cells + 1e-6
    return step_size / mean_step, volume_pull * (density_total / total_cells - volume_target)


def second_kernel(cells, loads, total_cells, share, self_weight, tile_in, moment_wide,
                  design_wide, base_far, lo_far, hi_far,
                  shown_ref, design_out, sense_ref, tile_ref,
                  stiff, weight, inverse, resid_ref, steps_ref, shown_to, design_new,
                  base_in, force_lo, force_hi, sems):
    copies = [
        pltpu.make_async_copy(source, target, sems.at[i])
        for i, (source, target) in enumerate(
            ((base_far, base_in), (lo_far, force_lo), (hi_far, force_hi)))
    ]
    for copy in copies:
        copy.start()
    _, is_first, is_last = place_of()
    shape = moment_wide.shape[1:]
    masks = inner_masks(shape)
    wide = cells + 2 * DESIGN
    rows = cells + 2 * SOURCE
    zero = jnp.zeros(shape, jnp.float32)
    rate, pull = rate_and_pull(tile_in[...], total_cells, share)
    for r in range(wide):
        signed = design_wide[r]
        before = jnp.abs(signed)
        moved = jnp.clip(before - rate * moment_wide[r] - pull, density_floor, 1.0)
        fixed = (before == density_floor) | (before == 1.0)
        design = jnp.where(fixed, before, moved)
        design_new[r] = design
        stiffness = stiffness_of(design)
        if r < DESIGN:
            stiff[r] = jnp.where(is_first, zero, stiffness)
        elif r >= DESIGN + cells:
            stiff[r] = jnp.where(is_last, zero, stiffness)
        else:
            stiff[r] = stiffness
    own_rows = pltpu.make_async_copy(design_new.at[pl.ds(DESIGN, cells)], design_out, sems.at[len(copies) + loads])
    own_rows.start()
    resid, steps, shown = Kept(), Kept(), Kept()
    first_scale, _ = chebyshev_factors()
    for q in range(rows):
        weight_row(q, design_wide[q + 1] > 0.0, stiff, weight, inverse, masks)
    for copy in copies:
        copy.wait()
    for q in range(rows):
        scale, design = inverse[q], design_new[q + 1]
        for l in range(loads):
            left = scale * (base_row(l, q, cells, base_in, force_lo, force_hi) + self_weight[l] * design)
            resid.put((l, q), resid_ref, (l, q), left)
            steps.put((0, l, q), steps_ref, (0, l, q), first_scale * left)
    for k in range(SWEEPS - 1):
        for q in range(k + 1, rows - k - 1):
            sweep_row(k, q, loads, weight, resid, steps, resid_ref, steps_ref, shown_to, shown)
    results = [
        pltpu.make_async_copy(shown_to.at[l, pl.ds(1, cells)], shown_ref.at[l], sems.at[len(copies) + l])
        for l in range(loads)
    ]
    for copy in results:
        copy.start()
    for i in range(cells):
        sense_ref[i] = energy_row(i, loads, design_new[DESIGN + i], shown, masks)
    own = design_new.at[pl.ds(DESIGN, cells)]
    spread_totals(tile_ref, filter_total(cells, sense_ref, is_first, is_last, masks), fold_rows(cells, own))
    for copy in results + [own_rows]:
        copy.wait()


def last_moment_kernel(cells, slab, sense, pair_a, pair_b, moment_wide, design_far, passive_far,
                       momentum_ref, kept_ref, before_ref, least_ref, most_ref, sense_wide, momentum_all,
                       kinds, sems):
    even, is_first, is_last = place_of()
    window = pl.ds(pl.multiple_of(lax.axis_index("load") * slab, 8), slab)
    copies = [
        pltpu.make_async_copy(design_far.at[:, window, :], before_ref, sems.at[1]),
        pltpu.make_async_copy(passive_far.at[:, window, :], kinds, sems.at[2]),
    ]
    for copy in copies:
        copy.start()
    shape = sense.shape[1:]
    masks = inner_masks(shape)
    zero = jnp.zeros(shape, jnp.float32)
    sense_wide[0] = jnp.where(is_first, zero, jnp.where(even, pair_a[0], pair_b[0]))
    sense_wide[cells + 1] = jnp.where(is_last, zero, jnp.where(even, pair_b[0], pair_a[0]))
    for i in range(cells):
        sense_wide[i + 1] = sense[i]
    inside, outer = edge_planes(masks)
    for i in range(cells):
        scale = inside
        if i == 0:
            scale = jnp.where(is_first, outer, inside)
        elif i == cells - 1:
            scale = jnp.where(is_last, outer, inside)
        momentum_all[i] = moment_decay * moment_wide[DESIGN + i] + filtered_row(i, sense_wide, masks) * scale
        momentum = momentum_all[i, window, :]
        kept_ref[i] = momentum
    copy = pltpu.make_async_copy(kept_ref, momentum_ref, sems.at[0])
    copy.start()
    for other in copies:
        other.wait()
    for i in range(cells):
        kind = kinds[i]
        least_ref[i] = jnp.where(kind == 2, 1.0, density_floor)
        most_ref[i] = jnp.where(kind == 1, density_floor, 1.0)
    copy.wait()


def last_kernel(cells, total_cells, share, tile_before, tile_in, momentum_ref, before_ref, least_ref, most_ref,
                design_ref, design_near, sems):
    half = tile_in.shape[1] // 2
    along = lax.broadcasted_iota(jnp.int32, tile_in.shape, 1)
    totals = tile_in[...] + jnp.where(along < half, moment_decay * tile_before[...], 0.0)
    rate, pull = rate_and_pull(totals, total_cells, share)
    for i in range(cells):
        moved = before_ref[i] - rate * momentum_ref[i] - pull
        design_near[i] = jnp.minimum(jnp.maximum(moved, least_ref[i]), most_ref[i])
    copy = pltpu.make_async_copy(design_near, design_ref, sems.at[0])
    copy.start()
    copy.wait()


VMEM = pl.BlockSpec(memory_space=pltpu.VMEM)
SMEM = pl.BlockSpec(memory_space=pltpu.SMEM)


def on_core(kernel, operands, scalars, outs, scratch, cost=0, limit=4, far=0, far_outs=0, keep=False):
    anywhere = pl.BlockSpec(memory_space=pl.ANY)
    operands = [
        pltpu.with_memory_space_constraint(operand, pltpu.VMEM)
        if scalars <= i and (i < len(operands) - far or keep) else pltpu.with_memory_space_constraint(operand, pltpu.HBM) if i >= len(operands) - far else operand
        for i, operand in enumerate(operands)
    ]
    return pl.pallas_call(
        kernel,
        out_shape=[
            jax.ShapeDtypeStruct(shape, jnp.float32) if i < far_outs else pltpu.VMEM(shape, jnp.float32)
            for i, shape in enumerate(outs)
        ],
        in_specs=[SMEM] * scalars + [VMEM] * (len(operands) - scalars - far) + [anywhere] * far,
        out_specs=[anywhere] * far_outs + [VMEM] * (len(outs) - far_outs),
        scratch_shapes=[pltpu.VMEM(item, jnp.float32) if isinstance(item, tuple) else item for item in scratch],
        cost_estimate=pl.CostEstimate(flops=cost, bytes_accessed=cost, transcendentals=0) if cost else None,
        compiler_params=pltpu.CompilerParams(vmem_limit_bytes=limit * 1024 * 1024),
    )(*operands)


def passive_apply(design, passive):
    return jnp.where(passive == 1, density_floor, jnp.where(passive == 2, 1.0, design))


def swap(value, axis, bit):
    count = lax.axis_size(axis)
    return lax.ppermute(value, axis, [(i, i ^ bit) for i in range(count)])


def swap_parts(value, count, bit=1):
    return jnp.concatenate([swap(value[i:i + count], "load", bit) for i in range(0, value.shape[0], count)])


def along(value, step):
    count = lax.axis_size("brick")
    pairs = [(i, i + step) for i in range(count) if 0 <= i + step < count]
    return lax.ppermute(value, "brick", pairs)


def both_ways(value):
    count, loads = lax.axis_size("brick"), lax.axis_size("load")
    pairs = []
    for l in range(loads):
        step = 1 if l % 2 == 0 else -1
        pairs += [(l * count + i, l * count + i + step) for i in range(count) if 0 <= i + step < count]
    return lax.ppermute(value, ("load", "brick"), pairs)


def bits_of(count):
    return [1 << k for k in range(count.bit_length() - 1)]


def sum_over(value, axis):
    for bit in bits_of(lax.axis_size(axis)):
        value = value + swap(value, axis, bit)
    return value


def load_terms(value):
    bits = bits_of(lax.axis_size("load"))
    for bit in bits[:-1]:
        value = value + swap(value, "load", bit)
    return value, swap_parts(value, 6, bits[-1])


def after(value, other):
    return lax.optimization_barrier((value, other))[0]


def meet(sense, tiles, width, even, filtered):
    cells = sense.shape[0]
    sense_a, sense_b = load_terms(sense)
    sense = sense_a + sense_b
    edge = lax.dynamic_slice_in_dim(sense, jnp.where(even, cells - width, 0), width, 0)
    pair_a = both_ways(edge)
    tiles = lax.all_to_all(after(tiles, edge), ("load", "brick"), 0, 0, tiled=True)
    pair_b = swap(after(pair_a, tiles), "load", 1)
    return filtered(sense, pair_a, pair_b), tiles


def body(density, passive, support, load_nodes, load_force, self_weight, body_force):
    cells, size_y, size_z = density.shape
    loads = body_force.shape[0]
    load_count, bricks = lax.axis_size("load"), lax.axis_size("brick")
    slab = size_y // load_count
    total_cells = float(cells * bricks * size_y * size_z)
    share = 1.0 / load_count
    even = lax.axis_index("load") % 2 == 0
    plane = (size_y, size_z)
    wide, rows = cells + 2 * DESIGN, cells + 2 * SOURCE
    tile = (load_count * bricks, 2 * size_z)
    shown_shape = (loads, cells + 2) + plane
    resid_shape = (loads, rows) + plane
    steps_shape = (SWEEPS - 1, loads, rows) + plane

    payload, upper, lower = on_core(
        functools.partial(prepare_kernel, cells),
        (density, passive, support, body_force),
        0,
        [(DESIGN + SOURCE,) + plane, (loads, SOURCE) + plane, (loads, SOURCE) + plane],
        [pltpu.VMEM((DESIGN,) + plane, jnp.float32), pltpu.VMEM((DESIGN,) + plane, jnp.int32),
         pltpu.VMEM((SOURCE,) + plane, jnp.int32), pltpu.SemaphoreType.DMA((5,))],
        far=4,
    )
    pair_a = both_ways(payload)
    force_lo = along(upper, 1)
    force_hi = along(lower, -1)
    (base,) = on_core(
        functools.partial(points_kernel, cells, loads),
        (load_nodes, load_force, after(body_force, (upper, lower))),
        2,
        [resid_shape],
        [],
        cost=1,
    )
    pair_b = swap_parts(after(pair_a, base), 3)
    design_wide, weight, inverse, resid, steps, shown = on_core(
        functools.partial(early_kernel, cells, loads),
        (self_weight, density, passive, support, base, pair_a, pair_b),
        1,
        [(wide,) + plane, (6, rows) + plane, (rows,) + plane,
         (loads, cells) + plane, (SWEEPS - 1, loads, cells) + plane, (loads, cells - 2 * (SWEEPS - 1)) + plane],
        [(wide,) + plane, (rows,) + plane, (DESIGN,) + plane, (DESIGN,) + plane],
        cost=1,
    )
    sense, tiles = on_core(
        functools.partial(first_kernel, cells, loads),
        (self_weight, force_lo, force_hi, base, design_wide, weight, inverse, resid, steps, shown),
        1,
        [(cells,) + plane, tile],
        [resid_shape, steps_shape, shown_shape],
    )
    (moment_wide,), tiles_first = meet(
        sense, tiles, SENSE, even,
        lambda *sensed: on_core(
            functools.partial(moment_kernel, cells),
            sensed,
            0,
            [(wide,) + plane],
            [(cells + 2 * SENSE,) + plane],
        ),
    )
    shown, design, sense, tiles = on_core(
        functools.partial(second_kernel, cells, loads, total_cells, share),
        (self_weight, tiles_first, moment_wide, design_wide, base, force_lo, force_hi),
        1,
        [(loads, cells) + plane, (cells,) + plane, (cells,) + plane, tile],
        [(wide,) + plane, (6, rows) + plane, (rows,) + plane, resid_shape, steps_shape, shown_shape, (wide,) + plane,
         resid_shape, (loads, SOURCE) + plane, (loads, SOURCE) + plane,
         pltpu.SemaphoreType.DMA((4 + loads,))],
        limit=14,
        far=3,
        far_outs=2,
        keep=True,
    )
    last_ones, tiles_last = meet(
        sense, tiles, 1, even,
        lambda *sensed: on_core(
            functools.partial(last_moment_kernel, cells, slab),
            sensed + (moment_wide, design, passive),
            0,
            [(cells, slab, size_z)] * 5,
            [(cells + 2,) + plane, (cells,) + plane,
             pltpu.VMEM((cells, slab, size_z), jnp.int32), pltpu.SemaphoreType.DMA((3,))],
            far=2,
            far_outs=1,
        ),
    )
    (design,) = on_core(
        functools.partial(last_kernel, cells, total_cells, share),
        (tiles_first, tiles_last) + tuple(last_ones[1:]),
        0,
        [(cells, slab, size_z)],
        [(cells, slab, size_z), pltpu.SemaphoreType.DMA((1,))],
        far_outs=1,
    )
    return design, last_ones[0], shown


def solution(mesh):
    placed = (
        P("brick", None, None),
        P("brick", None, None),
        P("brick", None, None),
        P("load", None),
        P("load", None),
        P("load"),
        P("load", "brick", None, None),
    )
    return jax.shard_map(
        body,
        mesh=mesh,
        in_specs=placed,
        out_specs=(
            P("brick", "load", None),
            P("brick", "load", None),
            P("load", "brick", None, None),
        ),
        check_vma=False,
    )
```

time: 99.3 us -> 80 us (0.81)
  waiting for transfers between devices: 37.5 us -> 19.4 us
  blocking collectives: 0 us -> 10.3 us
  starting transfers between devices: 31.4 us -> 22 us
  local copies, waits for them, and re-layouts: 7.06 us -> 4.07 us
    ppermute x15 -> x10, waiting for transfers between devices: 21.1 us -> 6.95 us  [swap(): return lax.ppermute(value, axis, [(i, i ^ bit) for i in range(count)])]
    ppermute x15 -> x10, starting transfers between devices: 13.7 us -> 1.96 us  [swap(): return lax.ppermute(value, axis, [(i, i ^ bit) for i in range(count)])]
    all_to_all x0 -> x1, blocking collectives: none -> 10.3 us  [meet(): lax.all_to_all(after(tiles, edge), ('load', 'brick'), 0, 0, tiled=True)]
    ppermute x2, waiting for transfers between devices: 7.6 us -> 0.01 us  [along(): return lax.ppermute(value, 'brick', pairs)]
    all_to_all x0 -> x1, waiting for transfers between devices: none -> 3.66 us  [meet(): lax.all_to_all(after(tiles, edge), ('load', 'brick'), 0, 0, tiled=True)]
    unnamed x34 -> x26, local copies, waits for them, and re-layouts: 6.13 us -> 3.26 us
    all_to_all x0 -> x1, starting transfers between devices: none -> 2.57 us  [meet(): lax.all_to_all(after(tiles, edge), ('load', 'brick'), 0, 0, tiled=True)]
    select_n x2 -> x0, other arithmetic: 1.28 us -> none  [the longest x1 1.23 us: body(): jnp.where(passive == 1, density_floor, jnp.where(passive == 2, 1.0, densi...]
  transfers between devices with their start and end apart: 20 -> 16, of which waited for: 12 -> 12; matrix products, arithmetic and copies ran while one was open for 1% -> 0% of each run, Pallas kernels for 6% -> 8%
where the time goes in v3:
time: 80 us; the launch traced here: 79.5 us
  starting transfers between devices  22 us (28%)
  Pallas kernels  21.6 us (27%)
  waiting for transfers between devices  19.4 us (24%)
  blocking collectives  10.3 us (13%)
  local copies, waits for them, and re-layouts  4.07 us (5%)
  between operations  1.11 us (1%)
  other arithmetic  1.04 us (1%)
    pallas_call x8, Pallas kernels, on_core(): pl.pallas_call(kernel, out_shape=[jax.ShapeDtypeStruct(shape, jnp.float32...  21.6 us
    ppermute x3, starting transfers between devices, both_ways(): return lax.ppermute(value, ('load', 'brick'), pairs)  12.8 us
    all_to_all x1, blocking collectives, meet(): lax.all_to_all(after(tiles, edge), ('load', 'brick'), 0, 0, tiled=True)  10.3 us
    ppermute x3, waiting for transfers between devices, both_ways(): return lax.ppermute(value, ('load', 'brick'), pairs)  8.82 us
    ppermute x10, waiting for transfers between devices, swap(): return lax.ppermute(value, axis, [(i, i ^ bit) for i in range(count)])  6.95 us
    ppermute x2, starting transfers between devices, along(): return lax.ppermute(value, 'brick', pairs)  4.69 us
    all_to_all x1, waiting for transfers between devices, meet(): lax.all_to_all(after(tiles, edge), ('load', 'brick'), 0, 0, tiled=True)  3.66 us
    unnamed x26, local copies, waits for them, and re-layouts  3.26 us
  transfers between devices with their start and end apart: 16, of which 12 were waited for; matrix products, arithmetic and copies ran while one was open for 0% of the time, Pallas kernels for 8%

profile of v3, /device:TPU:0, one launch (start us, length us, event | category | flops | bytes accessed | tf_op | source)
XLA Modules:
  0.0 79.5 jit_solution(18325679225728574589)
XLA Ops:
  0.7 1.5 %shard_map.94 = (f32[11,64,128]{2,1,0:T(8,128)S(1)}, f32[2,5,64,128]{3,2,1,0:T(8,128)S(1)}, f32[2,5,64,128]{3,2,1,0:T(8,128)S(1)}) custom-call(f32[12,64,128]{2,1,0:T(8,128)} %density.3, s32[12,64,128]{2,1,0:T(8,128)} %passive_far.1, s32[12,64,128]{2,1,0:T(8,128)} %support.3, f32[2,12,64,128]{3,2,1,0:T(8,128)} %force_ref), custom_call_target="tpu_custom_call" | custom-call | tf_op jit(solution)/shard_map/pallas_call | solution.py:481
  2.2 4.9 %collective-permute-start.2 = (f32[11,64,128]{2,1,0:T(8,128)S(1)}, f32[11,64,128]{2,1,0:T(8,128)S(1)}, u32[]{:S(2)}, u32[]{:S(2)}) collective-permute-start(f32[11,64,128]{2,1,0:T(8,128)S(1)} %get-tuple-element.32), channel_id=1, source_target_pairs={{0,1},{1,2},{2,3},{3,4},{4,5},{5,6},{6,7},{7,8},{8,9},{9,10},{10,1... | collective-permute-start | bytes 1081352 | tf_op jit(solution)/shard_map/ppermute | solution.py:520
  7.0 3.4 %collective-permute-start = (f32[2,5,64,128]{3,2,1,0:T(8,128)S(1)}, f32[2,5,64,128]{3,2,1,0:T(8,128)S(1)}, u32[]{:S(2)}, u32[]{:S(2)}) collective-permute-start(f32[2,5,64,128]{3,2,1,0:T(8,128)S(1)} %get-tuple-element.29), channel_id=1, source_target_pairs={{0,1},{1,2},{2,3},{3,4},{4,5},{5,6},{6,7},{7,8},{8,9},{9,10},{10,1... | collective-permute-start | bytes 983048 | tf_op jit(solution)/shard_map/ppermute | solution.py:511
  10.4 1.3 %collective-permute-start.1 = (f32[2,5,64,128]{3,2,1,0:T(8,128)S(1)}, f32[2,5,64,128]{3,2,1,0:T(8,128)S(1)}, u32[]{:S(2)}, u32[]{:S(2)}) collective-permute-start(f32[2,5,64,128]{3,2,1,0:T(8,128)S(1)} %get-tuple-element.30), channel_id=1, source_target_pairs={{1,0},{2,1},{3,2},{4,3},{5,4},{6,5},{7,6},{8,7},{9,8},{10,9},{11,1... | collective-permute-start | bytes 983048 | tf_op jit(solution)/shard_map/ppermute | solution.py:511
  11.8 1.1 %copy-done.1 = f32[2,12,64,128]{3,2,1,0:T(8,128)S(1)} copy-done((f32[2,12,64,128]{3,2,1,0:T(8,128)S(1)}, f32[2,12,64,128]{3,2,1,0:T(8,128)}, u32[]{:S(2)}) %copy-start.1) | copy-done | bytes 786456
  13.6 0.7 copy-done.11
  14.2 2.9 %shard_map.95.base_ref.base_in.base_far = f32[2,22,64,128]{3,2,1,0:T(8,128)S(1)} custom-call(s32[2,64]{1,0:T(2,128)S(1)} %copy-done.10, f32[2,64]{1,0:T(2,128)S(1)} %copy-done.11, f32[2,12,64,128]{3,2,1,0:T(8,128)S(1)} %copy-done.1), custom_call_target="tpu_custom_call" | custom-call | flops 1 | bytes 1 | tf_op jit(solution)/shard_map/pallas_call | solution.py:481
  17.1 8.8 %collective-permute-done.2.pair_a = f32[11,64,128]{2,1,0:T(8,128)S(1)} collective-permute-done((f32[11,64,128]{2,1,0:T(8,128)S(1)}, f32[11,64,128]{2,1,0:T(8,128)S(1)}, u32[]{:S(2)}, u32[]{:S(2)}) %collective-permute-start.2) | collective-permute-done | bytes 360480 | tf_op jit(solution)/shard_map/ppermute | solution.py:520
  28.6 3.4 %shard_map.96 = (f32[24,64,128]{2,1,0:T(8,128)S(1)}, f32[6,22,64,128]{3,2,1,0:T(8,128)S(1)}, f32[22,64,128]{2,1,0:T(8,128)S(1)}, f32[2,12,64,128]{3,2,1,0:T(8,12...) custom-call(f32[2]{0:T(128)S(1)} %copy-done.9, f32[12,64,128]{2,1,0:T(8,128)S(1)} %copy-done.2, ...), custom_call_target="tpu_custom_call" | custom-call | flops 1 | bytes 1 | tf_op jit(solution)/shard_map/pallas_call | solution.py:481
  32.0 3.9 %shard_map.97 = (f32[12,64,128]{2,1,0:T(8,128)S(1)}, f32[32,256]{1,0:T(8,128)S(1)}) custom-call(f32[2]{0:T(128)S(1)} %copy-done.9, f32[2,5,64,128]{3,2,1,0:T(8,128)S(1)} %collective-permute-done.force_lo.lo_far, f32[2,5,64,128]{3,2,1,0:T(8,128)S(1)} %collective-permute-done.1.force_hi.hi_far, f32[2,22,64,128]{3,2,1,0:T(8,128)S(1)} %shard_map.95.base_ref.base_in.base_far, ...), custom_call_target="tpu_custom_call" | custom-call | tf_op jit(solution)/shard_map/pallas_call | solution.py:481
  36.5 0.9 %collective-permute-done.7 = f32[6,64,128]{2,1,0:T(8,128)S(1)} collective-permute-done((f32[6,64,128]{2,1,0:T(8,128)S(1)}, f32[6,64,128]{2,1,0:T(8,128)S(1)}, u32[]{:S(2)}, u32[]{:S(2)}) %collective-permute-start.7) | collective-permute-done | bytes 196640 | tf_op jit(solution)/shard_map/ppermute | solution.py:501
  37.9 1.0 %maximum_add_fusion.sense = f32[12,64,128]{2,1,0:T(8,128)S(1)} fusion(f32[12,64,128]{2,1,0:T(8,128)S(1)} %get-tuple-element.41, f32[6,64,128]{2,1,0:T(8,128)} %collective-permute-done.8, f32[6,64,128]{2,1,0:T(8,128)S(1)} %collective-permute-done.7), kind=kLoop, calls=%fused_computation | loop fusion | flops 196608 | bytes 1179648 | tf_op jit(solution)/shard_map/add | solution.py:547
  38.9 4.4 %collective-permute-start.9 = (f32[7,64,128]{2,1,0:T(8,128)S(1)}, f32[7,64,128]{2,1,0:T(8,128)S(1)}, u32[]{:S(2)}, u32[]{:S(2)}) collective-permute-start(f32[7,64,128]{2,1,0:T(8,128)S(1)} %constant_dynamic-slice_fusion.1), channel_id=1, source_target_pairs={{0,1},{1,2},{2,3},{3,4},{4,5},{5,6},{6,7},{7,8},{8,9},{9,10},{10,1... | collective-permute-start | bytes 688136 | tf_op jit(solution)/shard_map/ppermute | solution.py:520
  43.3 10.3 %all_to_all.22 = f32[32,1,256]{2,1,0:T(1,128)S(1)} all-to-all(f32[32,1,256]{2,1,0:T(1,128)S(1)} %copy.10), channel_id=1, replica_groups=mesh['load'=2,'brick'=16] {'load','brick'}, dimensions={0} | all-to-all | bytes 65536 | tf_op jit(solution)/shard_map/all_to_all | solution.py:550
  53.6 1.5 %collective-permute-done.10.pair_b = f32[7,64,128]{2,1,0:T(8,128)S(1)} collective-permute-done((f32[7,64,128]{2,1,0:T(8,128)S(1)}, f32[7,64,128]{2,1,0:T(8,128)S(1)}, u32[]{:S(2)}, u32[]{:S(2)}) %collective-permute-start.10) | collective-permute-done | bytes 229408 | tf_op jit(solution)/shard_map/ppermute | solution.py:501
  55.6 7.3 %shard_map.99 = (f32[2,12,64,128]{3,2,1,0:T(8,128)}, f32[12,64,128]{2,1,0:T(8,128)S(1)}, f32[12,64,128]{2,1,0:T(8,128)S(1)}, f32[32,256]{1,0:T(8,128)S(1)}) custom-call(f32[2]{0:T(128)S(1)} %copy-done.9, f32[32,256]{1,0:T(8,128)S(1)} %bitcast.8, f32[24,64,128]{2,1,0:T(8,128)S(1)} %shard_map.98.moment_wide, f32[24,64,128]{2,1,0:T(8,128)S(1)} %get-tuple-element.34.design_wide, ...), custom_call_target="tpu_custom_call" | custom-call | tf_op jit(solution)/shard_map/pallas_call | solution.py:481
  62.9 0.7 copy-done.8
  64.2 0.9 %collective-permute-done.11 = f32[6,64,128]{2,1,0:T(8,128)S(1)} collective-permute-done((f32[6,64,128]{2,1,0:T(8,128)S(1)}, f32[6,64,128]{2,1,0:T(8,128)S(1)}, u32[]{:S(2)}, u32[]{:S(2)}) %collective-permute-start.11) | collective-permute-done | bytes 196640 | tf_op jit(solution)/shard_map/ppermute | solution.py:501
  66.2 2.6 %all-to-all-start.1 = ((f32[32,1,256]{2,1,0:T(1,128)}), f32[32,1,256]{2,1,0:T(1,128)S(1)}, u32[]{:S(2)}, u32[]{:S(2)}) async-start(f32[32,1,256]{2,1,0:T(1,128)} %copy.11), calls=%async_computation.1 | async-start | bytes 65536 | tf_op jit(solution)/shard_map/all_to_all | solution.py:550
  68.7 3.5 %collective-permute-start.13 = (f32[1,64,128]{2,1,0:T(8,128)S(1)}, f32[1,64,128]{2,1,0:T(8,128)S(1)}, u32[]{:S(2)}, u32[]{:S(2)}) collective-permute-start(f32[1,64,128]{2,1,0:T(8,128)S(1)} %constant_dynamic-slice_fusion), channel_id=1, source_target_pairs={{0,1},{1,2},{2,3},{3,4},{4,5},{5,6},{6,7},{7,8},{8,9},{9,10},{10,1... | collective-permute-start | bytes 98312 | tf_op jit(solution)/shard_map/ppermute | solution.py:520
  72.3 3.7 %all-to-all-done.1 = f32[32,1,256]{2,1,0:T(1,128)S(1)} async-done(((f32[32,1,256]{2,1,0:T(1,128)}), f32[32,1,256]{2,1,0:T(1,128)S(1)}, u32[]{:S(2)}, u32[]{:S(2)}) %all-to-all-start.1) | async-done | bytes 32800 | tf_op jit(solution)/shard_map/all_to_all | solution.py:550
  76.0 1.2 %collective-permute-done.14.pair_b = f32[1,64,128]{2,1,0:T(8,128)S(1)} collective-permute-done((f32[1,64,128]{2,1,0:T(8,128)S(1)}, f32[1,64,128]{2,1,0:T(8,128)S(1)}, u32[]{:S(2)}, u32[]{:S(2)}) %collective-permute-start.14) | collective-permute-done | bytes 32800 | tf_op jit(solution)/shard_map/ppermute | solution.py:501
  77.2 1.4 %shard_map.100 = (f32[12,32,128]{2,1,0:T(8,128)}, f32[12,32,128]{2,1,0:T(8,128)S(1)}, f32[12,32,128]{2,1,0:T(8,128)S(1)}, f32[12,32,128]{2,1,0:T(8,128)S(1)}, f32[12,32,128]{2,1,0:T(8,128)S(1)}) custom-call(f32[12,64,128]{2,1,0:T(8,128)S(1)} %maximum_add_fusion.1.sense, f32[1,64,128]{2,1,0:T(8,128)S(1)} %collective-permute-done.13.pair_a, ...), custom_call_target="tpu_custom_call" | custom-call | tf_op jit(solution)/shard_map/pallas_call | solution.py:481
  78.5 0.9 %shard_map.101 = f32[12,32,128]{2,1,0:T(8,128)} custom-call(f32[32,256]{1,0:T(8,128)S(1)} %bitcast.9, f32[32,256]{1,0:T(8,128)S(1)} %bitcast.10, f32[12,32,128]{2,1,0:T(8,128)S(1)} %get-tuple-element.49.momentum_ref, f32[12,32,128]{2,1,0:T(8,128)S(1)} %get-tuple-element.50.before_ref, f32[12,32,128]{2,1,0:T(8,128)S(1)} %get-tuple-element.51.least_ref, ...), custom_call_target="tpu_custom_call" | custom-call | tf_op jit(solution)/shard_map/pallas_call | solution.py:481
  (54 shorter events, 6.5 us)
Async XLA Ops:
  0.6 27.9 %copy-start.2 = (f32[12,64,128]{2,1,0:T(8,128)S(1)}, f32[12,64,128]{2,1,0:T(8,128)}, u32[]{:S(2)}) copy-start(f32[12,64,128]{2,1,0:T(8,128)} %density.3) | copy-start | bytes 1179652
  0.6 27.9 %copy-start = (s32[12,64,128]{2,1,0:T(8,128)S(1)}, s32[12,64,128]{2,1,0:T(8,128)}, u32[]{:S(2)}) copy-start(s32[12,64,128]{2,1,0:T(8,128)} %passive_far.1) | copy-start | bytes 1179652
  0.7 27.9 %copy-start.3 = (s32[12,64,128]{2,1,0:T(8,128)S(1)}, s32[12,64,128]{2,1,0:T(8,128)}, u32[]{:S(2)}) copy-start(s32[12,64,128]{2,1,0:T(8,128)} %support.3) | copy-start | bytes 1179652
  0.7 27.9 %copy-start.9 = (f32[2]{0:T(128)S(1)}, f32[2]{0:T(128)}, u32[]{:S(2)}) copy-start(f32[2]{0:T(128)} %self_weight.5) | copy-start | bytes 28
  2.2 23.8 %collective-permute-start.2 = (f32[11,64,128]{2,1,0:T(8,128)S(1)}, f32[11,64,128]{2,1,0:T(8,128)S(1)}, u32[]{:S(2)}, u32[]{:S(2)}) collective-permute-start(f32[11,64,128]{2,1,0:T(8,128)S(1)} %get-tuple-element.32), channel_id=1, source_target_pairs={{0,1},{1,2},{2,3},{3,4},{4,5},{5,6},{6,7},{7,8},{8,9},{9,10},{10,1... | collective-permute-start | bytes 1081352 | tf_op jit(solution)/shard_map/ppermute | solution.py:520
  7.0 24.9 %collective-permute-start = (f32[2,5,64,128]{3,2,1,0:T(8,128)S(1)}, f32[2,5,64,128]{3,2,1,0:T(8,128)S(1)}, u32[]{:S(2)}, u32[]{:S(2)}) collective-permute-start(f32[2,5,64,128]{3,2,1,0:T(8,128)S(1)} %get-tuple-element.29), channel_id=1, source_target_pairs={{0,1},{1,2},{2,3},{3,4},{4,5},{5,6},{6,7},{7,8},{8,9},{9,10},{10,1... | collective-permute-start | bytes 983048 | tf_op jit(solution)/shard_map/ppermute | solution.py:511
  10.4 21.5 %collective-permute-start.1 = (f32[2,5,64,128]{3,2,1,0:T(8,128)S(1)}, f32[2,5,64,128]{3,2,1,0:T(8,128)S(1)}, u32[]{:S(2)}, u32[]{:S(2)}) collective-permute-start(f32[2,5,64,128]{3,2,1,0:T(8,128)S(1)} %get-tuple-element.30), channel_id=1, source_target_pairs={{1,0},{2,1},{3,2},{4,3},{5,4},{6,5},{7,6},{8,7},{9,8},{10,9},{11,1... | collective-permute-start | bytes 983048 | tf_op jit(solution)/shard_map/ppermute | solution.py:511
  25.9 1.3 %collective-permute-start.6 = (f32[2,64,128]{2,1,0:T(8,128)S(1)}, f32[2,64,128]{2,1,0:T(8,128)S(1)}, u32[]{:S(2)}, u32[]{:S(2)}) collective-permute-start(f32[2,64,128]{2,1,0:T(8,128)S(1)} %slice.27), channel_id=1, source_target_pairs={{0,16},{16,0},{1,17},{17,1},{2,18},{18,2},{3,19},{19,3},{4,20},{20... | collective-permute-start | bytes 196616 | tf_op jit(solution)/shard_map/ppermute | solution.py:501
  26.0 1.5 %collective-permute-start.3 = (f32[3,64,128]{2,1,0:T(8,128)S(1)}, f32[3,64,128]{2,1,0:T(8,128)S(1)}, u32[]{:S(2)}, u32[]{:S(2)}) collective-permute-start(f32[3,64,128]{2,1,0:T(8,128)S(1)} %get-tuple-element.59), channel_id=1, source_target_pairs={{0,16},{16,0},{1,17},{17,1},{2,18},{18,2},{3,19},{19,3},{4,20},{20... | collective-permute-start | bytes 294920 | tf_op jit(solution)/shard_map/ppermute | solution.py:501
  26.5 1.3 %collective-permute-start.4 = (f32[3,64,128]{2,1,0:T(8,128)S(1)}, f32[3,64,128]{2,1,0:T(8,128)S(1)}, u32[]{:S(2)}, u32[]{:S(2)}) collective-permute-start(f32[3,64,128]{2,1,0:T(8,128)S(1)} %get-tuple-element.61), channel_id=1, source_target_pairs={{0,16},{16,0},{1,17},{17,1},{2,18},{18,2},{3,19},{19,3},{4,20},{20... | collective-permute-start | bytes 294920 | tf_op jit(solution)/shard_map/ppermute | solution.py:501
  27.2 1.3 %collective-permute-start.5 = (f32[3,64,128]{2,1,0:T(8,128)S(1)}, f32[3,64,128]{2,1,0:T(8,128)S(1)}, u32[]{:S(2)}, u32[]{:S(2)}) collective-permute-start(f32[3,64,128]{2,1,0:T(8,128)S(1)} %get-tuple-element.60), channel_id=1, source_target_pairs={{0,16},{16,0},{1,17},{17,1},{2,18},{18,2},{3,19},{19,3},{4,20},{20... | collective-permute-start | bytes 294920 | tf_op jit(solution)/shard_map/ppermute | solution.py:501
  31.9 4.0 %copy-start.4 = (f32[2,5,64,128]{3,2,1,0:T(8,128)}, f32[2,5,64,128]{3,2,1,0:T(8,128)S(1)}, u32[]{:S(2)}) copy-start(f32[2,5,64,128]{3,2,1,0:T(8,128)S(1)} %collective-permute-done.force_lo.lo_far) | copy-start | bytes 983044
  32.0 3.9 %copy-start.6 = (f32[2,5,64,128]{3,2,1,0:T(8,128)}, f32[2,5,64,128]{3,2,1,0:T(8,128)S(1)}, u32[]{:S(2)}) copy-start(f32[2,5,64,128]{3,2,1,0:T(8,128)S(1)} %collective-permute-done.1.force_hi.hi_far) | copy-start | bytes 983044
  35.9 1.5 %collective-permute-start.7 = (f32[6,64,128]{2,1,0:T(8,128)S(1)}, f32[6,64,128]{2,1,0:T(8,128)S(1)}, u32[]{:S(2)}, u32[]{:S(2)}) collective-permute-start(f32[6,64,128]{2,1,0:T(8,128)S(1)} %get-tuple-element.57), channel_id=1, source_target_pairs={{0,16},{16,0},{1,17},{17,1},{2,18},{18,2},{3,19},{19,3},{4,20},{20... | collective-permute-start | bytes 589832 | tf_op jit(solution)/shard_map/ppermute | solution.py:501
  36.2 1.7 %collective-permute-start.8 = (f32[6,64,128]{2,1,0:T(8,128)S(1)}, f32[6,64,128]{2,1,0:T(8,128)}, u32[]{:S(2)}, u32[]{:S(2)}) collective-permute-start(f32[6,64,128]{2,1,0:T(8,128)S(1)} %get-tuple-element.58), channel_id=1, source_target_pairs={{0,16},{16,0},{1,17},{17,1},{2,18},{18,2},{3,19},{19,3},{4,20},{20... | collective-permute-start | bytes 589832 | tf_op jit(solution)/shard_map/ppermute | solution.py:501
  36.5 19.1 %copy-start.5 = (f32[2,5,64,128]{3,2,1,0:T(8,128)S(1)}, f32[2,5,64,128]{3,2,1,0:T(8,128)}, u32[]{:S(2)}) copy-start(f32[2,5,64,128]{3,2,1,0:T(8,128)} %copy-done.4) | copy-start | bytes 983044
  36.5 19.1 %copy-start.7 = (f32[2,5,64,128]{3,2,1,0:T(8,128)S(1)}, f32[2,5,64,128]{3,2,1,0:T(8,128)}, u32[]{:S(2)}) copy-start(f32[2,5,64,128]{3,2,1,0:T(8,128)} %copy-done.6) | copy-start | bytes 983044
  38.9 14.7 %collective-permute-start.9 = (f32[7,64,128]{2,1,0:T(8,128)S(1)}, f32[7,64,128]{2,1,0:T(8,128)S(1)}, u32[]{:S(2)}, u32[]{:S(2)}) collective-permute-start(f32[7,64,128]{2,1,0:T(8,128)S(1)} %constant_dynamic-slice_fusion.1), channel_id=1, source_target_pairs={{0,1},{1,2},{2,3},{3,4},{4,5},{5,6},{6,7},{7,8},{8,9},{9,10},{10,1... | collective-permute-start | bytes 688136 | tf_op jit(solution)/shard_map/ppermute | solution.py:520
  53.6 1.5 %collective-permute-start.10 = (f32[7,64,128]{2,1,0:T(8,128)S(1)}, f32[7,64,128]{2,1,0:T(8,128)S(1)}, u32[]{:S(2)}, u32[]{:S(2)}) collective-permute-start(f32[7,64,128]{2,1,0:T(8,128)S(1)} %collective-permute-done.9.pair_a), channel_id=1, source_target_pairs={{0,16},{16,0},{1,17},{17,1},{2,18},{18,2},{3,19},{19,3},{4,20},{20... | collective-permute-start | bytes 688136 | tf_op jit(solution)/shard_map/ppermute | solution.py:501
  63.7 1.5 %collective-permute-start.11 = (f32[6,64,128]{2,1,0:T(8,128)S(1)}, f32[6,64,128]{2,1,0:T(8,128)S(1)}, u32[]{:S(2)}, u32[]{:S(2)}) collective-permute-start(f32[6,64,128]{2,1,0:T(8,128)S(1)} %get-tuple-element.55), channel_id=1, source_target_pairs={{0,16},{16,0},{1,17},{17,1},{2,18},{18,2},{3,19},{19,3},{4,20},{20... | collective-permute-start | bytes 589832 | tf_op jit(solution)/shard_map/ppermute | solution.py:501
  63.9 1.6 %collective-permute-start.12 = (f32[6,64,128]{2,1,0:T(8,128)S(1)}, f32[6,64,128]{2,1,0:T(8,128)S(1)}, u32[]{:S(2)}, u32[]{:S(2)}) collective-permute-start(f32[6,64,128]{2,1,0:T(8,128)S(1)} %get-tuple-element.56), channel_id=1, source_target_pairs={{0,16},{16,0},{1,17},{17,1},{2,18},{18,2},{3,19},{19,3},{4,20},{20... | collective-permute-start | bytes 589832 | tf_op jit(solution)/shard_map/ppermute | solution.py:501
  66.2 9.8 %all-to-all-start.1 = ((f32[32,1,256]{2,1,0:T(1,128)}), f32[32,1,256]{2,1,0:T(1,128)S(1)}, u32[]{:S(2)}, u32[]{:S(2)}) async-start(f32[32,1,256]{2,1,0:T(1,128)} %copy.11), calls=%async_computation.1 | async-start | bytes 65536 | tf_op jit(solution)/shard_map/all_to_all | solution.py:550
  68.7 7.2 %collective-permute-start.13 = (f32[1,64,128]{2,1,0:T(8,128)S(1)}, f32[1,64,128]{2,1,0:T(8,128)S(1)}, u32[]{:S(2)}, u32[]{:S(2)}) collective-permute-start(f32[1,64,128]{2,1,0:T(8,128)S(1)} %constant_dynamic-slice_fusion), channel_id=1, source_target_pairs={{0,1},{1,2},{2,3},{3,4},{4,5},{5,6},{6,7},{7,8},{8,9},{9,10},{10,1... | collective-permute-start | bytes 98312 | tf_op jit(solution)/shard_map/ppermute | solution.py:520
  76.0 1.2 %collective-permute-start.14 = (f32[1,64,128]{2,1,0:T(8,128)S(1)}, f32[1,64,128]{2,1,0:T(8,128)S(1)}, u32[]{:S(2)}, u32[]{:S(2)}) collective-permute-start(f32[1,64,128]{2,1,0:T(8,128)S(1)} %collective-permute-done.13.pair_a), channel_id=1, source_target_pairs={{0,16},{16,0},{1,17},{17,1},{2,18},{18,2},{3,19},{19,3},{4,20},{20... | collective-permute-start | bytes 98312 | tf_op jit(solution)/shard_map/ppermute | solution.py:501
  (4 other events, 3.2 us)

commit v4 on v3

--- a/solution.py
+++ b/solution.py
@@ -187,7 +187,7 @@
         copy.wait()
 
 
-def points_kernel(cells, loads, nodes, forces, force_ref, base_ref):
+def points_kernel(cells, loads, nodes, forces, force_ref, base_far, base_ref, sems):
     rows = cells + 2 * SOURCE
     size_y, size_z = base_ref.shape[2:]
     zero = jnp.zeros((size_y, size_z), jnp.float32)
@@ -212,6 +212,9 @@
             return carry
 
         lax.fori_loop(0, nodes.shape[1], one_point, 0)
+    copy = pltpu.make_async_copy(base_ref, base_far, sems.at[0])
+    copy.start()
+    copy.wait()
 
 
 def base_row(l, q, cells, base_in, force_lo, force_hi):
@@ -226,7 +229,7 @@
     return [range(SOURCE + k, SOURCE + cells - k) for k in range(SWEEPS)]
 
 
-def early_kernel(cells, loads, self_weight, density, passive, support, base_ref, pair_a, pair_b,
+def early_kernel(cells, loads, self_weight, density, passive, support, base_ref, pair_a, pair_b, pair_c,
                  design_wide, weight, inverse, resid_ref, steps_ref, shown_ref, stiff,
                  free_wide, design_low, design_high):
     even, is_first, is_last = place_of()
@@ -242,8 +245,8 @@
         stiff[i] = jnp.where(is_first, zero, stiffness_of(low))
         stiff[DESIGN + cells + i] = jnp.where(is_last, zero, stiffness_of(high))
     for i in range(SOURCE):
-        low = jnp.where(even, pair_a[DESIGN + i], pair_b[DESIGN + i])
-        high = jnp.where(even, pair_b[DESIGN + i], pair_a[DESIGN + i])
+        low = jnp.where(even, pair_a[DESIGN + i], pair_c[i])
+        high = jnp.where(even, pair_c[i], pair_a[DESIGN + i])
         free_wide[i] = jnp.where(is_first, zero, low)
         free_wide[SOURCE + cells + i] = jnp.where(is_last, zero, high)
     for i in range(cells):
@@ -276,8 +279,15 @@
 
 
 def first_kernel(cells, loads, self_weight, force_lo, force_hi, base_in, design_wide, weight, inverse,
-                 resid_in, steps_in, shown_in, sense_ref, tile_ref, resid_ref, steps_ref, shown_ref):
-    _, is_first, is_last = place_of()
+                 resid_in, steps_in, shown_in, lo_far, hi_far, keep, spare, outer, rest, tile_ref,
+                 resid_ref, steps_ref, shown_ref, sense_ref, sems):
+    copies = [
+        pltpu.make_async_copy(source, target, sems.at[i])
+        for i, (source, target) in enumerate(((force_lo, lo_far), (force_hi, hi_far)))
+    ]
+    for copy in copies:
+        copy.start()
+    even, is_first, is_last = place_of()
     shape = design_wide.shape[1:]
     masks = inner_masks(shape)
     rows = cells + 2 * SOURCE
@@ -306,13 +316,35 @@
                 sweep_row(k, q, loads, weight, resid, steps, resid_ref, steps_ref, shown_ref, shown)
     for i in range(cells):
         sense_ref[i] = energy_row(i, loads, design_wide[DESIGN + i], shown, masks)
+    cut_rows(cells, even, sense_ref, keep, spare, outer, rest)
     own = design_wide.at[pl.ds(DESIGN, cells)]
     spread_totals(tile_ref, filter_total(cells, sense_ref, is_first, is_last, masks), fold_rows(cells, own))
-
-
-def moment_kernel(cells, sense, pair_a, pair_b, moment_ref, sense_wide):
+    for copy in copies:
+        copy.wait()
+
+
+def cut_rows(cells, even, sense, keep, spare, outer, rest):
+    width = keep.shape[0]
+    for i in range(width):
+        first, last = sense[i], sense[cells - width + i]
+        keep[i] = jnp.where(even, last, first)
+        outer[i] = jnp.where(even, first, last)
+    for i in range(cells - width):
+        first, last = sense[i], sense[width + i]
+        spare[i] = jnp.where(even, first, last)
+        rest[i] = jnp.where(even, last, first)
+
+
+def whole_row(i, cells, even, edge, spare, rest):
+    width = edge.shape[0]
+    if_even = spare[i] + rest[i] if i < cells - width else edge[i - (cells - width)]
+    if_odd = edge[i] if i < width else spare[i - width] + rest[i - width]
+    return jnp.where(even, if_even, if_odd)
+
+
+def moment_kernel(cells, edge, spare, rest, pair_a, pair_b, moment_ref, sense_wide):
     even, is_first, is_last = place_of()
-    shape = sense.shape[1:]
+    shape = edge.shape[1:]
     masks = inner_masks(shape)
     zero = jnp.zeros(shape, jnp.float32)
     for i in range(SENSE):
@@ -321,11 +353,11 @@
         sense_wide[i] = jnp.where(is_first, zero, low)
         sense_wide[SENSE + cells + i] = jnp.where(is_last, zero, high)
     for i in range(cells):
-        sense_wide[SENSE + i] = sense[i]
-    inside, outer = edge_planes(masks)
+        sense_wide[SENSE + i] = whole_row(i, cells, even, edge, spare, rest)
+    inside, at_ends = edge_planes(masks)
     for r in range(cells + 2 * DESIGN):
         at_end = (is_first & (r == DESIGN)) | (is_last & (r == DESIGN + cells - 1))
-        moment_ref[r] = filtered_row(r, sense_wide, masks) * jnp.where(at_end, outer, inside)
+        moment_ref[r] = filtered_row(r, sense_wide, masks) * jnp.where(at_end, at_ends, inside)
 
 
 def filtered_row(r, sense_wide, masks):
@@ -337,38 +369,41 @@
 
 
 def spread_totals(tile_ref, abs_tile, density_tile):
-    count, width = tile_ref.shape
     row = jnp.concatenate([jnp.sum(tile, axis=0, keepdims=True) for tile in (abs_tile, density_tile)], axis=1)
-    tile_ref[...] = jnp.broadcast_to(row, (count, width))
-
-
-def rate_and_pull(totals, total_cells, share):
-    half = totals.shape[1] // 2
+    tile_ref[...] = jnp.broadcast_to(row[None], tile_ref.shape)
+
+
+def totals_kernel(total_cells, share, decay, tile_in, before, total_ref):
+    half = tile_in.shape[2] // 2
+    totals = jnp.sum(tile_in[...], axis=0)
     abs_total = jnp.sum(totals[:, :half], keepdims=True)
+    if decay:
+        abs_total = abs_total + decay * before[2:3, :1]
     density_total = jnp.sum(totals[:, half:], keepdims=True) * share
-    mean_step = abs_total / total_cells + 1e-6
-    return step_size / mean_step, volume_pull * (density_total / total_cells - volume_target)
-
-
-def second_kernel(cells, loads, total_cells, share, self_weight, tile_in, moment_wide,
+    rate = step_size / (abs_total / total_cells + 1e-6)
+    pull = volume_pull * (density_total / total_cells - volume_target)
+    row = lax.broadcasted_iota(jnp.int32, total_ref.shape, 0)
+    total_ref[...] = jnp.where(row == 0, rate, jnp.where(row == 1, pull, abs_total))
+
+
+def second_kernel(cells, loads, self_weight, step_ref, moment_wide,
                   design_wide, base_far, lo_far, hi_far,
-                  shown_ref, design_out, sense_ref, tile_ref,
+                  shown_ref, design_out, keep, spare, outer, rest, tile_ref,
                   stiff, weight, inverse, resid_ref, steps_ref, shown_to, design_new,
-                  base_in, force_lo, force_hi, sems):
+                  base_in, force_lo, force_hi, sense_ref, sems):
     copies = [
         pltpu.make_async_copy(source, target, sems.at[i])
-        for i, (source, target) in enumerate(
-            ((base_far, base_in), (lo_far, force_lo), (hi_far, force_hi)))
+        for i, (source, target) in enumerate(((base_far, base_in), (lo_far, force_lo), (hi_far, force_hi)))
     ]
     for copy in copies:
         copy.start()
-    _, is_first, is_last = place_of()
+    even, is_first, is_last = place_of()
     shape = moment_wide.shape[1:]
     masks = inner_masks(shape)
     wide = cells + 2 * DESIGN
     rows = cells + 2 * SOURCE
     zero = jnp.zeros(shape, jnp.float32)
-    rate, pull = rate_and_pull(tile_in[...], total_cells, share)
+    rate, pull = step_ref[0:1, :], step_ref[1:2, :]
     for r in range(wide):
         signed = design_wide[r]
         before = jnp.abs(signed)
@@ -408,13 +443,14 @@
         copy.start()
     for i in range(cells):
         sense_ref[i] = energy_row(i, loads, design_new[DESIGN + i], shown, masks)
+    cut_rows(cells, even, sense_ref, keep, spare, outer, rest)
     own = design_new.at[pl.ds(DESIGN, cells)]
     spread_totals(tile_ref, filter_total(cells, sense_ref, is_first, is_last, masks), fold_rows(cells, own))
     for copy in results + [own_rows]:
         copy.wait()
 
 
-def last_moment_kernel(cells, slab, sense, pair_a, pair_b, moment_wide, design_far, passive_far,
+def last_moment_kernel(cells, slab, edge, spare, rest, pair_a, pair_b, moment_wide, design_far, passive_far,
                        momentum_ref, kept_ref, before_ref, least_ref, most_ref, sense_wide, momentum_all,
                        kinds, sems):
     even, is_first, is_last = place_of()
@@ -425,20 +461,20 @@
     ]
     for copy in copies:
         copy.start()
-    shape = sense.shape[1:]
+    shape = edge.shape[1:]
     masks = inner_masks(shape)
     zero = jnp.zeros(shape, jnp.float32)
     sense_wide[0] = jnp.where(is_first, zero, jnp.where(even, pair_a[0], pair_b[0]))
     sense_wide[cells + 1] = jnp.where(is_last, zero, jnp.where(even, pair_b[0], pair_a[0]))
     for i in range(cells):
-        sense_wide[i + 1] = sense[i]
-    inside, outer = edge_planes(masks)
+        sense_wide[i + 1] = whole_row(i, cells, even, edge, spare, rest)
+    inside, at_ends = edge_planes(masks)
     for i in range(cells):
         scale = inside
         if i == 0:
-            scale = jnp.where(is_first, outer, inside)
+            scale = jnp.where(is_first, at_ends, inside)
         elif i == cells - 1:
-            scale = jnp.where(is_last, outer, inside)
+            scale = jnp.where(is_last, at_ends, inside)
         momentum_all[i] = moment_decay * moment_wide[DESIGN + i] + filtered_row(i, sense_wide, masks) * scale
         momentum = momentum_all[i, window, :]
         kept_ref[i] = momentum
@@ -453,12 +489,8 @@
     copy.wait()
 
 
-def last_kernel(cells, total_cells, share, tile_before, tile_in, momentum_ref, before_ref, least_ref, most_ref,
-                design_ref, design_near, sems):
-    half = tile_in.shape[1] // 2
-    along = lax.broadcasted_iota(jnp.int32, tile_in.shape, 1)
-    totals = tile_in[...] + jnp.where(along < half, moment_decay * tile_before[...], 0.0)
-    rate, pull = rate_and_pull(totals, total_cells, share)
+def last_kernel(cells, step_ref, momentum_ref, before_ref, least_ref, most_ref, design_ref, design_near, sems):
+    rate, pull = step_ref[0:1, :], step_ref[1:2, :]
     for i in range(cells):
         moved = before_ref[i] - rate * momentum_ref[i] - pull
         design_near[i] = jnp.minimum(jnp.maximum(moved, least_ref[i]), most_ref[i])
@@ -471,17 +503,17 @@
 SMEM = pl.BlockSpec(memory_space=pltpu.SMEM)
 
 
-def on_core(kernel, operands, scalars, outs, scratch, cost=0, limit=4, far=0, far_outs=0, keep=False):
+def on_core(kernel, operands, scalars, outs, scratch, cost=0, limit=4, far=0, far_outs=0):
     anywhere = pl.BlockSpec(memory_space=pl.ANY)
     operands = [
         pltpu.with_memory_space_constraint(operand, pltpu.VMEM)
-        if scalars <= i and (i < len(operands) - far or keep) else pltpu.with_memory_space_constraint(operand, pltpu.HBM) if i >= len(operands) - far else operand
+        if scalars <= i < len(operands) - far else pltpu.with_memory_space_constraint(operand, pltpu.HBM) if i >= len(operands) - far else operand
         for i, operand in enumerate(operands)
     ]
     return pl.pallas_call(
         kernel,
         out_shape=[
-            jax.ShapeDtypeStruct(shape, jnp.float32) if i < far_outs else pltpu.VMEM(shape, jnp.float32)
+            pltpu.HBM(shape, jnp.float32) if i < far_outs else pltpu.VMEM(shape, jnp.float32)
             for i, shape in enumerate(outs)
         ],
         in_specs=[SMEM] * scalars + [VMEM] * (len(operands) - scalars - far) + [anywhere] * far,
@@ -501,10 +533,6 @@
     return lax.ppermute(value, axis, [(i, i ^ bit) for i in range(count)])
 
 
-def swap_parts(value, count, bit=1):
-    return jnp.concatenate([swap(value[i:i + count], "load", bit) for i in range(0, value.shape[0], count)])
-
-
 def along(value, step):
     count = lax.axis_size("brick")
     pairs = [(i, i + step) for i in range(count) if 0 <= i + step < count]
@@ -530,26 +558,24 @@
     return value
 
 
-def load_terms(value):
-    bits = bits_of(lax.axis_size("load"))
-    for bit in bits[:-1]:
-        value = value + swap(value, "load", bit)
-    return value, swap_parts(value, 6, bits[-1])
-
-
 def after(value, other):
     return lax.optimization_barrier((value, other))[0]
 
 
-def meet(sense, tiles, width, even, filtered):
-    cells = sense.shape[0]
-    sense_a, sense_b = load_terms(sense)
-    sense = sense_a + sense_b
-    edge = lax.dynamic_slice_in_dim(sense, jnp.where(even, cells - width, 0), width, 0)
+def add_kernel(first, second, sum_ref):
+    sum_ref[...] = first[...] + second[...]
+
+
+def meet(parts, tiles, filtered, totals):
+    total = totals(lax.all_to_all(tiles, ("load", "brick"), 0, 0, tiled=True))
+    for bit in bits_of(lax.axis_size("load"))[1:]:
+        parts = [part + swap(part, "load", bit) for part in parts]
+    keep, spare, outer, rest = parts
+    (edge,) = on_core(add_kernel, (keep, swap(outer, "load", 1)), 0, [keep.shape], [])
     pair_a = both_ways(edge)
-    tiles = lax.all_to_all(after(tiles, edge), ("load", "brick"), 0, 0, tiled=True)
-    pair_b = swap(after(pair_a, tiles), "load", 1)
-    return filtered(sense, pair_a, pair_b), tiles
+    rest = swap(rest, "load", 1)
+    pair_b = swap(pair_a, "load", 1)
+    return filtered(edge, spare, rest, pair_a, pair_b), total
 
 
 def body(density, passive, support, load_nodes, load_force, self_weight, body_force):
@@ -559,13 +585,15 @@
     slab = size_y // load_count
     total_cells = float(cells * bricks * size_y * size_z)
     share = 1.0 / load_count
-    even = lax.axis_index("load") % 2 == 0
     plane = (size_y, size_z)
     wide, rows = cells + 2 * DESIGN, cells + 2 * SOURCE
-    tile = (load_count * bricks, 2 * size_z)
+    tile = (load_count * bricks, 1, 2 * size_z)
     shown_shape = (loads, cells + 2) + plane
     resid_shape = (loads, rows) + plane
     steps_shape = (SWEEPS - 1, loads, rows) + plane
+
+    def parts_of(width):
+        return [(count,) + plane for count in (width, cells - width, width, cells - width)]
 
     payload, upper, lower = on_core(
         functools.partial(prepare_kernel, cells),
@@ -579,33 +607,47 @@
     pair_a = both_ways(payload)
     force_lo = along(upper, 1)
     force_hi = along(lower, -1)
-    (base,) = on_core(
+    base_far, base = on_core(
         functools.partial(points_kernel, cells, loads),
         (load_nodes, load_force, after(body_force, (upper, lower))),
         2,
-        [resid_shape],
-        [],
+        [resid_shape, resid_shape],
+        [pltpu.SemaphoreType.DMA((1,))],
         cost=1,
-    )
-    pair_b = swap_parts(after(pair_a, base), 3)
+        far_outs=1,
+    )
+    pair_a = after(pair_a, base)
+    pair_b = swap(pair_a[:DESIGN], "load", 1)
+    pair_c = swap(pair_a[DESIGN:], "load", 1)
     design_wide, weight, inverse, resid, steps, shown = on_core(
         functools.partial(early_kernel, cells, loads),
-        (self_weight, density, passive, support, base, pair_a, pair_b),
+        (self_weight, density, passive, support, base, pair_a, pair_b, pair_c),
         1,
         [(wide,) + plane, (6, rows) + plane, (rows,) + plane,
          (loads, cells) + plane, (SWEEPS - 1, loads, cells) + plane, (loads, cells - 2 * (SWEEPS - 1)) + plane],
         [(wide,) + plane, (rows,) + plane, (DESIGN,) + plane, (DESIGN,) + plane],
         cost=1,
     )
-    sense, tiles = on_core(
+    lo_far, hi_far, *parts, tiles = on_core(
         functools.partial(first_kernel, cells, loads),
         (self_weight, force_lo, force_hi, base, design_wide, weight, inverse, resid, steps, shown),
         1,
-        [(cells,) + plane, tile],
-        [resid_shape, steps_shape, shown_shape],
-    )
-    (moment_wide,), tiles_first = meet(
-        sense, tiles, SENSE, even,
+        [(loads, SOURCE) + plane] * 2 + parts_of(SENSE) + [tile],
+        [resid_shape, steps_shape, shown_shape, (cells,) + plane, pltpu.SemaphoreType.DMA((2,))],
+        far_outs=2,
+    )
+    def totals(decay, before):
+        return lambda tiles: on_core(
+            functools.partial(totals_kernel, total_cells, share, decay),
+            (tiles, before),
+            0,
+            [(8, size_z)],
+            [],
+            cost=2000000000,
+        )[0]
+
+    (moment_wide,), step_first = meet(
+        parts, tiles,
         lambda *sensed: on_core(
             functools.partial(moment_kernel, cells),
             sensed,
@@ -613,22 +655,22 @@
             [(wide,) + plane],
             [(cells + 2 * SENSE,) + plane],
         ),
-    )
-    shown, design, sense, tiles = on_core(
-        functools.partial(second_kernel, cells, loads, total_cells, share),
-        (self_weight, tiles_first, moment_wide, design_wide, base, force_lo, force_hi),
+        totals(0.0, tiles),
+    )
+    shown, design, *parts, tiles = on_core(
+        functools.partial(second_kernel, cells, loads),
+        (self_weight, step_first, moment_wide, design_wide, base_far, lo_far, hi_far),
         1,
-        [(loads, cells) + plane, (cells,) + plane, (cells,) + plane, tile],
+        [(loads, cells) + plane, (cells,) + plane] + parts_of(1) + [tile],
         [(wide,) + plane, (6, rows) + plane, (rows,) + plane, resid_shape, steps_shape, shown_shape, (wide,) + plane,
-         resid_shape, (loads, SOURCE) + plane, (loads, SOURCE) + plane,
+         resid_shape, (loads, SOURCE) + plane, (loads, SOURCE) + plane, (cells,) + plane,
          pltpu.SemaphoreType.DMA((4 + loads,))],
         limit=14,
         far=3,
         far_outs=2,
-        keep=True,
-    )
-    last_ones, tiles_last = meet(
-        sense, tiles, 1, even,
+    )
+    last_ones, step_last = meet(
+        parts, tiles,
         lambda *sensed: on_core(
             functools.partial(last_moment_kernel, cells, slab),
             sensed + (moment_wide, design, passive),
@@ -639,10 +681,11 @@
             far=2,
             far_outs=1,
         ),
+        totals(moment_decay, step_first),
     )
     (design,) = on_core(
-        functools.partial(last_kernel, cells, total_cells, share),
-        (tiles_first, tiles_last) + tuple(last_ones[1:]),
+        functools.partial(last_kernel, cells),
+        (step_last,) + tuple(last_ones[1:]),
         0,
         [(cells, slab, size_z)],
         [(cells, slab, size_z), pltpu.SemaphoreType.DMA((1,))],

time: 80 us -> 75.4 us (0.943)
  blocking collectives: 10.3 us -> 0 us
  starting transfers between devices: 22 us -> 26.8 us
  Pallas kernels: 21.6 us -> 25 us
  local copies, waits for them, and re-layouts: 4.07 us -> 2.53 us
  other arithmetic: 1.04 us -> 0 us
    all_to_all x1 -> x0, blocking collectives: 10.3 us -> none  [meet(): lax.all_to_all(after(tiles, edge), ('load', 'brick'), 0, 0, tiled=True)]
    ppermute x10 -> x8, waiting for transfers between devices: 6.95 us -> 2.28 us  [swap(): return lax.ppermute(value, axis, [(i, i ^ bit) for i in range(count)])]
    all_to_all x1 -> x2, starting transfers between devices: 2.57 us -> 6.09 us  [meet(): total = totals(lax.all_to_all(tiles, ('load', 'brick'), 0, 0, tiled=True))]
    pallas_call x8 -> x12, Pallas kernels: 21.6 us -> 25 us  [on_core(): pl.pallas_call(kernel, out_shape=[pltpu.HBM(shape, jnp.float32) if i < fa...]
    all_to_all x1 -> x2, waiting for transfers between devices: 3.66 us -> 7.03 us  [meet(): total = totals(lax.all_to_all(tiles, ('load', 'brick'), 0, 0, tiled=True))]
    ppermute x10 -> x8, starting transfers between devices: 1.96 us -> 3.16 us  [swap(): return lax.ppermute(value, axis, [(i, i ^ bit) for i in range(count)])]
    add x2 -> x0, other arithmetic: 1.02 us -> none  [meet(): sense = sense_a + sense_b]
    ppermute x3, waiting for transfers between devices: 8.82 us -> 9.81 us  [both_ways(): return lax.ppermute(value, ('load', 'brick'), pairs)]
  transfers between devices with their start and end apart: 16 -> 15, of which waited for: 12 -> 7; matrix products, arithmetic and copies ran while one was open for 0% -> 0% of each run, Pallas kernels for 8% -> 11%
where the time goes in v4:
time: 75.4 us; the launch traced here: 74.4 us
  starting transfers between devices  26.8 us (36%)
  Pallas kernels  25 us (33%)
  waiting for transfers between devices  19.1 us (25%)
  local copies, waits for them, and re-layouts  2.53 us (3%)
  between operations  1.08 us (1%)
    pallas_call x12, Pallas kernels, on_core(): pl.pallas_call(kernel, out_shape=[pltpu.HBM(shape, jnp.float32) if i < fa...  25 us
    ppermute x3, starting transfers between devices, both_ways(): return lax.ppermute(value, ('load', 'brick'), pairs)  12.8 us
    ppermute x3, waiting for transfers between devices, both_ways(): return lax.ppermute(value, ('load', 'brick'), pairs)  9.81 us
    all_to_all x2, waiting for transfers between devices, meet(): total = totals(lax.all_to_all(tiles, ('load', 'brick'), 0, 0, tiled=True))  7.03 us
    all_to_all x2, starting transfers between devices, meet(): total = totals(lax.all_to_all(tiles, ('load', 'brick'), 0, 0, tiled=True))  6.09 us
    ppermute x2, starting transfers between devices, along(): return lax.ppermute(value, 'brick', pairs)  4.69 us
    ppermute x8, starting transfers between devices, swap(): return lax.ppermute(value, axis, [(i, i ^ bit) for i in range(count)])  3.16 us
    unnamed x14, local copies, waits for them, and re-layouts  2.5 us
  transfers between devices with their start and end apart: 15, of which 7 were waited for; matrix products, arithmetic and copies ran while one was open for 0% of the time, Pallas kernels for 11%

profile of v4, /device:TPU:0, one launch (start us, length us, event | category | flops | bytes accessed | tf_op | source)
XLA Modules:
  0.0 74.4 jit_solution(13864111625750743453)
XLA Ops:
  0.7 1.5 %shard_map.94 = (f32[11,64,128]{2,1,0:T(8,128)S(1)}, f32[2,5,64,128]{3,2,1,0:T(8,128)S(1)}, f32[2,5,64,128]{3,2,1,0:T(8,128)S(1)}) custom-call(f32[12,64,128]{2,1,0:T(8,128)} %density.3, s32[12,64,128]{2,1,0:T(8,128)} %passive_far.1, s32[12,64,128]{2,1,0:T(8,128)} %support.3, f32[2,12,64,128]{3,2,1,0:T(8,128)} %force_ref), custom_call_target="tpu_custom_call" | custom-call | tf_op jit(solution)/shard_map/pallas_call | solution.py:513
  2.2 4.9 %collective-permute-start.2 = (f32[11,64,128]{2,1,0:T(8,128)S(1)}, f32[11,64,128]{2,1,0:T(8,128)S(1)}, u32[]{:S(2)}, u32[]{:S(2)}) collective-permute-start(f32[11,64,128]{2,1,0:T(8,128)S(1)} %get-tuple-element.39), channel_id=1, source_target_pairs={{0,1},{1,2},{2,3},{3,4},{4,5},{5,6},{6,7},{7,8},{8,9},{9,10},{10,1... | collective-permute-start | bytes 1081352 | tf_op jit(solution)/shard_map/ppermute | solution.py:548
  7.0 3.4 %collective-permute-start = (f32[2,5,64,128]{3,2,1,0:T(8,128)S(1)}, f32[2,5,64,128]{3,2,1,0:T(8,128)S(1)}, u32[]{:S(2)}, u32[]{:S(2)}) collective-permute-start(f32[2,5,64,128]{3,2,1,0:T(8,128)S(1)} %get-tuple-element.35), channel_id=1, source_target_pairs={{0,1},{1,2},{2,3},{3,4},{4,5},{5,6},{6,7},{7,8},{8,9},{9,10},{10,1... | collective-permute-start | bytes 983048 | tf_op jit(solution)/shard_map/ppermute | solution.py:539
  10.4 1.3 %collective-permute-start.1 = (f32[2,5,64,128]{3,2,1,0:T(8,128)S(1)}, f32[2,5,64,128]{3,2,1,0:T(8,128)S(1)}, u32[]{:S(2)}, u32[]{:S(2)}) collective-permute-start(f32[2,5,64,128]{3,2,1,0:T(8,128)S(1)} %get-tuple-element.36), channel_id=1, source_target_pairs={{1,0},{2,1},{3,2},{4,3},{5,4},{6,5},{7,6},{8,7},{9,8},{10,9},{11,1... | collective-permute-start | bytes 983048 | tf_op jit(solution)/shard_map/ppermute | solution.py:539
  11.8 1.1 %copy-done.1 = f32[2,12,64,128]{3,2,1,0:T(8,128)S(1)} copy-done((f32[2,12,64,128]{3,2,1,0:T(8,128)S(1)}, f32[2,12,64,128]{3,2,1,0:T(8,128)}, u32[]{:S(2)}) %copy-start.1) | copy-done | bytes 786456
  12.9 0.7 copy-done.5
  14.2 3.9 %shard_map.95 = (f32[2,22,64,128]{3,2,1,0:T(8,128)}, f32[2,22,64,128]{3,2,1,0:T(8,128)S(1)}) custom-call(s32[2,64]{1,0:T(2,128)S(1)} %copy-done.5, f32[2,64]{1,0:T(2,128)S(1)} %copy-done.6, f32[2,12,64,128]{3,2,1,0:T(8,128)S(1)} %copy-done.1), custom_call_target="tpu_custom_call" | custom-call | flops 1 | bytes 1 | tf_op jit(solution)/shard_map/pallas_call | solution.py:513
  18.2 7.8 %collective-permute-done.2.pair_a = f32[11,64,128]{2,1,0:T(8,128)S(1)} collective-permute-done((f32[11,64,128]{2,1,0:T(8,128)S(1)}, f32[11,64,128]{2,1,0:T(8,128)S(1)}, u32[]{:S(2)}, u32[]{:S(2)}) %collective-permute-start.2) | collective-permute-done | bytes 360480 | tf_op jit(solution)/shard_map/ppermute | solution.py:548
  26.6 1.1 %collective-permute-done.4.pair_c = f32[5,64,128]{2,1,0:T(8,128)S(1)} collective-permute-done((f32[5,64,128]{2,1,0:T(8,128)S(1)}, f32[5,64,128]{2,1,0:T(8,128)S(1)}, u32[]{:S(2)}, u32[]{:S(2)}) %collective-permute-start.4) | collective-permute-done | bytes 163872 | tf_op jit(solution)/shard_map/ppermute | solution.py:533
  27.7 3.4 %shard_map.96 = (f32[24,64,128]{2,1,0:T(8,128)S(1)}, f32[6,22,64,128]{3,2,1,0:T(8,128)S(1)}, f32[22,64,128]{2,1,0:T(8,128)S(1)}, f32[2,12,64,128]{3,2,1,0:T(8,12...) custom-call(f32[2]{0:T(128)S(1)} %copy-done.4, f32[12,64,128]{2,1,0:T(8,128)S(1)} %copy-done.2, ...), custom_call_target="tpu_custom_call" | custom-call | flops 1 | bytes 1 | tf_op jit(solution)/shard_map/pallas_call | solution.py:513
  31.1 5.2 %shard_map.97 = (f32[2,5,64,128]{3,2,1,0:T(8,128)}, f32[2,5,64,128]{3,2,1,0:T(8,128)}, f32[7,64,128]{2,1,0:T(8,128)S(1)}, f32[5,64,128]{2,1,0:T(8,128)S(1)}, f32...) custom-call(f32[2]{0:T(128)S(1)} %copy-done.4, ...), custom_call_target="tpu_custom_call" | custom-call | tf_op jit(solution)/shard_map/pallas_call | solution.py:513
  36.7 1.2 %collective-permute-done.5.second = f32[7,64,128]{2,1,0:T(8,128)S(1)} collective-permute-done((f32[7,64,128]{2,1,0:T(8,128)S(1)}, f32[7,64,128]{2,1,0:T(8,128)S(1)}, u32[]{:S(2)}, u32[]{:S(2)}) %collective-permute-start.5) | collective-permute-done | bytes 229408 | tf_op jit(solution)/shard_map/ppermute | solution.py:533
  37.9 4.4 %collective-permute-start.7 = (f32[7,64,128]{2,1,0:T(8,128)S(1)}, f32[7,64,128]{2,1,0:T(8,128)S(1)}, u32[]{:S(2)}, u32[]{:S(2)}) collective-permute-start(f32[7,64,128]{2,1,0:T(8,128)S(1)} %shard_map.99.edge), channel_id=1, source_target_pairs={{0,1},{1,2},{2,3},{3,4},{4,5},{5,6},{6,7},{7,8},{8,9},{9,10},{10,1... | collective-permute-start | bytes 688136 | tf_op jit(solution)/shard_map/ppermute | solution.py:548
  42.3 3.5 %all-to-all-start = ((f32[32,1,256]{2,1,0:T(1,128)}), f32[32,1,256]{2,1,0:T(1,128)S(1)}, u32[]{:S(2)}, u32[]{:S(2)}) async-start(f32[32,1,256]{2,1,0:T(1,128)} %get-tuple-element.47.before), calls=%async_computation | async-start | bytes 65536 | tf_op jit(solution)/shard_map/all_to_all | solution.py:570
  46.3 1.6 %collective-permute-start.8 = (f32[7,64,128]{2,1,0:T(8,128)S(1)}, f32[7,64,128]{2,1,0:T(8,128)S(1)}, u32[]{:S(2)}, u32[]{:S(2)}) collective-permute-start(f32[7,64,128]{2,1,0:T(8,128)S(1)} %collective-permute-done.7.pair_a), channel_id=1, source_target_pairs={{0,16},{16,0},{1,17},{17,1},{2,18},{18,2},{3,19},{19,3},{4,20},{20... | collective-permute-start | bytes 688136 | tf_op jit(solution)/shard_map/ppermute | solution.py:533
  47.9 5.0 %all-to-all-done.tile_in = f32[32,1,256]{2,1,0:T(1,128)S(1)} async-done(((f32[32,1,256]{2,1,0:T(1,128)}), f32[32,1,256]{2,1,0:T(1,128)S(1)}, u32[]{:S(2)}, u32[]{:S(2)}) %all-to-all-start) | async-done | bytes 32800 | tf_op jit(solution)/shard_map/all_to_all | solution.py:570
  52.9 0.9 %shard_map.98.step_ref.before = f32[8,128]{1,0:T(8,128)S(1)} custom-call(f32[32,1,256]{2,1,0:T(1,128)S(1)} %all-to-all-done.tile_in, f32[32,1,256]{2,1,0:T(1,128)} %get-tuple-element.47.before), custom_call_target="tpu_custom_call" | custom-call | flops 2000000000 | bytes 2000000000 | tf_op jit(solution)/shard_map/pallas_call | solution.py:513
  54.3 7.3 %shard_map.101 = (f32[2,12,64,128]{3,2,1,0:T(8,128)}, f32[12,64,128]{2,1,0:T(8,128)}, f32[1,64,128]{2,1,0:T(8,128)S(1)}, f32[11,64,128]{2,1,0:T(8,128)S(1)}, f32...) custom-call(f32[2]{0:T(128)S(1)} %copy-done.4, f32[8,128]{1,0:T(8,128)S(1)} %shard_map.98.step_ref.before, ...), custom_call_target="tpu_custom_call" | custom-call | tf_op jit(solution)/shard_map/pallas_call | solution.py:513
  62.1 2.6 %all-to-all-start.1 = ((f32[32,1,256]{2,1,0:T(1,128)}), f32[32,1,256]{2,1,0:T(1,128)S(1)}, u32[]{:S(2)}, u32[]{:S(2)}) async-start(f32[32,1,256]{2,1,0:T(1,128)} %get-tuple-element.55), calls=%async_computation.1 | async-start | bytes 65536 | tf_op jit(solution)/shard_map/all_to_all | solution.py:570
  64.7 3.5 %collective-permute-start.11 = (f32[1,64,128]{2,1,0:T(8,128)S(1)}, f32[1,64,128]{2,1,0:T(8,128)S(1)}, u32[]{:S(2)}, u32[]{:S(2)}) collective-permute-start(f32[1,64,128]{2,1,0:T(8,128)S(1)} %shard_map.103.edge), channel_id=1, source_target_pairs={{0,1},{1,2},{2,3},{3,4},{4,5},{5,6},{6,7},{7,8},{8,9},{9,10},{10,1... | collective-permute-start | bytes 98312 | tf_op jit(solution)/shard_map/ppermute | solution.py:548
  68.3 1.6 %collective-permute-done.11.pair_a = f32[1,64,128]{2,1,0:T(8,128)S(1)} collective-permute-done((f32[1,64,128]{2,1,0:T(8,128)S(1)}, f32[1,64,128]{2,1,0:T(8,128)S(1)}, u32[]{:S(2)}, u32[]{:S(2)}) %collective-permute-start.11) | collective-permute-done | bytes 32800 | tf_op jit(solution)/shard_map/ppermute | solution.py:548
  69.9 2.0 %all-to-all-done.1.tile_in = f32[32,1,256]{2,1,0:T(1,128)S(1)} async-done(((f32[32,1,256]{2,1,0:T(1,128)}), f32[32,1,256]{2,1,0:T(1,128)S(1)}, u32[]{:S(2)}, u32[]{:S(2)}) %all-to-all-start.1) | async-done | bytes 32800 | tf_op jit(solution)/shard_map/all_to_all | solution.py:570
  72.1 1.4 %shard_map.104 = (f32[12,32,128]{2,1,0:T(8,128)}, f32[12,32,128]{2,1,0:T(8,128)S(1)}, f32[12,32,128]{2,1,0:T(8,128)S(1)}, f32[12,32,128]{2,1,0:T(8,128)S(1)}, f32[12,32,128]{2,1,0:T(8,128)S(1)}) custom-call(f32[1,64,128]{2,1,0:T(8,128)S(1)} %shard_map.103.edge, f32[11,64,128]{2,1,0:T(8,128)S(1)} %get-tuple-element.58.spare, ...), custom_call_target="tpu_custom_call" | custom-call | tf_op jit(solution)/shard_map/pallas_call | solution.py:513
  73.5 0.7 shard_map.105
  (34 shorter events, 3.5 us)
Async XLA Ops:
  0.6 27.1 %copy-start = (s32[12,64,128]{2,1,0:T(8,128)S(1)}, s32[12,64,128]{2,1,0:T(8,128)}, u32[]{:S(2)}) copy-start(s32[12,64,128]{2,1,0:T(8,128)} %passive_far.1) | copy-start | bytes 1179652
  0.6 27.1 %copy-start.3 = (s32[12,64,128]{2,1,0:T(8,128)S(1)}, s32[12,64,128]{2,1,0:T(8,128)}, u32[]{:S(2)}) copy-start(s32[12,64,128]{2,1,0:T(8,128)} %support.3) | copy-start | bytes 1179652
  0.7 27.1 %copy-start.2 = (f32[12,64,128]{2,1,0:T(8,128)S(1)}, f32[12,64,128]{2,1,0:T(8,128)}, u32[]{:S(2)}) copy-start(f32[12,64,128]{2,1,0:T(8,128)} %density.3) | copy-start | bytes 1179652
  0.7 27.1 %copy-start.4 = (f32[2]{0:T(128)S(1)}, f32[2]{0:T(128)}, u32[]{:S(2)}) copy-start(f32[2]{0:T(128)} %self_weight.5) | copy-start | bytes 28
  2.2 23.8 %collective-permute-start.2 = (f32[11,64,128]{2,1,0:T(8,128)S(1)}, f32[11,64,128]{2,1,0:T(8,128)S(1)}, u32[]{:S(2)}, u32[]{:S(2)}) collective-permute-start(f32[11,64,128]{2,1,0:T(8,128)S(1)} %get-tuple-element.39), channel_id=1, source_target_pairs={{0,1},{1,2},{2,3},{3,4},{4,5},{5,6},{6,7},{7,8},{8,9},{9,10},{10,1... | collective-permute-start | bytes 1081352 | tf_op jit(solution)/shard_map/ppermute | solution.py:548
  7.0 24.1 %collective-permute-start = (f32[2,5,64,128]{3,2,1,0:T(8,128)S(1)}, f32[2,5,64,128]{3,2,1,0:T(8,128)S(1)}, u32[]{:S(2)}, u32[]{:S(2)}) collective-permute-start(f32[2,5,64,128]{3,2,1,0:T(8,128)S(1)} %get-tuple-element.35), channel_id=1, source_target_pairs={{0,1},{1,2},{2,3},{3,4},{4,5},{5,6},{6,7},{7,8},{8,9},{9,10},{10,1... | collective-permute-start | bytes 983048 | tf_op jit(solution)/shard_map/ppermute | solution.py:539
  10.4 20.7 %collective-permute-start.1 = (f32[2,5,64,128]{3,2,1,0:T(8,128)S(1)}, f32[2,5,64,128]{3,2,1,0:T(8,128)S(1)}, u32[]{:S(2)}, u32[]{:S(2)}) collective-permute-start(f32[2,5,64,128]{3,2,1,0:T(8,128)S(1)} %get-tuple-element.36), channel_id=1, source_target_pairs={{1,0},{2,1},{3,2},{4,3},{5,4},{6,5},{7,6},{8,7},{9,8},{10,9},{11,1... | collective-permute-start | bytes 983048 | tf_op jit(solution)/shard_map/ppermute | solution.py:539
  11.7 1.1 %copy-start.1 = (f32[2,12,64,128]{3,2,1,0:T(8,128)S(1)}, f32[2,12,64,128]{3,2,1,0:T(8,128)}, u32[]{:S(2)}) copy-start(f32[2,12,64,128]{3,2,1,0:T(8,128)} %force_ref) | copy-start | bytes 2359300
  12.9 0.7 copy-start.5
  13.6 0.7 copy-start.6
  26.0 1.7 %collective-permute-start.3 = (f32[6,64,128]{2,1,0:T(8,128)S(1)}, f32[6,64,128]{2,1,0:T(8,128)S(1)}, u32[]{:S(2)}, u32[]{:S(2)}) collective-permute-start(f32[6,64,128]{2,1,0:T(8,128)S(1)} %slice.6), channel_id=1, source_target_pairs={{0,16},{16,0},{1,17},{17,1},{2,18},{18,2},{3,19},{19,3},{4,20},{20... | collective-permute-start | bytes 589832 | tf_op jit(solution)/shard_map/ppermute | solution.py:533
  26.1 1.6 %collective-permute-start.4 = (f32[5,64,128]{2,1,0:T(8,128)S(1)}, f32[5,64,128]{2,1,0:T(8,128)S(1)}, u32[]{:S(2)}, u32[]{:S(2)}) collective-permute-start(f32[5,64,128]{2,1,0:T(8,128)S(1)} %slice.7), channel_id=1, source_target_pairs={{0,16},{16,0},{1,17},{17,1},{2,18},{18,2},{3,19},{19,3},{4,20},{20... | collective-permute-start | bytes 491528 | tf_op jit(solution)/shard_map/ppermute | solution.py:533
  36.3 1.6 %collective-permute-start.5 = (f32[7,64,128]{2,1,0:T(8,128)S(1)}, f32[7,64,128]{2,1,0:T(8,128)S(1)}, u32[]{:S(2)}, u32[]{:S(2)}) collective-permute-start(f32[7,64,128]{2,1,0:T(8,128)S(1)} %get-tuple-element.49), channel_id=1, source_target_pairs={{0,16},{16,0},{1,17},{17,1},{2,18},{18,2},{3,19},{19,3},{4,20},{20... | collective-permute-start | bytes 688136 | tf_op jit(solution)/shard_map/ppermute | solution.py:533
  37.9 8.4 %collective-permute-start.7 = (f32[7,64,128]{2,1,0:T(8,128)S(1)}, f32[7,64,128]{2,1,0:T(8,128)S(1)}, u32[]{:S(2)}, u32[]{:S(2)}) collective-permute-start(f32[7,64,128]{2,1,0:T(8,128)S(1)} %shard_map.99.edge), channel_id=1, source_target_pairs={{0,1},{1,2},{2,3},{3,4},{4,5},{5,6},{6,7},{7,8},{8,9},{9,10},{10,1... | collective-permute-start | bytes 688136 | tf_op jit(solution)/shard_map/ppermute | solution.py:548
  42.3 10.6 %all-to-all-start = ((f32[32,1,256]{2,1,0:T(1,128)}), f32[32,1,256]{2,1,0:T(1,128)S(1)}, u32[]{:S(2)}, u32[]{:S(2)}) async-start(f32[32,1,256]{2,1,0:T(1,128)} %get-tuple-element.47.before), calls=%async_computation | async-start | bytes 65536 | tf_op jit(solution)/shard_map/all_to_all | solution.py:570
  46.3 7.5 %collective-permute-start.8 = (f32[7,64,128]{2,1,0:T(8,128)S(1)}, f32[7,64,128]{2,1,0:T(8,128)S(1)}, u32[]{:S(2)}, u32[]{:S(2)}) collective-permute-start(f32[7,64,128]{2,1,0:T(8,128)S(1)} %collective-permute-done.7.pair_a), channel_id=1, source_target_pairs={{0,16},{16,0},{1,17},{17,1},{2,18},{18,2},{3,19},{19,3},{4,20},{20... | collective-permute-start | bytes 688136 | tf_op jit(solution)/shard_map/ppermute | solution.py:533
  47.9 5.9 %collective-permute-start.6 = (f32[5,64,128]{2,1,0:T(8,128)S(1)}, f32[5,64,128]{2,1,0:T(8,128)S(1)}, u32[]{:S(2)}, u32[]{:S(2)}) collective-permute-start(f32[5,64,128]{2,1,0:T(8,128)S(1)} %get-tuple-element.51), channel_id=1, source_target_pairs={{0,16},{16,0},{1,17},{17,1},{2,18},{18,2},{3,19},{19,3},{4,20},{20... | collective-permute-start | bytes 491528 | tf_op jit(solution)/shard_map/ppermute | solution.py:533
  61.6 10.6 %collective-permute-start.10 = (f32[11,64,128]{2,1,0:T(8,128)S(1)}, f32[11,64,128]{2,1,0:T(8,128)S(1)}, u32[]{:S(2)}, u32[]{:S(2)}) collective-permute-start(f32[11,64,128]{2,1,0:T(8,128)S(1)} %get-tuple-element.59), channel_id=1, source_target_pairs={{0,16},{16,0},{1,17},{17,1},{2,18},{18,2},{3,19},{19,3},{4,20},{20... | collective-permute-start | bytes 1081352 | tf_op jit(solution)/shard_map/ppermute | solution.py:533
  61.6 3.1 %collective-permute-start.9 = (f32[1,64,128]{2,1,0:T(8,128)S(1)}, f32[1,64,128]{2,1,0:T(8,128)S(1)}, u32[]{:S(2)}, u32[]{:S(2)}) collective-permute-start(f32[1,64,128]{2,1,0:T(8,128)S(1)} %get-tuple-element.57), channel_id=1, source_target_pairs={{0,16},{16,0},{1,17},{17,1},{2,18},{18,2},{3,19},{19,3},{4,20},{20... | collective-permute-start | bytes 98312 | tf_op jit(solution)/shard_map/ppermute | solution.py:533
  62.1 9.8 %all-to-all-start.1 = ((f32[32,1,256]{2,1,0:T(1,128)}), f32[32,1,256]{2,1,0:T(1,128)S(1)}, u32[]{:S(2)}, u32[]{:S(2)}) async-start(f32[32,1,256]{2,1,0:T(1,128)} %get-tuple-element.55), calls=%async_computation.1 | async-start | bytes 65536 | tf_op jit(solution)/shard_map/all_to_all | solution.py:570
  64.7 5.1 %collective-permute-start.11 = (f32[1,64,128]{2,1,0:T(8,128)S(1)}, f32[1,64,128]{2,1,0:T(8,128)S(1)}, u32[]{:S(2)}, u32[]{:S(2)}) collective-permute-start(f32[1,64,128]{2,1,0:T(8,128)S(1)} %shard_map.103.edge), channel_id=1, source_target_pairs={{0,1},{1,2},{2,3},{3,4},{4,5},{5,6},{6,7},{7,8},{8,9},{9,10},{10,1... | collective-permute-start | bytes 98312 | tf_op jit(solution)/shard_map/ppermute | solution.py:548
  69.9 2.3 %collective-permute-start.12 = (f32[1,64,128]{2,1,0:T(8,128)S(1)}, f32[1,64,128]{2,1,0:T(8,128)S(1)}, u32[]{:S(2)}, u32[]{:S(2)}) collective-permute-start(f32[1,64,128]{2,1,0:T(8,128)S(1)} %collective-permute-done.11.pair_a), channel_id=1, source_target_pairs={{0,16},{16,0},{1,17},{17,1},{2,18},{18,2},{3,19},{19,3},{4,20},{20... | collective-permute-start | bytes 98312 | tf_op jit(solution)/shard_map/ppermute | solution.py:533

commit v5 on v4

--- a/solution.py
+++ b/solution.py
@@ -66,7 +66,20 @@
     return stiff_floor + (1.0 - stiff_floor) * (design * design * design)
 
 
-def weight_row(q, is_free, stiff, weight, inverse, masks):
+class Kept:
+    def __init__(self):
+        self.places = {}
+
+    def put(self, key, ref, index, value):
+        ref[index] = value
+        self.places[key] = (ref, index)
+
+    def get(self, key):
+        ref, index = self.places[key]
+        return ref[index]
+
+
+def weight_row(q, is_free, stiff, weight, inverse, weight_to, inverse_to, place, masks):
     here, below, above = stiff[q + 1], stiff[q], stiff[q + 2]
     around = (below, above) + beside_planes(here, masks)
     total = around[0]
@@ -74,32 +87,19 @@
         total = total + plane
     diagonal = (3.0 + mass_shift) * here + 0.5 * total
     scale = jnp.where(is_free, 1.0 / diagonal, 0.0)
-    inverse[q] = scale
+    inverse.put(q, inverse_to, place, scale)
     half = 0.5 * scale
-    weight[0, q] = half * (here + below)
-    weight[1, q] = half * (here + above)
+    weight.put((0, q), weight_to, (0, place), half * (here + below))
+    weight.put((1, q), weight_to, (1, place), half * (here + above))
     for j in range(4):
-        weight[2 + j, q] = jnp.where(masks[j], half * (here + around[2 + j]), 0.0)
-
-
-class Kept:
-    def __init__(self):
-        self.places = {}
-
-    def put(self, key, ref, index, value):
-        ref[index] = value
-        self.places[key] = (ref, index)
-
-    def get(self, key):
-        ref, index = self.places[key]
-        return ref[index]
+        weight.put((2 + j, q), weight_to, (2 + j, place), jnp.where(masks[j], half * (here + around[2 + j]), 0.0))
 
 
 def sweep_row(k, q, loads, weight, resid, steps, resid_to, steps_to, shown_to, shown, first=0, first_shown=SWEEPS - 1):
     _, factors = chebyshev_factors()
     keep, gain = factors[k]
     last = k == len(factors) - 1
-    faces = [weight[j, q] for j in range(6)]
+    faces = [weight.get((j, q)) for j in range(6)]
     for l in range(loads):
         here = steps.get((k, l, q))
         total = faces[0] * steps.get((k, l, q - 1)) + faces[1] * steps.get((k, l, q + 1))
@@ -225,51 +225,69 @@
     return base_in[l, q]
 
 
-def inner_steps(cells):
-    return [range(SOURCE + k, SOURCE + cells - k) for k in range(SWEEPS)]
-
-
-def early_kernel(cells, loads, self_weight, density, passive, support, base_ref, pair_a, pair_b, pair_c,
-                 design_wide, weight, inverse, resid_ref, steps_ref, shown_ref, stiff,
-                 free_wide, design_low, design_high):
-    even, is_first, is_last = place_of()
-    shape = density.shape[1:]
-    masks = inner_masks(shape)
+def inner_steps(cells, margin):
+    return [range(SOURCE + margin + k, SOURCE + cells - margin - k) for k in range(SWEEPS)]
+
+
+def outer_place(q, cells):
+    return q if q <= SOURCE else q - (cells - 2)
+
+
+def start_row(q, base, design, self_weight, inverse, resid, steps, resid_to, steps_to, first):
+    first_scale, _ = chebyshev_factors()
+    for l, one in enumerate(base):
+        left = inverse.get(q) * (one + self_weight[l] * design)
+        resid.put((l, q), resid_to, (l, q - first), left)
+        steps.put((0, l, q), steps_to, (0, l, q - first), first_scale * left)
+
+
+def inner_places(cells, loads, near, early):
+    weight, inverse, resid, steps, shown = Kept(), Kept(), Kept(), Kept(), Kept()
     rows = cells + 2 * SOURCE
-    zero = jnp.zeros(shape, jnp.float32)
-    for i in range(DESIGN):
-        low = jnp.where(even, pair_a[i], pair_b[i])
-        high = jnp.where(even, pair_b[i], pair_a[i])
-        design_low[i] = low
-        design_high[i] = high
-        stiff[i] = jnp.where(is_first, zero, stiffness_of(low))
-        stiff[DESIGN + cells + i] = jnp.where(is_last, zero, stiffness_of(high))
-    for i in range(SOURCE):
-        low = jnp.where(even, pair_a[DESIGN + i], pair_c[i])
-        high = jnp.where(even, pair_c[i], pair_a[DESIGN + i])
-        free_wide[i] = jnp.where(is_first, zero, low)
-        free_wide[SOURCE + cells + i] = jnp.where(is_last, zero, high)
+    near_rows, early_rows = inner_steps(cells, 1), inner_steps(cells, 0)
+    for q in range(rows):
+        inside = q in near_rows[0]
+        if not inside and early is None:
+            continue
+        place = q - SOURCE if inside else outer_place(q, cells)
+        weights, inverses = (near if inside else early)[:2]
+        inverse.places[q] = (inverses, place)
+        for j in range(6):
+            weight.places[(j, q)] = (weights, (j, place))
+    for refs, ranges in ((early, early_rows), (near, near_rows)):
+        if refs is None:
+            continue
+        for l in range(loads):
+            for k in range(SWEEPS - 1):
+                for q in ranges[k]:
+                    steps.places[(k, l, q)] = (refs[3], (k, l, q - SOURCE))
+            for q in ranges[SWEEPS - 1]:
+                shown.places[(l, q)] = (refs[4], (l, q - SOURCE - (SWEEPS - 1)))
+    for l in range(loads):
+        for q in early_rows[0]:
+            depth = min(q - SOURCE, SOURCE + cells - 1 - q)
+            at_early = early is not None and depth < SWEEPS - 1
+            if at_early or q in near_rows[0]:
+                resid.places[(l, q)] = ((early if at_early else near)[2], (l, q - SOURCE))
+    return weight, inverse, resid, steps, shown
+
+
+def own_kernel(cells, loads, self_weight, density, passive, support, base_ref,
+               design_own, stiff, weight_ref, inverse_ref, resid_ref, steps_ref, shown_ref, stiff_wide):
+    masks = inner_masks(density.shape[1:])
+    weight, inverse, resid, steps, shown = Kept(), Kept(), Kept(), Kept(), Kept()
     for i in range(cells):
         design = passive_apply(density[i], passive[i])
-        stiff[DESIGN + i] = stiffness_of(design)
-        free_wide[SOURCE + i] = (1 - support[i]).astype(jnp.float32)
-        design_wide[DESIGN + i] = jnp.where(support[i] == 0, design, -design)
-    for r in range(DESIGN):
-        free = free_wide[r - 1] > 0.5 if r > 0 else zero > 0.5
-        design_wide[r] = jnp.where(free, design_low[r], -design_low[r])
-        q = SOURCE + cells + r
-        free = free_wide[q] > 0.5 if q < rows else zero > 0.5
-        design_wide[DESIGN + cells + r] = jnp.where(free, design_high[r], -design_high[r])
-    for q in range(rows):
-        weight_row(q, free_wide[q] > 0.5, stiff, weight, inverse, masks)
-    first_scale, _ = chebyshev_factors()
-    resid, steps, shown = Kept(), Kept(), Kept()
-    inner = inner_steps(cells)
+        stiffness = stiffness_of(design)
+        stiff[i] = stiffness
+        stiff_wide[DESIGN + i] = stiffness
+        design_own[i] = jnp.where(support[i] == 0, design, -design)
+    inner = inner_steps(cells, 1)
     for q in inner[0]:
-        for l in range(loads):
-            left = inverse[q] * (base_ref[l, q] + self_weight[l] * jnp.abs(design_wide[q + 1]))
-            resid.put((l, q), resid_ref, (l, q - SOURCE), left)
-            steps.put((0, l, q), steps_ref, (0, l, q - SOURCE), first_scale * left)
+        i = q - SOURCE
+        weight_row(q, support[i] == 0, stiff_wide, weight, inverse, weight_ref, inverse_ref, i, masks)
+        base = [base_ref[l, q] for l in range(loads)]
+        start_row(q, base, jnp.abs(design_own[i]), self_weight, inverse, resid, steps, resid_ref, steps_ref, SOURCE)
     for k in range(SWEEPS - 1):
         for q in inner[k + 1]:
             sweep_row(
@@ -278,8 +296,61 @@
             )
 
 
-def first_kernel(cells, loads, self_weight, force_lo, force_hi, base_in, design_wide, weight, inverse,
-                 resid_in, steps_in, shown_in, lo_far, hi_far, keep, spare, outer, rest, tile_ref,
+def early_kernel(cells, loads, self_weight, base_ref, pair_a, pair_b, pair_c, design_own, stiff_own,
+                 near_weight, near_inverse, near_resid, near_steps, near_shown,
+                 design_wide, weight_ref, inverse_ref, resid_ref, steps_ref, shown_ref, stiff):
+    even, is_first, is_last = place_of()
+    shape = design_own.shape[1:]
+    masks = inner_masks(shape)
+    zero = jnp.zeros(shape, jnp.float32)
+    weight, inverse, resid, steps, shown = inner_places(
+        cells, loads, (near_weight, near_inverse, near_resid, near_steps, near_shown), None
+    )
+    for i in range(DESIGN):
+        low = jnp.where(even, pair_a[i], pair_b[i])
+        high = jnp.where(even, pair_b[i], pair_a[i])
+        stiff[i] = jnp.where(is_first, zero, stiffness_of(low))
+        stiff[DESIGN + cells + i] = jnp.where(is_last, zero, stiffness_of(high))
+        below, above = i - 1, i
+        if below >= 0:
+            free = jnp.where(even, pair_a[DESIGN + below], pair_c[below])
+            low = jnp.where((free > 0.5) & jnp.logical_not(is_first), low, -low)
+        else:
+            low = -low
+        if above < SOURCE:
+            free = jnp.where(even, pair_c[above], pair_a[DESIGN + above])
+            high = jnp.where((free > 0.5) & jnp.logical_not(is_last), high, -high)
+        else:
+            high = -high
+        design_wide[i] = low
+        design_wide[DESIGN + cells + i] = high
+    for i in range(cells):
+        design_wide[DESIGN + i] = design_own[i]
+        stiff[DESIGN + i] = stiff_own[i]
+    near, inner = inner_steps(cells, 1), inner_steps(cells, 0)
+    for q in range(cells + 2 * SOURCE):
+        if q not in near[0]:
+            weight_row(
+                q, design_wide[q + 1] > 0.0, stiff, weight, inverse, weight_ref, inverse_ref, outer_place(q, cells), masks
+            )
+    for q in inner[0]:
+        if q not in near[0]:
+            base = [base_ref[l, q] for l in range(loads)]
+            design = jnp.abs(design_wide[q + 1])
+            start_row(q, base, design, self_weight, inverse, resid, steps, resid_ref, steps_ref, SOURCE)
+    for k in range(SWEEPS - 1):
+        for q in inner[k + 1]:
+            if q not in near[k + 1]:
+                sweep_row(
+                    k, q, loads, weight, resid, steps, resid_ref, steps_ref, shown_ref, shown,
+                    SOURCE, SOURCE + SWEEPS - 1,
+                )
+
+
+def first_kernel(cells, loads, self_weight, force_lo, force_hi, base_in, design_wide,
+                 near_weight, near_inverse, near_resid, near_steps, near_shown,
+                 early_weight, early_inverse, early_resid, early_steps, early_shown,
+                 lo_far, hi_far, keep, spare, outer, rest, tile_ref,
                  resid_ref, steps_ref, shown_ref, sense_ref, sems):
     copies = [
         pltpu.make_async_copy(source, target, sems.at[i])
@@ -291,25 +362,16 @@
     shape = design_wide.shape[1:]
     masks = inner_masks(shape)
     rows = cells + 2 * SOURCE
-    first_scale, _ = chebyshev_factors()
-    resid, steps, shown = Kept(), Kept(), Kept()
-    inner = inner_steps(cells)
-    for l in range(loads):
-        for k in range(SWEEPS - 1):
-            for q in inner[k]:
-                steps.places[(k, l, q)] = (steps_in, (k, l, q - SOURCE))
-        for q in inner[0]:
-            resid.places[(l, q)] = (resid_in, (l, q - SOURCE))
-        for q in inner[SWEEPS - 1]:
-            shown.places[(l, q)] = (shown_in, (l, q - SOURCE - (SWEEPS - 1)))
-    for l in range(loads):
-        for q in range(rows):
-            if q in inner[0]:
-                continue
-            base = base_row(l, q, cells, base_in, force_lo, force_hi)
-            left = inverse[q] * (base + self_weight[l] * jnp.abs(design_wide[q + 1]))
-            resid.put((l, q), resid_ref, (l, q), left)
-            steps.put((0, l, q), steps_ref, (0, l, q), first_scale * left)
+    weight, inverse, resid, steps, shown = inner_places(
+        cells, loads, (near_weight, near_inverse, near_resid, near_steps, near_shown),
+        (early_weight, early_inverse, early_resid, early_steps, early_shown),
+    )
+    inner = inner_steps(cells, 0)
+    for q in range(rows):
+        if q not in inner[0]:
+            base = [base_row(l, q, cells, base_in, force_lo, force_hi) for l in range(loads)]
+            design = jnp.abs(design_wide[q + 1])
+            start_row(q, base, design, self_weight, inverse, resid, steps, resid_ref, steps_ref, 0)
     for k in range(SWEEPS - 1):
         for q in range(k + 1, rows - k - 1):
             if q not in inner[k + 1]:
@@ -389,7 +451,7 @@
 def second_kernel(cells, loads, self_weight, step_ref, moment_wide,
                   design_wide, base_far, lo_far, hi_far,
                   shown_ref, design_out, keep, spare, outer, rest, tile_ref,
-                  stiff, weight, inverse, resid_ref, steps_ref, shown_to, design_new,
+                  stiff, weight_ref, inverse_ref, resid_ref, steps_ref, shown_to, design_new,
                   base_in, force_lo, force_hi, sense_ref, sems):
     copies = [
         pltpu.make_async_copy(source, target, sems.at[i])
@@ -420,18 +482,14 @@
             stiff[r] = stiffness
     own_rows = pltpu.make_async_copy(design_new.at[pl.ds(DESIGN, cells)], design_out, sems.at[len(copies) + loads])
     own_rows.start()
-    resid, steps, shown = Kept(), Kept(), Kept()
-    first_scale, _ = chebyshev_factors()
+    weight, inverse, resid, steps, shown = Kept(), Kept(), Kept(), Kept(), Kept()
     for q in range(rows):
-        weight_row(q, design_wide[q + 1] > 0.0, stiff, weight, inverse, masks)
+        weight_row(q, design_wide[q + 1] > 0.0, stiff, weight, inverse, weight_ref, inverse_ref, q, masks)
     for copy in copies:
         copy.wait()
     for q in range(rows):
-        scale, design = inverse[q], design_new[q + 1]
-        for l in range(loads):
-            left = scale * (base_row(l, q, cells, base_in, force_lo, force_hi) + self_weight[l] * design)
-            resid.put((l, q), resid_ref, (l, q), left)
-            steps.put((0, l, q), steps_ref, (0, l, q), first_scale * left)
+        base = [base_row(l, q, cells, base_in, force_lo, force_hi) for l in range(loads)]
+        start_row(q, base, design_new[q + 1], self_weight, inverse, resid, steps, resid_ref, steps_ref, 0)
     for k in range(SWEEPS - 1):
         for q in range(k + 1, rows - k - 1):
             sweep_row(k, q, loads, weight, resid, steps, resid_ref, steps_ref, shown_to, shown)
@@ -616,21 +674,31 @@
         cost=1,
         far_outs=1,
     )
-    pair_a = after(pair_a, base)
+    inner_shapes = [(loads, cells) + plane, (SWEEPS - 1, loads, cells) + plane]
+    design_own, stiff_own, *near = on_core(
+        functools.partial(own_kernel, cells, loads),
+        (self_weight, density, passive, support, base),
+        1,
+        [(cells,) + plane, (cells,) + plane, (6, cells) + plane, (cells,) + plane]
+        + inner_shapes + [(loads, cells - 2 * (SWEEPS - 1)) + plane],
+        [(wide,) + plane],
+        cost=1,
+    )
+    pair_a = after(pair_a, stiff_own)
     pair_b = swap(pair_a[:DESIGN], "load", 1)
     pair_c = swap(pair_a[DESIGN:], "load", 1)
-    design_wide, weight, inverse, resid, steps, shown = on_core(
+    design_wide, *early = on_core(
         functools.partial(early_kernel, cells, loads),
-        (self_weight, density, passive, support, base, pair_a, pair_b, pair_c),
+        (self_weight, base, pair_a, pair_b, pair_c, design_own, stiff_own, *near),
         1,
-        [(wide,) + plane, (6, rows) + plane, (rows,) + plane,
-         (loads, cells) + plane, (SWEEPS - 1, loads, cells) + plane, (loads, cells - 2 * (SWEEPS - 1)) + plane],
-        [(wide,) + plane, (rows,) + plane, (DESIGN,) + plane, (DESIGN,) + plane],
+        [(wide,) + plane, (6, 2 * SOURCE + 2) + plane, (2 * SOURCE + 2,) + plane]
+        + inner_shapes + [(loads, cells - 2 * (SWEEPS - 1)) + plane],
+        [(wide,) + plane],
         cost=1,
     )
     lo_far, hi_far, *parts, tiles = on_core(
         functools.partial(first_kernel, cells, loads),
-        (self_weight, force_lo, force_hi, base, design_wide, weight, inverse, resid, steps, shown),
+        (self_weight, force_lo, force_hi, base, design_wide, *near, *early),
         1,
         [(loads, SOURCE) + plane] * 2 + parts_of(SENSE) + [tile],
         [resid_shape, steps_shape, shown_shape, (cells,) + plane, pltpu.SemaphoreType.DMA((2,))],

time: 75.4 us -> 74.8 us (level)
  local copies, waits for them, and re-layouts: 2.53 us -> 1.4 us
    ppermute x3, waiting for transfers between devices: 9.81 us -> 8.14 us  [both_ways(): return lax.ppermute(value, ('load', 'brick'), pairs)]
    unnamed x14, local copies, waits for them, and re-layouts: 2.5 us -> 1.38 us
    all_to_all x2, waiting for transfers between devices: 7.03 us -> 8.13 us  [meet(): total = totals(lax.all_to_all(tiles, ('load', 'brick'), 0, 0, tiled=True))]
    ppermute x8, starting transfers between devices: 3.16 us -> 2.2 us  [swap(): return lax.ppermute(value, axis, [(i, i ^ bit) for i in range(count)])]
    pallas_call x12 -> x13, Pallas kernels: 25 us -> 25.6 us  [on_core(): pl.pallas_call(kernel, out_shape=[pltpu.HBM(shape, jnp.float32) if i < fa...]
  transfers between devices with their start and end apart: 15 -> 15, of which waited for: 7 -> 7; matrix products, arithmetic and copies ran while one was open for 0% -> 0% of each run, Pallas kernels for 11% -> 12%
where the time goes in v5:
time: 74.8 us; the launch traced here: 74 us
  starting transfers between devices  26.5 us (35%)
  Pallas kernels  25.6 us (34%)
  waiting for transfers between devices  19.4 us (26%)
  local copies, waits for them, and re-layouts  1.4 us (2%)
  between operations  1.11 us (1%)
    pallas_call x13, Pallas kernels, on_core(): pl.pallas_call(kernel, out_shape=[pltpu.HBM(shape, jnp.float32) if i < fa...  25.6 us
    ppermute x3, starting transfers between devices, both_ways(): return lax.ppermute(value, ('load', 'brick'), pairs)  12.8 us
    ppermute x3, waiting for transfers between devices, both_ways(): return lax.ppermute(value, ('load', 'brick'), pairs)  8.14 us
    all_to_all x2, waiting for transfers between devices, meet(): total = totals(lax.all_to_all(tiles, ('load', 'brick'), 0, 0, tiled=True))  8.13 us
    all_to_all x2, starting transfers between devices, meet(): total = totals(lax.all_to_all(tiles, ('load', 'brick'), 0, 0, tiled=True))  6.83 us
    ppermute x2, starting transfers between devices, along(): return lax.ppermute(value, 'brick', pairs)  4.69 us
    ppermute x8, waiting for transfers between devices, swap(): return lax.ppermute(value, axis, [(i, i ^ bit) for i in range(count)])  2.58 us
    ppermute x8, starting transfers between devices, swap(): return lax.ppermute(value, axis, [(i, i ^ bit) for i in range(count)])  2.2 us
  transfers between devices with their start and end apart: 15, of which 7 were waited for; matrix products, arithmetic and copies ran while one was open for 0% of the time, Pallas kernels for 12%

profile of v5, /device:TPU:0, one launch (start us, length us, event | category | flops | bytes accessed | tf_op | source)
XLA Modules:
  0.0 74.0 jit_solution(9491420889869507332)
XLA Ops:
  0.7 1.5 %shard_map.94 = (f32[11,64,128]{2,1,0:T(8,128)S(1)}, f32[2,5,64,128]{3,2,1,0:T(8,128)S(1)}, f32[2,5,64,128]{3,2,1,0:T(8,128)S(1)}) custom-call(f32[12,64,128]{2,1,0:T(8,128)} %density.3, s32[12,64,128]{2,1,0:T(8,128)} %passive_far.1, s32[12,64,128]{2,1,0:T(8,128)} %support.3, f32[2,12,64,128]{3,2,1,0:T(8,128)} %force_ref), custom_call_target="tpu_custom_call" | custom-call | tf_op jit(solution)/shard_map/pallas_call | solution.py:571
  2.2 4.9 %collective-permute-start.2 = (f32[11,64,128]{2,1,0:T(8,128)S(1)}, f32[11,64,128]{2,1,0:T(8,128)S(1)}, u32[]{:S(2)}, u32[]{:S(2)}) collective-permute-start(f32[11,64,128]{2,1,0:T(8,128)S(1)} %get-tuple-element.46), channel_id=1, source_target_pairs={{0,1},{1,2},{2,3},{3,4},{4,5},{5,6},{6,7},{7,8},{8,9},{9,10},{10,1... | collective-permute-start | bytes 1081352 | tf_op jit(solution)/shard_map/ppermute | solution.py:606
  7.1 3.4 %collective-permute-start = (f32[2,5,64,128]{3,2,1,0:T(8,128)S(1)}, f32[2,5,64,128]{3,2,1,0:T(8,128)S(1)}, u32[]{:S(2)}, u32[]{:S(2)}) collective-permute-start(f32[2,5,64,128]{3,2,1,0:T(8,128)S(1)} %get-tuple-element.42), channel_id=1, source_target_pairs={{0,1},{1,2},{2,3},{3,4},{4,5},{5,6},{6,7},{7,8},{8,9},{9,10},{10,1... | collective-permute-start | bytes 983048 | tf_op jit(solution)/shard_map/ppermute | solution.py:597
  10.5 1.3 %collective-permute-start.1 = (f32[2,5,64,128]{3,2,1,0:T(8,128)S(1)}, f32[2,5,64,128]{3,2,1,0:T(8,128)S(1)}, u32[]{:S(2)}, u32[]{:S(2)}) collective-permute-start(f32[2,5,64,128]{3,2,1,0:T(8,128)S(1)} %get-tuple-element.43), channel_id=1, source_target_pairs={{1,0},{2,1},{3,2},{4,3},{5,4},{6,5},{7,6},{8,7},{9,8},{10,9},{11,1... | collective-permute-start | bytes 983048 | tf_op jit(solution)/shard_map/ppermute | solution.py:597
  12.5 0.7 copy-done.6
  13.2 4.0 %shard_map.95 = (f32[2,22,64,128]{3,2,1,0:T(8,128)}, f32[2,22,64,128]{3,2,1,0:T(8,128)S(1)}) custom-call(s32[2,64]{1,0:T(2,128)S(1)} %copy-done.5, f32[2,64]{1,0:T(2,128)S(1)} %copy-done.6, f32[2,12,64,128]{3,2,1,0:T(8,128)S(1)} %copy-done.1), custom_call_target="tpu_custom_call" | custom-call | flops 1 | bytes 1 | tf_op jit(solution)/shard_map/pallas_call | solution.py:571
  17.2 2.2 %shard_map.96 = (f32[12,64,128]{2,1,0:T(8,128)S(1)}, f32[12,64,128]{2,1,0:T(8,128)S(1)}, f32[6,12,64,128]{3,2,1,0:T(8,128)S(1)}, f32[12,64,128]{2,1,0:T(8,128)S(...) custom-call(f32[2]{0:T(128)S(1)} %copy-done.4, ...), custom_call_target="tpu_custom_call" | custom-call | flops 1 | bytes 1 | tf_op jit(solution)/shard_map/pallas_call | solution.py:571
  19.4 6.6 %collective-permute-done.2.pair_a = f32[11,64,128]{2,1,0:T(8,128)S(1)} collective-permute-done((f32[11,64,128]{2,1,0:T(8,128)S(1)}, f32[11,64,128]{2,1,0:T(8,128)S(1)}, u32[]{:S(2)}, u32[]{:S(2)}) %collective-permute-start.2) | collective-permute-done | bytes 360480 | tf_op jit(solution)/shard_map/ppermute | solution.py:606
  26.7 1.1 %collective-permute-done.4.pair_c = f32[5,64,128]{2,1,0:T(8,128)S(1)} collective-permute-done((f32[5,64,128]{2,1,0:T(8,128)S(1)}, f32[5,64,128]{2,1,0:T(8,128)S(1)}, u32[]{:S(2)}, u32[]{:S(2)}) %collective-permute-start.4) | collective-permute-done | bytes 163872 | tf_op jit(solution)/shard_map/ppermute | solution.py:591
  27.8 1.6 %shard_map.97 = (f32[24,64,128]{2,1,0:T(8,128)S(1)}, f32[6,12,64,128]{3,2,1,0:T(8,128)S(1)}, f32[12,64,128]{2,1,0:T(8,128)S(1)}, f32[2,12,64,128]{3,2,1,0:T(8,12...) custom-call(f32[2]{0:T(128)S(1)} %copy-done.4, ...), custom_call_target="tpu_custom_call" | custom-call | flops 1 | bytes 1 | tf_op jit(solution)/shard_map/pallas_call | solution.py:571
  29.9 5.2 %shard_map.98 = (f32[2,5,64,128]{3,2,1,0:T(8,128)}, f32[2,5,64,128]{3,2,1,0:T(8,128)}, f32[7,64,128]{2,1,0:T(8,128)S(1)}, f32[5,64,128]{2,1,0:T(8,128)S(1)}, f32...) custom-call(f32[2]{0:T(128)S(1)} %copy-done.4, ...), custom_call_target="tpu_custom_call" | custom-call | tf_op jit(solution)/shard_map/pallas_call | solution.py:571
  35.2 1.5 %collective-permute-done.5.second = f32[7,64,128]{2,1,0:T(8,128)S(1)} collective-permute-done((f32[7,64,128]{2,1,0:T(8,128)S(1)}, f32[7,64,128]{2,1,0:T(8,128)S(1)}, u32[]{:S(2)}, u32[]{:S(2)}) %collective-permute-start.5) | collective-permute-done | bytes 229408 | tf_op jit(solution)/shard_map/ppermute | solution.py:591
  36.7 4.4 %collective-permute-start.7 = (f32[7,64,128]{2,1,0:T(8,128)S(1)}, f32[7,64,128]{2,1,0:T(8,128)S(1)}, u32[]{:S(2)}, u32[]{:S(2)}) collective-permute-start(f32[7,64,128]{2,1,0:T(8,128)S(1)} %shard_map.100.edge), channel_id=1, source_target_pairs={{0,1},{1,2},{2,3},{3,4},{4,5},{5,6},{6,7},{7,8},{8,9},{9,10},{10,1... | collective-permute-start | bytes 688136 | tf_op jit(solution)/shard_map/ppermute | solution.py:606
  41.1 4.3 %all-to-all-start = ((f32[32,1,256]{2,1,0:T(1,128)}), f32[32,1,256]{2,1,0:T(1,128)S(1)}, u32[]{:S(2)}, u32[]{:S(2)}) async-start(f32[32,1,256]{2,1,0:T(1,128)} %get-tuple-element.61.before), calls=%async_computation | async-start | bytes 65536 | tf_op jit(solution)/shard_map/all_to_all | solution.py:628
  45.4 0.9 %collective-permute-start.8 = (f32[7,64,128]{2,1,0:T(8,128)S(1)}, f32[7,64,128]{2,1,0:T(8,128)S(1)}, u32[]{:S(2)}, u32[]{:S(2)}) collective-permute-start(f32[7,64,128]{2,1,0:T(8,128)S(1)} %collective-permute-done.7.pair_a), channel_id=1, source_target_pairs={{0,16},{16,0},{1,17},{17,1},{2,18},{18,2},{3,19},{19,3},{4,20},{20... | collective-permute-start | bytes 688136 | tf_op jit(solution)/shard_map/ppermute | solution.py:591
  46.3 6.1 %all-to-all-done.tile_in = f32[32,1,256]{2,1,0:T(1,128)S(1)} async-done(((f32[32,1,256]{2,1,0:T(1,128)}), f32[32,1,256]{2,1,0:T(1,128)S(1)}, u32[]{:S(2)}, u32[]{:S(2)}) %all-to-all-start) | async-done | bytes 32800 | tf_op jit(solution)/shard_map/all_to_all | solution.py:628
  52.4 0.9 %shard_map.99.step_ref.before = f32[8,128]{1,0:T(8,128)S(1)} custom-call(f32[32,1,256]{2,1,0:T(1,128)S(1)} %all-to-all-done.tile_in, f32[32,1,256]{2,1,0:T(1,128)} %get-tuple-element.61.before), custom_call_target="tpu_custom_call" | custom-call | flops 2000000000 | bytes 2000000000 | tf_op jit(solution)/shard_map/pallas_call | solution.py:571
  53.8 7.3 %shard_map.102 = (f32[2,12,64,128]{3,2,1,0:T(8,128)}, f32[12,64,128]{2,1,0:T(8,128)}, f32[1,64,128]{2,1,0:T(8,128)S(1)}, f32[11,64,128]{2,1,0:T(8,128)S(1)}, f32...) custom-call(f32[2]{0:T(128)S(1)} %copy-done.4, f32[8,128]{1,0:T(8,128)S(1)} %shard_map.99.step_ref.before, ...), custom_call_target="tpu_custom_call" | custom-call | tf_op jit(solution)/shard_map/pallas_call | solution.py:571
  61.7 2.6 %all-to-all-start.1 = ((f32[32,1,256]{2,1,0:T(1,128)}), f32[32,1,256]{2,1,0:T(1,128)S(1)}, u32[]{:S(2)}, u32[]{:S(2)}) async-start(f32[32,1,256]{2,1,0:T(1,128)} %get-tuple-element.69), calls=%async_computation.1 | async-start | bytes 65536 | tf_op jit(solution)/shard_map/all_to_all | solution.py:628
  64.3 3.5 %collective-permute-start.11 = (f32[1,64,128]{2,1,0:T(8,128)S(1)}, f32[1,64,128]{2,1,0:T(8,128)S(1)}, u32[]{:S(2)}, u32[]{:S(2)}) collective-permute-start(f32[1,64,128]{2,1,0:T(8,128)S(1)} %shard_map.104.edge), channel_id=1, source_target_pairs={{0,1},{1,2},{2,3},{3,4},{4,5},{5,6},{6,7},{7,8},{8,9},{9,10},{10,1... | collective-permute-start | bytes 98312 | tf_op jit(solution)/shard_map/ppermute | solution.py:606
  67.8 1.6 %collective-permute-done.11.pair_a = f32[1,64,128]{2,1,0:T(8,128)S(1)} collective-permute-done((f32[1,64,128]{2,1,0:T(8,128)S(1)}, f32[1,64,128]{2,1,0:T(8,128)S(1)}, u32[]{:S(2)}, u32[]{:S(2)}) %collective-permute-start.11) | collective-permute-done | bytes 32800 | tf_op jit(solution)/shard_map/ppermute | solution.py:606
  69.4 2.0 %all-to-all-done.1.tile_in = f32[32,1,256]{2,1,0:T(1,128)S(1)} async-done(((f32[32,1,256]{2,1,0:T(1,128)}), f32[32,1,256]{2,1,0:T(1,128)S(1)}, u32[]{:S(2)}, u32[]{:S(2)}) %all-to-all-start.1) | async-done | bytes 32800 | tf_op jit(solution)/shard_map/all_to_all | solution.py:628
  71.7 1.4 %shard_map.105 = (f32[12,32,128]{2,1,0:T(8,128)}, f32[12,32,128]{2,1,0:T(8,128)S(1)}, f32[12,32,128]{2,1,0:T(8,128)S(1)}, f32[12,32,128]{2,1,0:T(8,128)S(1)}, f32[12,32,128]{2,1,0:T(8,128)S(1)}) custom-call(f32[1,64,128]{2,1,0:T(8,128)S(1)} %shard_map.104.edge, f32[11,64,128]{2,1,0:T(8,128)S(1)} %get-tuple-element.72.spare, ...), custom_call_target="tpu_custom_call" | custom-call | tf_op jit(solution)/shard_map/pallas_call | solution.py:571
  73.1 0.7 %shard_map.106 = f32[12,32,128]{2,1,0:T(8,128)} custom-call(f32[8,128]{1,0:T(8,128)S(1)} %shard_map.103.step_ref, f32[12,32,128]{2,1,0:T(8,128)S(1)} %get-tuple-element.75.momentum_ref, f32[12,32,128]{2,1,0:T(8,128)S(1)} %get-tuple-element.76.before_ref, f32[12,32,128]{2,1,0:T(8,128)S(1)} %get-tuple-element.77.least_ref, ...), custom_call_target="tpu_custom_call" | custom-call | tf_op jit(solution)/shard_map/pallas_call | solution.py:571
  (35 shorter events, 3.3 us)
Async XLA Ops:
  0.6 16.5 %copy-start = (s32[12,64,128]{2,1,0:T(8,128)S(1)}, s32[12,64,128]{2,1,0:T(8,128)}, u32[]{:S(2)}) copy-start(s32[12,64,128]{2,1,0:T(8,128)} %passive_far.1) | copy-start | bytes 1179652
  0.6 11.2 %copy-start.1 = (f32[2,12,64,128]{3,2,1,0:T(8,128)S(1)}, f32[2,12,64,128]{3,2,1,0:T(8,128)}, u32[]{:S(2)}) copy-start(f32[2,12,64,128]{3,2,1,0:T(8,128)} %force_ref) | copy-start | bytes 2359300
  0.7 16.5 %copy-start.3 = (s32[12,64,128]{2,1,0:T(8,128)S(1)}, s32[12,64,128]{2,1,0:T(8,128)}, u32[]{:S(2)}) copy-start(s32[12,64,128]{2,1,0:T(8,128)} %support.3) | copy-start | bytes 1179652
  0.7 16.5 %copy-start.2 = (f32[12,64,128]{2,1,0:T(8,128)S(1)}, f32[12,64,128]{2,1,0:T(8,128)}, u32[]{:S(2)}) copy-start(f32[12,64,128]{2,1,0:T(8,128)} %density.3) | copy-start | bytes 1179652
  0.7 16.5 %copy-start.4 = (f32[2]{0:T(128)S(1)}, f32[2]{0:T(128)}, u32[]{:S(2)}) copy-start(f32[2]{0:T(128)} %self_weight.7) | copy-start | bytes 28
  2.2 23.8 %collective-permute-start.2 = (f32[11,64,128]{2,1,0:T(8,128)S(1)}, f32[11,64,128]{2,1,0:T(8,128)S(1)}, u32[]{:S(2)}, u32[]{:S(2)}) collective-permute-start(f32[11,64,128]{2,1,0:T(8,128)S(1)} %get-tuple-element.46), channel_id=1, source_target_pairs={{0,1},{1,2},{2,3},{3,4},{4,5},{5,6},{6,7},{7,8},{8,9},{9,10},{10,1... | collective-permute-start | bytes 1081352 | tf_op jit(solution)/shard_map/ppermute | solution.py:606
  7.1 22.8 %collective-permute-start = (f32[2,5,64,128]{3,2,1,0:T(8,128)S(1)}, f32[2,5,64,128]{3,2,1,0:T(8,128)S(1)}, u32[]{:S(2)}, u32[]{:S(2)}) collective-permute-start(f32[2,5,64,128]{3,2,1,0:T(8,128)S(1)} %get-tuple-element.42), channel_id=1, source_target_pairs={{0,1},{1,2},{2,3},{3,4},{4,5},{5,6},{6,7},{7,8},{8,9},{9,10},{10,1... | collective-permute-start | bytes 983048 | tf_op jit(solution)/shard_map/ppermute | solution.py:597
  10.5 19.4 %collective-permute-start.1 = (f32[2,5,64,128]{3,2,1,0:T(8,128)S(1)}, f32[2,5,64,128]{3,2,1,0:T(8,128)S(1)}, u32[]{:S(2)}, u32[]{:S(2)}) collective-permute-start(f32[2,5,64,128]{3,2,1,0:T(8,128)S(1)} %get-tuple-element.43), channel_id=1, source_target_pairs={{1,0},{2,1},{3,2},{4,3},{5,4},{6,5},{7,6},{8,7},{9,8},{10,9},{11,1... | collective-permute-start | bytes 983048 | tf_op jit(solution)/shard_map/ppermute | solution.py:597
  11.8 0.7 copy-start.5
  12.5 0.7 copy-start.6
  26.0 1.7 %collective-permute-start.3 = (f32[6,64,128]{2,1,0:T(8,128)S(1)}, f32[6,64,128]{2,1,0:T(8,128)S(1)}, u32[]{:S(2)}, u32[]{:S(2)}) collective-permute-start(f32[6,64,128]{2,1,0:T(8,128)S(1)} %slice.6), channel_id=1, source_target_pairs={{0,16},{16,0},{1,17},{17,1},{2,18},{18,2},{3,19},{19,3},{4,20},{20... | collective-permute-start | bytes 589832 | tf_op jit(solution)/shard_map/ppermute | solution.py:591
  26.1 1.6 %collective-permute-start.4 = (f32[5,64,128]{2,1,0:T(8,128)S(1)}, f32[5,64,128]{2,1,0:T(8,128)S(1)}, u32[]{:S(2)}, u32[]{:S(2)}) collective-permute-start(f32[5,64,128]{2,1,0:T(8,128)S(1)} %slice.7), channel_id=1, source_target_pairs={{0,16},{16,0},{1,17},{17,1},{2,18},{18,2},{3,19},{19,3},{4,20},{20... | collective-permute-start | bytes 491528 | tf_op jit(solution)/shard_map/ppermute | solution.py:591
  35.1 1.6 %collective-permute-start.5 = (f32[7,64,128]{2,1,0:T(8,128)S(1)}, f32[7,64,128]{2,1,0:T(8,128)S(1)}, u32[]{:S(2)}, u32[]{:S(2)}) collective-permute-start(f32[7,64,128]{2,1,0:T(8,128)S(1)} %get-tuple-element.63), channel_id=1, source_target_pairs={{0,16},{16,0},{1,17},{17,1},{2,18},{18,2},{3,19},{19,3},{4,20},{20... | collective-permute-start | bytes 688136 | tf_op jit(solution)/shard_map/ppermute | solution.py:591
  36.7 8.7 %collective-permute-start.7 = (f32[7,64,128]{2,1,0:T(8,128)S(1)}, f32[7,64,128]{2,1,0:T(8,128)S(1)}, u32[]{:S(2)}, u32[]{:S(2)}) collective-permute-start(f32[7,64,128]{2,1,0:T(8,128)S(1)} %shard_map.100.edge), channel_id=1, source_target_pairs={{0,1},{1,2},{2,3},{3,4},{4,5},{5,6},{6,7},{7,8},{8,9},{9,10},{10,1... | collective-permute-start | bytes 688136 | tf_op jit(solution)/shard_map/ppermute | solution.py:606
  41.1 11.3 %all-to-all-start = ((f32[32,1,256]{2,1,0:T(1,128)}), f32[32,1,256]{2,1,0:T(1,128)S(1)}, u32[]{:S(2)}, u32[]{:S(2)}) async-start(f32[32,1,256]{2,1,0:T(1,128)} %get-tuple-element.61.before), calls=%async_computation | async-start | bytes 65536 | tf_op jit(solution)/shard_map/all_to_all | solution.py:628
  45.4 8.0 %collective-permute-start.8 = (f32[7,64,128]{2,1,0:T(8,128)S(1)}, f32[7,64,128]{2,1,0:T(8,128)S(1)}, u32[]{:S(2)}, u32[]{:S(2)}) collective-permute-start(f32[7,64,128]{2,1,0:T(8,128)S(1)} %collective-permute-done.7.pair_a), channel_id=1, source_target_pairs={{0,16},{16,0},{1,17},{17,1},{2,18},{18,2},{3,19},{19,3},{4,20},{20... | collective-permute-start | bytes 688136 | tf_op jit(solution)/shard_map/ppermute | solution.py:591
  46.3 7.0 %collective-permute-start.6 = (f32[5,64,128]{2,1,0:T(8,128)S(1)}, f32[5,64,128]{2,1,0:T(8,128)S(1)}, u32[]{:S(2)}, u32[]{:S(2)}) collective-permute-start(f32[5,64,128]{2,1,0:T(8,128)S(1)} %get-tuple-element.65), channel_id=1, source_target_pairs={{0,16},{16,0},{1,17},{17,1},{2,18},{18,2},{3,19},{19,3},{4,20},{20... | collective-permute-start | bytes 491528 | tf_op jit(solution)/shard_map/ppermute | solution.py:591
  61.1 10.6 %collective-permute-start.10 = (f32[11,64,128]{2,1,0:T(8,128)S(1)}, f32[11,64,128]{2,1,0:T(8,128)S(1)}, u32[]{:S(2)}, u32[]{:S(2)}) collective-permute-start(f32[11,64,128]{2,1,0:T(8,128)S(1)} %get-tuple-element.73), channel_id=1, source_target_pairs={{0,16},{16,0},{1,17},{17,1},{2,18},{18,2},{3,19},{19,3},{4,20},{20... | collective-permute-start | bytes 1081352 | tf_op jit(solution)/shard_map/ppermute | solution.py:591
  61.2 3.1 %collective-permute-start.9 = (f32[1,64,128]{2,1,0:T(8,128)S(1)}, f32[1,64,128]{2,1,0:T(8,128)S(1)}, u32[]{:S(2)}, u32[]{:S(2)}) collective-permute-start(f32[1,64,128]{2,1,0:T(8,128)S(1)} %get-tuple-element.71), channel_id=1, source_target_pairs={{0,16},{16,0},{1,17},{17,1},{2,18},{18,2},{3,19},{19,3},{4,20},{20... | collective-permute-start | bytes 98312 | tf_op jit(solution)/shard_map/ppermute | solution.py:591
  61.7 9.8 %all-to-all-start.1 = ((f32[32,1,256]{2,1,0:T(1,128)}), f32[32,1,256]{2,1,0:T(1,128)S(1)}, u32[]{:S(2)}, u32[]{:S(2)}) async-start(f32[32,1,256]{2,1,0:T(1,128)} %get-tuple-element.69), calls=%async_computation.1 | async-start | bytes 65536 | tf_op jit(solution)/shard_map/all_to_all | solution.py:628
  64.3 5.1 %collective-permute-start.11 = (f32[1,64,128]{2,1,0:T(8,128)S(1)}, f32[1,64,128]{2,1,0:T(8,128)S(1)}, u32[]{:S(2)}, u32[]{:S(2)}) collective-permute-start(f32[1,64,128]{2,1,0:T(8,128)S(1)} %shard_map.104.edge), channel_id=1, source_target_pairs={{0,1},{1,2},{2,3},{3,4},{4,5},{5,6},{6,7},{7,8},{8,9},{9,10},{10,1... | collective-permute-start | bytes 98312 | tf_op jit(solution)/shard_map/ppermute | solution.py:606
  69.4 2.3 %collective-permute-start.12 = (f32[1,64,128]{2,1,0:T(8,128)S(1)}, f32[1,64,128]{2,1,0:T(8,128)S(1)}, u32[]{:S(2)}, u32[]{:S(2)}) collective-permute-start(f32[1,64,128]{2,1,0:T(8,128)S(1)} %collective-permute-done.11.pair_a), channel_id=1, source_target_pairs={{0,16},{16,0},{1,17},{17,1},{2,18},{18,2},{3,19},{19,3},{4,20},{20... | collective-permute-start | bytes 98312 | tf_op jit(solution)/shard_map/ppermute | solution.py:591

commit v6 on v5

--- a/solution.py
+++ b/solution.py
@@ -350,8 +350,8 @@
 def first_kernel(cells, loads, self_weight, force_lo, force_hi, base_in, design_wide,
                  near_weight, near_inverse, near_resid, near_steps, near_shown,
                  early_weight, early_inverse, early_resid, early_steps, early_shown,
-                 lo_far, hi_far, keep, spare, outer, rest, tile_ref,
-                 resid_ref, steps_ref, shown_ref, sense_ref, sems):
+                 lo_far, hi_far, sense_ref, outer, rest, tile_ref,
+                 resid_ref, steps_ref, shown_ref, sems):
     copies = [
         pltpu.make_async_copy(source, target, sems.at[i])
         for i, (source, target) in enumerate(((force_lo, lo_far), (force_hi, hi_far)))
@@ -378,33 +378,36 @@
                 sweep_row(k, q, loads, weight, resid, steps, resid_ref, steps_ref, shown_ref, shown)
     for i in range(cells):
         sense_ref[i] = energy_row(i, loads, design_wide[DESIGN + i], shown, masks)
-    cut_rows(cells, even, sense_ref, keep, spare, outer, rest)
+    cut_rows(cells, even, sense_ref, outer, rest)
     own = design_wide.at[pl.ds(DESIGN, cells)]
     spread_totals(tile_ref, filter_total(cells, sense_ref, is_first, is_last, masks), fold_rows(cells, own))
     for copy in copies:
         copy.wait()
 
 
-def cut_rows(cells, even, sense, keep, spare, outer, rest):
-    width = keep.shape[0]
+def cut_rows(cells, even, sense, outer, rest):
+    width = outer.shape[0]
     for i in range(width):
-        first, last = sense[i], sense[cells - width + i]
-        keep[i] = jnp.where(even, last, first)
-        outer[i] = jnp.where(even, first, last)
+        outer[i] = jnp.where(even, sense[i], sense[cells - width + i])
     for i in range(cells - width):
-        first, last = sense[i], sense[width + i]
-        spare[i] = jnp.where(even, first, last)
-        rest[i] = jnp.where(even, last, first)
-
-
-def whole_row(i, cells, even, edge, spare, rest):
+        rest[i] = jnp.where(even, sense[width + i], sense[i])
+
+
+def edge_kernel(cells, sense, outer, edge):
+    even, _, _ = place_of()
+    width = outer.shape[0]
+    for i in range(width):
+        edge[i] = jnp.where(even, sense[cells - width + i], sense[i]) + outer[i]
+
+
+def whole_row(i, cells, even, sense, edge, rest):
     width = edge.shape[0]
-    if_even = spare[i] + rest[i] if i < cells - width else edge[i - (cells - width)]
-    if_odd = edge[i] if i < width else spare[i - width] + rest[i - width]
+    if_even = sense[i] + rest[i] if i < cells - width else edge[i - (cells - width)]
+    if_odd = edge[i] if i < width else sense[i] + rest[i - width]
     return jnp.where(even, if_even, if_odd)
 
 
-def moment_kernel(cells, edge, spare, rest, pair_a, pair_b, moment_ref, sense_wide):
+def moment_kernel(cells, sense, edge, rest, pair_a, pair_b, moment_ref, sense_wide):
     even, is_first, is_last = place_of()
     shape = edge.shape[1:]
     masks = inner_masks(shape)
@@ -415,7 +418,7 @@
         sense_wide[i] = jnp.where(is_first, zero, low)
         sense_wide[SENSE + cells + i] = jnp.where(is_last, zero, high)
     for i in range(cells):
-        sense_wide[SENSE + i] = whole_row(i, cells, even, edge, spare, rest)
+        sense_wide[SENSE + i] = whole_row(i, cells, even, sense, edge, rest)
     inside, at_ends = edge_planes(masks)
     for r in range(cells + 2 * DESIGN):
         at_end = (is_first & (r == DESIGN)) | (is_last & (r == DESIGN + cells - 1))
@@ -450,9 +453,9 @@
 
 def second_kernel(cells, loads, self_weight, step_ref, moment_wide,
                   design_wide, base_far, lo_far, hi_far,
-                  shown_ref, design_out, keep, spare, outer, rest, tile_ref,
+                  shown_ref, design_out, sense_ref, outer, rest, tile_ref,
                   stiff, weight_ref, inverse_ref, resid_ref, steps_ref, shown_to, design_new,
-                  base_in, force_lo, force_hi, sense_ref, sems):
+                  base_in, force_lo, force_hi, sems):
     copies = [
         pltpu.make_async_copy(source, target, sems.at[i])
         for i, (source, target) in enumerate(((base_far, base_in), (lo_far, force_lo), (hi_far, force_hi)))
@@ -501,14 +504,14 @@
         copy.start()
     for i in range(cells):
         sense_ref[i] = energy_row(i, loads, design_new[DESIGN + i], shown, masks)
-    cut_rows(cells, even, sense_ref, keep, spare, outer, rest)
+    cut_rows(cells, even, sense_ref, outer, rest)
     own = design_new.at[pl.ds(DESIGN, cells)]
     spread_totals(tile_ref, filter_total(cells, sense_ref, is_first, is_last, masks), fold_rows(cells, own))
     for copy in results + [own_rows]:
         copy.wait()
 
 
-def last_moment_kernel(cells, slab, edge, spare, rest, pair_a, pair_b, moment_wide, design_far, passive_far,
+def last_moment_kernel(cells, slab, sense, edge, rest, pair_a, pair_b, moment_wide, design_far, passive_far,
                        momentum_ref, kept_ref, before_ref, least_ref, most_ref, sense_wide, momentum_all,
                        kinds, sems):
     even, is_first, is_last = place_of()
@@ -525,7 +528,7 @@
     sense_wide[0] = jnp.where(is_first, zero, jnp.where(even, pair_a[0], pair_b[0]))
     sense_wide[cells + 1] = jnp.where(is_last, zero, jnp.where(even, pair_b[0], pair_a[0]))
     for i in range(cells):
-        sense_wide[i + 1] = whole_row(i, cells, even, edge, spare, rest)
+        sense_wide[i + 1] = whole_row(i, cells, even, sense, edge, rest)
     inside, at_ends = edge_planes(masks)
     for i in range(cells):
         scale = inside
@@ -620,20 +623,17 @@
     return lax.optimization_barrier((value, other))[0]
 
 
-def add_kernel(first, second, sum_ref):
-    sum_ref[...] = first[...] + second[...]
-
-
 def meet(parts, tiles, filtered, totals):
     total = totals(lax.all_to_all(tiles, ("load", "brick"), 0, 0, tiled=True))
     for bit in bits_of(lax.axis_size("load"))[1:]:
         parts = [part + swap(part, "load", bit) for part in parts]
-    keep, spare, outer, rest = parts
-    (edge,) = on_core(add_kernel, (keep, swap(outer, "load", 1)), 0, [keep.shape], [])
+    sense, outer, rest = parts
+    outer = swap(outer, "load", 1)
+    (edge,) = on_core(functools.partial(edge_kernel, sense.shape[0]), (sense, outer), 0, [outer.shape], [])
     pair_a = both_ways(edge)
     rest = swap(rest, "load", 1)
     pair_b = swap(pair_a, "load", 1)
-    return filtered(edge, spare, rest, pair_a, pair_b), total
+    return filtered(sense, edge, rest, pair_a, pair_b), total
 
 
 def body(density, passive, support, load_nodes, load_force, self_weight, body_force):
@@ -651,7 +651,7 @@
     steps_shape = (SWEEPS - 1, loads, rows) + plane
 
     def parts_of(width):
-        return [(count,) + plane for count in (width, cells - width, width, cells - width)]
+        return [(count,) + plane for count in (cells, width, cells - width)]
 
     payload, upper, lower = on_core(
         functools.partial(prepare_kernel, cells),
@@ -701,7 +701,7 @@
         (self_weight, force_lo, force_hi, base, design_wide, *near, *early),
         1,
         [(loads, SOURCE) + plane] * 2 + parts_of(SENSE) + [tile],
-        [resid_shape, steps_shape, shown_shape, (cells,) + plane, pltpu.SemaphoreType.DMA((2,))],
+        [resid_shape, steps_shape, shown_shape, pltpu.SemaphoreType.DMA((2,))],
         far_outs=2,
     )
     def totals(decay, before):
@@ -731,7 +731,7 @@
         1,
         [(loads, cells) + plane, (cells,) + plane] + parts_of(1) + [tile],
         [(wide,) + plane, (6, rows) + plane, (rows,) + plane, resid_shape, steps_shape, shown_shape, (wide,) + plane,
-         resid_shape, (loads, SOURCE) + plane, (loads, SOURCE) + plane, (cells,) + plane,
+         resid_shape, (loads, SOURCE) + plane, (loads, SOURCE) + plane,
          pltpu.SemaphoreType.DMA((4 + loads,))],
         limit=14,
         far=3,

time: 74.8 us -> 74.1 us (level)
  no operation moved by 1% of the time
where the time goes in v6:
time: 74.1 us; the launch traced here: 73.2 us
  starting transfers between devices  26.5 us (36%)
  Pallas kernels  24.9 us (34%)
  waiting for transfers between devices  19.3 us (26%)
  local copies, waits for them, and re-layouts  1.4 us (2%)
  between operations  1.11 us (1%)
    pallas_call x13, Pallas kernels, on_core(): pl.pallas_call(kernel, out_shape=[pltpu.HBM(shape, jnp.float32) if i < fa...  24.9 us
    ppermute x3, starting transfers between devices, both_ways(): return lax.ppermute(value, ('load', 'brick'), pairs)  12.8 us
    all_to_all x2, waiting for transfers between devices, meet(): total = totals(lax.all_to_all(tiles, ('load', 'brick'), 0, 0, tiled=True))  8.11 us
    ppermute x3, waiting for transfers between devices, both_ways(): return lax.ppermute(value, ('load', 'brick'), pairs)  8.06 us
    all_to_all x2, starting transfers between devices, meet(): total = totals(lax.all_to_all(tiles, ('load', 'brick'), 0, 0, tiled=True))  6.83 us
    ppermute x2, starting transfers between devices, along(): return lax.ppermute(value, 'brick', pairs)  4.69 us
    ppermute x8, waiting for transfers between devices, swap(): return lax.ppermute(value, axis, [(i, i ^ bit) for i in range(count)])  2.58 us
    ppermute x8, starting transfers between devices, swap(): return lax.ppermute(value, axis, [(i, i ^ bit) for i in range(count)])  2.2 us
  transfers between devices with their start and end apart: 15, of which 7 were waited for; matrix products, arithmetic and copies ran while one was open for 0% of the time, Pallas kernels for 12%

profile of v6, /device:TPU:0, one launch (start us, length us, event | category | flops | bytes accessed | tf_op | source)
XLA Modules:
  0.0 73.2 jit_solution(3503305648540689120)
XLA Ops:
  0.7 1.5 %shard_map.94 = (f32[11,64,128]{2,1,0:T(8,128)S(1)}, f32[2,5,64,128]{3,2,1,0:T(8,128)S(1)}, f32[2,5,64,128]{3,2,1,0:T(8,128)S(1)}) custom-call(f32[12,64,128]{2,1,0:T(8,128)} %density.3, s32[12,64,128]{2,1,0:T(8,128)} %passive_far.1, s32[12,64,128]{2,1,0:T(8,128)} %support.3, f32[2,12,64,128]{3,2,1,0:T(8,128)} %force_ref), custom_call_target="tpu_custom_call" | custom-call | tf_op jit(solution)/shard_map/pallas_call | solution.py:574
  2.2 4.9 %collective-permute-start.2 = (f32[11,64,128]{2,1,0:T(8,128)S(1)}, f32[11,64,128]{2,1,0:T(8,128)S(1)}, u32[]{:S(2)}, u32[]{:S(2)}) collective-permute-start(f32[11,64,128]{2,1,0:T(8,128)S(1)} %get-tuple-element.44), channel_id=1, source_target_pairs={{0,1},{1,2},{2,3},{3,4},{4,5},{5,6},{6,7},{7,8},{8,9},{9,10},{10,1... | collective-permute-start | bytes 1081352 | tf_op jit(solution)/shard_map/ppermute | solution.py:609
  7.1 3.4 %collective-permute-start = (f32[2,5,64,128]{3,2,1,0:T(8,128)S(1)}, f32[2,5,64,128]{3,2,1,0:T(8,128)S(1)}, u32[]{:S(2)}, u32[]{:S(2)}) collective-permute-start(f32[2,5,64,128]{3,2,1,0:T(8,128)S(1)} %get-tuple-element.40), channel_id=1, source_target_pairs={{0,1},{1,2},{2,3},{3,4},{4,5},{5,6},{6,7},{7,8},{8,9},{9,10},{10,1... | collective-permute-start | bytes 983048 | tf_op jit(solution)/shard_map/ppermute | solution.py:600
  10.5 1.3 %collective-permute-start.1 = (f32[2,5,64,128]{3,2,1,0:T(8,128)S(1)}, f32[2,5,64,128]{3,2,1,0:T(8,128)S(1)}, u32[]{:S(2)}, u32[]{:S(2)}) collective-permute-start(f32[2,5,64,128]{3,2,1,0:T(8,128)S(1)} %get-tuple-element.41), channel_id=1, source_target_pairs={{1,0},{2,1},{3,2},{4,3},{5,4},{6,5},{7,6},{8,7},{9,8},{10,9},{11,1... | collective-permute-start | bytes 983048 | tf_op jit(solution)/shard_map/ppermute | solution.py:600
  12.5 0.7 copy-done.6
  13.2 4.1 %shard_map.95 = (f32[2,22,64,128]{3,2,1,0:T(8,128)}, f32[2,22,64,128]{3,2,1,0:T(8,128)S(1)}) custom-call(s32[2,64]{1,0:T(2,128)S(1)} %copy-done.5, f32[2,64]{1,0:T(2,128)S(1)} %copy-done.6, f32[2,12,64,128]{3,2,1,0:T(8,128)S(1)} %copy-done.1), custom_call_target="tpu_custom_call" | custom-call | flops 1 | bytes 1 | tf_op jit(solution)/shard_map/pallas_call | solution.py:574
  17.3 2.2 %shard_map.96 = (f32[12,64,128]{2,1,0:T(8,128)S(1)}, f32[12,64,128]{2,1,0:T(8,128)S(1)}, f32[6,12,64,128]{3,2,1,0:T(8,128)S(1)}, f32[12,64,128]{2,1,0:T(8,128)S(...) custom-call(f32[2]{0:T(128)S(1)} %copy-done.4, ...), custom_call_target="tpu_custom_call" | custom-call | flops 1 | bytes 1 | tf_op jit(solution)/shard_map/pallas_call | solution.py:574
  19.5 6.5 %collective-permute-done.2.pair_a = f32[11,64,128]{2,1,0:T(8,128)S(1)} collective-permute-done((f32[11,64,128]{2,1,0:T(8,128)S(1)}, f32[11,64,128]{2,1,0:T(8,128)S(1)}, u32[]{:S(2)}, u32[]{:S(2)}) %collective-permute-start.2) | collective-permute-done | bytes 360480 | tf_op jit(solution)/shard_map/ppermute | solution.py:609
  26.7 1.1 %collective-permute-done.4.pair_c = f32[5,64,128]{2,1,0:T(8,128)S(1)} collective-permute-done((f32[5,64,128]{2,1,0:T(8,128)S(1)}, f32[5,64,128]{2,1,0:T(8,128)S(1)}, u32[]{:S(2)}, u32[]{:S(2)}) %collective-permute-start.4) | collective-permute-done | bytes 163872 | tf_op jit(solution)/shard_map/ppermute | solution.py:594
  27.8 1.6 %shard_map.97 = (f32[24,64,128]{2,1,0:T(8,128)S(1)}, f32[6,12,64,128]{3,2,1,0:T(8,128)S(1)}, f32[12,64,128]{2,1,0:T(8,128)S(1)}, f32[2,12,64,128]{3,2,1,0:T(8,12...) custom-call(f32[2]{0:T(128)S(1)} %copy-done.4, ...), custom_call_target="tpu_custom_call" | custom-call | flops 1 | bytes 1 | tf_op jit(solution)/shard_map/pallas_call | solution.py:574
  29.9 4.5 %shard_map.98 = (f32[2,5,64,128]{3,2,1,0:T(8,128)}, f32[2,5,64,128]{3,2,1,0:T(8,128)}, f32[12,64,128]{2,1,0:T(8,128)S(1)}, f32[7,64,128]{2,1,0:T(8,128)S(1)}, f3...) custom-call(f32[2]{0:T(128)S(1)} %copy-done.4, f32[2,5,64,128]{3,2,1,0:T(8,128)S(1)} %collective-permute-done.force_lo, ...), custom_call_target="tpu_custom_call" | custom-call | tf_op jit(solution)/shard_map/pallas_call | solution.py:574
  34.5 1.5 %collective-permute-done.5.outer = f32[7,64,128]{2,1,0:T(8,128)S(1)} collective-permute-done((f32[7,64,128]{2,1,0:T(8,128)S(1)}, f32[7,64,128]{2,1,0:T(8,128)S(1)}, u32[]{:S(2)}, u32[]{:S(2)}) %collective-permute-start.5) | collective-permute-done | bytes 229408 | tf_op jit(solution)/shard_map/ppermute | solution.py:594
  36.1 4.4 %collective-permute-start.7 = (f32[7,64,128]{2,1,0:T(8,128)S(1)}, f32[7,64,128]{2,1,0:T(8,128)S(1)}, u32[]{:S(2)}, u32[]{:S(2)}) collective-permute-start(f32[7,64,128]{2,1,0:T(8,128)S(1)} %shard_map.100.edge), channel_id=1, source_target_pairs={{0,1},{1,2},{2,3},{3,4},{4,5},{5,6},{6,7},{7,8},{8,9},{9,10},{10,1... | collective-permute-start | bytes 688136 | tf_op jit(solution)/shard_map/ppermute | solution.py:609
  40.5 4.3 %all-to-all-start = ((f32[32,1,256]{2,1,0:T(1,128)}), f32[32,1,256]{2,1,0:T(1,128)S(1)}, u32[]{:S(2)}, u32[]{:S(2)}) async-start(f32[32,1,256]{2,1,0:T(1,128)} %get-tuple-element.59.before), calls=%async_computation | async-start | bytes 65536 | tf_op jit(solution)/shard_map/all_to_all | solution.py:627
  44.7 0.9 %collective-permute-start.8 = (f32[7,64,128]{2,1,0:T(8,128)S(1)}, f32[7,64,128]{2,1,0:T(8,128)S(1)}, u32[]{:S(2)}, u32[]{:S(2)}) collective-permute-start(f32[7,64,128]{2,1,0:T(8,128)S(1)} %collective-permute-done.7.pair_a), channel_id=1, source_target_pairs={{0,16},{16,0},{1,17},{17,1},{2,18},{18,2},{3,19},{19,3},{4,20},{20... | collective-permute-start | bytes 688136 | tf_op jit(solution)/shard_map/ppermute | solution.py:594
  45.7 6.1 %all-to-all-done.tile_in = f32[32,1,256]{2,1,0:T(1,128)S(1)} async-done(((f32[32,1,256]{2,1,0:T(1,128)}), f32[32,1,256]{2,1,0:T(1,128)S(1)}, u32[]{:S(2)}, u32[]{:S(2)}) %all-to-all-start) | async-done | bytes 32800 | tf_op jit(solution)/shard_map/all_to_all | solution.py:627
  51.8 0.9 %shard_map.99.step_ref.before = f32[8,128]{1,0:T(8,128)S(1)} custom-call(f32[32,1,256]{2,1,0:T(1,128)S(1)} %all-to-all-done.tile_in, f32[32,1,256]{2,1,0:T(1,128)} %get-tuple-element.59.before), custom_call_target="tpu_custom_call" | custom-call | flops 2000000000 | bytes 2000000000 | tf_op jit(solution)/shard_map/pallas_call | solution.py:574
  53.2 7.3 %shard_map.102 = (f32[2,12,64,128]{3,2,1,0:T(8,128)}, f32[12,64,128]{2,1,0:T(8,128)}, f32[12,64,128]{2,1,0:T(8,128)S(1)}, f32[1,64,128]{2,1,0:T(8,128)S(1)}, f32...) custom-call(f32[2]{0:T(128)S(1)} %copy-done.4, f32[8,128]{1,0:T(8,128)S(1)} %shard_map.99.step_ref.before, ...), custom_call_target="tpu_custom_call" | custom-call | tf_op jit(solution)/shard_map/pallas_call | solution.py:574
  61.0 2.6 %all-to-all-start.1 = ((f32[32,1,256]{2,1,0:T(1,128)}), f32[32,1,256]{2,1,0:T(1,128)S(1)}, u32[]{:S(2)}, u32[]{:S(2)}) async-start(f32[32,1,256]{2,1,0:T(1,128)} %get-tuple-element.66), calls=%async_computation.1 | async-start | bytes 65536 | tf_op jit(solution)/shard_map/all_to_all | solution.py:627
  63.7 3.5 %collective-permute-start.11 = (f32[1,64,128]{2,1,0:T(8,128)S(1)}, f32[1,64,128]{2,1,0:T(8,128)S(1)}, u32[]{:S(2)}, u32[]{:S(2)}) collective-permute-start(f32[1,64,128]{2,1,0:T(8,128)S(1)} %shard_map.104.edge), channel_id=1, source_target_pairs={{0,1},{1,2},{2,3},{3,4},{4,5},{5,6},{6,7},{7,8},{8,9},{9,10},{10,1... | collective-permute-start | bytes 98312 | tf_op jit(solution)/shard_map/ppermute | solution.py:609
  67.2 1.6 %collective-permute-done.11.pair_a = f32[1,64,128]{2,1,0:T(8,128)S(1)} collective-permute-done((f32[1,64,128]{2,1,0:T(8,128)S(1)}, f32[1,64,128]{2,1,0:T(8,128)S(1)}, u32[]{:S(2)}, u32[]{:S(2)}) %collective-permute-start.11) | collective-permute-done | bytes 32800 | tf_op jit(solution)/shard_map/ppermute | solution.py:609
  68.8 2.0 %all-to-all-done.1.tile_in = f32[32,1,256]{2,1,0:T(1,128)S(1)} async-done(((f32[32,1,256]{2,1,0:T(1,128)}), f32[32,1,256]{2,1,0:T(1,128)S(1)}, u32[]{:S(2)}, u32[]{:S(2)}) %all-to-all-start.1) | async-done | bytes 32800 | tf_op jit(solution)/shard_map/all_to_all | solution.py:627
  71.1 1.2 %shard_map.105 = (f32[12,32,128]{2,1,0:T(8,128)}, f32[12,32,128]{2,1,0:T(8,128)S(1)}, f32[12,32,128]{2,1,0:T(8,128)S(1)}, f32[12,32,128]{2,1,0:T(8,128)S(1)}, f32[12,32,128]{2,1,0:T(8,128)S(1)}) custom-call(f32[12,64,128]{2,1,0:T(8,128)S(1)} %get-tuple-element.67.sense, f32[1,64,128]{2,1,0:T(8,128)S(1)} %shard_map.104.edge, ...), custom_call_target="tpu_custom_call" | custom-call | tf_op jit(solution)/shard_map/pallas_call | solution.py:574
  72.3 0.7 %shard_map.106 = f32[12,32,128]{2,1,0:T(8,128)} custom-call(f32[8,128]{1,0:T(8,128)S(1)} %shard_map.103.step_ref, f32[12,32,128]{2,1,0:T(8,128)S(1)} %get-tuple-element.71.momentum_ref, f32[12,32,128]{2,1,0:T(8,128)S(1)} %get-tuple-element.72.before_ref, f32[12,32,128]{2,1,0:T(8,128)S(1)} %get-tuple-element.73.least_ref, ...), custom_call_target="tpu_custom_call" | custom-call | tf_op jit(solution)/shard_map/pallas_call | solution.py:574
  (35 shorter events, 3.3 us)
Async XLA Ops:
  0.6 16.6 %copy-start = (s32[12,64,128]{2,1,0:T(8,128)S(1)}, s32[12,64,128]{2,1,0:T(8,128)}, u32[]{:S(2)}) copy-start(s32[12,64,128]{2,1,0:T(8,128)} %passive_far.1) | copy-start | bytes 1179652
  0.6 11.2 %copy-start.1 = (f32[2,12,64,128]{3,2,1,0:T(8,128)S(1)}, f32[2,12,64,128]{3,2,1,0:T(8,128)}, u32[]{:S(2)}) copy-start(f32[2,12,64,128]{3,2,1,0:T(8,128)} %force_ref) | copy-start | bytes 2359300
  0.7 16.6 %copy-start.3 = (s32[12,64,128]{2,1,0:T(8,128)S(1)}, s32[12,64,128]{2,1,0:T(8,128)}, u32[]{:S(2)}) copy-start(s32[12,64,128]{2,1,0:T(8,128)} %support.3) | copy-start | bytes 1179652
  0.7 16.6 %copy-start.2 = (f32[12,64,128]{2,1,0:T(8,128)S(1)}, f32[12,64,128]{2,1,0:T(8,128)}, u32[]{:S(2)}) copy-start(f32[12,64,128]{2,1,0:T(8,128)} %density.3) | copy-start | bytes 1179652
  0.7 16.6 %copy-start.4 = (f32[2]{0:T(128)S(1)}, f32[2]{0:T(128)}, u32[]{:S(2)}) copy-start(f32[2]{0:T(128)} %self_weight.7) | copy-start | bytes 28
  2.2 23.8 %collective-permute-start.2 = (f32[11,64,128]{2,1,0:T(8,128)S(1)}, f32[11,64,128]{2,1,0:T(8,128)S(1)}, u32[]{:S(2)}, u32[]{:S(2)}) collective-permute-start(f32[11,64,128]{2,1,0:T(8,128)S(1)} %get-tuple-element.44), channel_id=1, source_target_pairs={{0,1},{1,2},{2,3},{3,4},{4,5},{5,6},{6,7},{7,8},{8,9},{9,10},{10,1... | collective-permute-start | bytes 1081352 | tf_op jit(solution)/shard_map/ppermute | solution.py:609
  7.1 22.8 %collective-permute-start = (f32[2,5,64,128]{3,2,1,0:T(8,128)S(1)}, f32[2,5,64,128]{3,2,1,0:T(8,128)S(1)}, u32[]{:S(2)}, u32[]{:S(2)}) collective-permute-start(f32[2,5,64,128]{3,2,1,0:T(8,128)S(1)} %get-tuple-element.40), channel_id=1, source_target_pairs={{0,1},{1,2},{2,3},{3,4},{4,5},{5,6},{6,7},{7,8},{8,9},{9,10},{10,1... | collective-permute-start | bytes 983048 | tf_op jit(solution)/shard_map/ppermute | solution.py:600
  10.5 19.4 %collective-permute-start.1 = (f32[2,5,64,128]{3,2,1,0:T(8,128)S(1)}, f32[2,5,64,128]{3,2,1,0:T(8,128)S(1)}, u32[]{:S(2)}, u32[]{:S(2)}) collective-permute-start(f32[2,5,64,128]{3,2,1,0:T(8,128)S(1)} %get-tuple-element.41), channel_id=1, source_target_pairs={{1,0},{2,1},{3,2},{4,3},{5,4},{6,5},{7,6},{8,7},{9,8},{10,9},{11,1... | collective-permute-start | bytes 983048 | tf_op jit(solution)/shard_map/ppermute | solution.py:600
  11.8 0.7 copy-start.5
  12.5 0.7 copy-start.6
  26.0 1.7 %collective-permute-start.3 = (f32[6,64,128]{2,1,0:T(8,128)S(1)}, f32[6,64,128]{2,1,0:T(8,128)S(1)}, u32[]{:S(2)}, u32[]{:S(2)}) collective-permute-start(f32[6,64,128]{2,1,0:T(8,128)S(1)} %slice.6), channel_id=1, source_target_pairs={{0,16},{16,0},{1,17},{17,1},{2,18},{18,2},{3,19},{19,3},{4,20},{20... | collective-permute-start | bytes 589832 | tf_op jit(solution)/shard_map/ppermute | solution.py:594
  26.1 1.6 %collective-permute-start.4 = (f32[5,64,128]{2,1,0:T(8,128)S(1)}, f32[5,64,128]{2,1,0:T(8,128)S(1)}, u32[]{:S(2)}, u32[]{:S(2)}) collective-permute-start(f32[5,64,128]{2,1,0:T(8,128)S(1)} %slice.7), channel_id=1, source_target_pairs={{0,16},{16,0},{1,17},{17,1},{2,18},{18,2},{3,19},{19,3},{4,20},{20... | collective-permute-start | bytes 491528 | tf_op jit(solution)/shard_map/ppermute | solution.py:594
  34.5 1.6 %collective-permute-start.5 = (f32[7,64,128]{2,1,0:T(8,128)S(1)}, f32[7,64,128]{2,1,0:T(8,128)S(1)}, u32[]{:S(2)}, u32[]{:S(2)}) collective-permute-start(f32[7,64,128]{2,1,0:T(8,128)S(1)} %get-tuple-element.61), channel_id=1, source_target_pairs={{0,16},{16,0},{1,17},{17,1},{2,18},{18,2},{3,19},{19,3},{4,20},{20... | collective-permute-start | bytes 688136 | tf_op jit(solution)/shard_map/ppermute | solution.py:594
  36.1 8.7 %collective-permute-start.7 = (f32[7,64,128]{2,1,0:T(8,128)S(1)}, f32[7,64,128]{2,1,0:T(8,128)S(1)}, u32[]{:S(2)}, u32[]{:S(2)}) collective-permute-start(f32[7,64,128]{2,1,0:T(8,128)S(1)} %shard_map.100.edge), channel_id=1, source_target_pairs={{0,1},{1,2},{2,3},{3,4},{4,5},{5,6},{6,7},{7,8},{8,9},{9,10},{10,1... | collective-permute-start | bytes 688136 | tf_op jit(solution)/shard_map/ppermute | solution.py:609
  40.5 11.3 %all-to-all-start = ((f32[32,1,256]{2,1,0:T(1,128)}), f32[32,1,256]{2,1,0:T(1,128)S(1)}, u32[]{:S(2)}, u32[]{:S(2)}) async-start(f32[32,1,256]{2,1,0:T(1,128)} %get-tuple-element.59.before), calls=%async_computation | async-start | bytes 65536 | tf_op jit(solution)/shard_map/all_to_all | solution.py:627
  44.7 8.0 %collective-permute-start.8 = (f32[7,64,128]{2,1,0:T(8,128)S(1)}, f32[7,64,128]{2,1,0:T(8,128)S(1)}, u32[]{:S(2)}, u32[]{:S(2)}) collective-permute-start(f32[7,64,128]{2,1,0:T(8,128)S(1)} %collective-permute-done.7.pair_a), channel_id=1, source_target_pairs={{0,16},{16,0},{1,17},{17,1},{2,18},{18,2},{3,19},{19,3},{4,20},{20... | collective-permute-start | bytes 688136 | tf_op jit(solution)/shard_map/ppermute | solution.py:594
  45.7 7.0 %collective-permute-start.6 = (f32[5,64,128]{2,1,0:T(8,128)S(1)}, f32[5,64,128]{2,1,0:T(8,128)S(1)}, u32[]{:S(2)}, u32[]{:S(2)}) collective-permute-start(f32[5,64,128]{2,1,0:T(8,128)S(1)} %get-tuple-element.62), channel_id=1, source_target_pairs={{0,16},{16,0},{1,17},{17,1},{2,18},{18,2},{3,19},{19,3},{4,20},{20... | collective-permute-start | bytes 491528 | tf_op jit(solution)/shard_map/ppermute | solution.py:594
  60.5 10.6 %collective-permute-start.10 = (f32[11,64,128]{2,1,0:T(8,128)S(1)}, f32[11,64,128]{2,1,0:T(8,128)S(1)}, u32[]{:S(2)}, u32[]{:S(2)}) collective-permute-start(f32[11,64,128]{2,1,0:T(8,128)S(1)} %get-tuple-element.69), channel_id=1, source_target_pairs={{0,16},{16,0},{1,17},{17,1},{2,18},{18,2},{3,19},{19,3},{4,20},{20... | collective-permute-start | bytes 1081352 | tf_op jit(solution)/shard_map/ppermute | solution.py:594
  60.6 3.1 %collective-permute-start.9 = (f32[1,64,128]{2,1,0:T(8,128)S(1)}, f32[1,64,128]{2,1,0:T(8,128)S(1)}, u32[]{:S(2)}, u32[]{:S(2)}) collective-permute-start(f32[1,64,128]{2,1,0:T(8,128)S(1)} %get-tuple-element.68), channel_id=1, source_target_pairs={{0,16},{16,0},{1,17},{17,1},{2,18},{18,2},{3,19},{19,3},{4,20},{20... | collective-permute-start | bytes 98312 | tf_op jit(solution)/shard_map/ppermute | solution.py:594
  61.0 9.8 %all-to-all-start.1 = ((f32[32,1,256]{2,1,0:T(1,128)}), f32[32,1,256]{2,1,0:T(1,128)S(1)}, u32[]{:S(2)}, u32[]{:S(2)}) async-start(f32[32,1,256]{2,1,0:T(1,128)} %get-tuple-element.66), calls=%async_computation.1 | async-start | bytes 65536 | tf_op jit(solution)/shard_map/all_to_all | solution.py:627
  63.7 5.1 %collective-permute-start.11 = (f32[1,64,128]{2,1,0:T(8,128)S(1)}, f32[1,64,128]{2,1,0:T(8,128)S(1)}, u32[]{:S(2)}, u32[]{:S(2)}) collective-permute-start(f32[1,64,128]{2,1,0:T(8,128)S(1)} %shard_map.104.edge), channel_id=1, source_target_pairs={{0,1},{1,2},{2,3},{3,4},{4,5},{5,6},{6,7},{7,8},{8,9},{9,10},{10,1... | collective-permute-start | bytes 98312 | tf_op jit(solution)/shard_map/ppermute | solution.py:609
  68.8 2.2 %collective-permute-start.12 = (f32[1,64,128]{2,1,0:T(8,128)S(1)}, f32[1,64,128]{2,1,0:T(8,128)S(1)}, u32[]{:S(2)}, u32[]{:S(2)}) collective-permute-start(f32[1,64,128]{2,1,0:T(8,128)S(1)} %collective-permute-done.11.pair_a), channel_id=1, source_target_pairs={{0,16},{16,0},{1,17},{17,1},{2,18},{18,2},{3,19},{19,3},{4,20},{20... | collective-permute-start | bytes 98312 | tf_op jit(solution)/shard_map/ppermute | solution.py:594

commit v7 on v6

--- a/solution.py
+++ b/solution.py
@@ -86,7 +86,7 @@
     for plane in around[1:]:
         total = total + plane
     diagonal = (3.0 + mass_shift) * here + 0.5 * total
-    scale = jnp.where(is_free, 1.0 / diagonal, 0.0)
+    scale = jnp.where(is_free, pl.reciprocal(diagonal), 0.0)
     inverse.put(q, inverse_to, place, scale)
     half = 0.5 * scale
     weight.put((0, q), weight_to, (0, place), half * (here + below))
@@ -160,8 +160,7 @@
     return lax.axis_index("load") % 2 == 0, brick == 0, brick == lax.axis_size("brick") - 1
 
 
-def prepare_kernel(cells, density, passive, support, force, payload_ref, upper_ref, lower_ref,
-                   design_rows, kind_rows, hold_rows, sems):
+def prepare_kernel(cells, density, passive, support, payload_ref, design_rows, kind_rows, hold_rows, sems):
     even, _, _ = place_of()
     start = jnp.where(even, cells - DESIGN, 0)
     start_mask = jnp.where(even, cells - SOURCE, 0)
@@ -171,19 +170,26 @@
             (density.at[pl.ds(start, DESIGN)], design_rows),
             (passive.at[pl.ds(start, DESIGN)], kind_rows),
             (support.at[pl.ds(start_mask, SOURCE)], hold_rows),
-            (force.at[:, pl.ds(cells - SOURCE, SOURCE)], upper_ref),
-            (force.at[:, pl.ds(0, SOURCE)], lower_ref),
         ))
     ]
     for copy in copies:
         copy.start()
-    for copy in copies[:3]:
+    for copy in copies:
         copy.wait()
     for i in range(DESIGN):
         payload_ref[i] = passive_apply(design_rows[i], kind_rows[i])
     for i in range(SOURCE):
         payload_ref[DESIGN + i] = (1 - hold_rows[i]).astype(jnp.float32)
-    for copy in copies[3:]:
+
+
+def edges_kernel(cells, force, upper_ref, lower_ref, sems):
+    copies = [
+        pltpu.make_async_copy(force.at[:, pl.ds(cells - SOURCE, SOURCE)], upper_ref, sems.at[0]),
+        pltpu.make_async_copy(force.at[:, pl.ds(0, SOURCE)], lower_ref, sems.at[1]),
+    ]
+    for copy in copies:
+        copy.start()
+    for copy in copies:
         copy.wait()
 
 
@@ -653,14 +659,22 @@
     def parts_of(width):
         return [(count,) + plane for count in (cells, width, cells - width)]
 
-    payload, upper, lower = on_core(
+    (payload,) = on_core(
         functools.partial(prepare_kernel, cells),
-        (density, passive, support, body_force),
+        (density, passive, support),
         0,
-        [(DESIGN + SOURCE,) + plane, (loads, SOURCE) + plane, (loads, SOURCE) + plane],
+        [(DESIGN + SOURCE,) + plane],
         [pltpu.VMEM((DESIGN,) + plane, jnp.float32), pltpu.VMEM((DESIGN,) + plane, jnp.int32),
-         pltpu.VMEM((SOURCE,) + plane, jnp.int32), pltpu.SemaphoreType.DMA((5,))],
-        far=4,
+         pltpu.VMEM((SOURCE,) + plane, jnp.int32), pltpu.SemaphoreType.DMA((3,))],
+        far=3,
+    )
+    upper, lower = on_core(
+        functools.partial(edges_kernel, cells),
+        (after(body_force, payload),),
+        0,
+        [(loads, SOURCE) + plane, (loads, SOURCE) + plane],
+        [pltpu.SemaphoreType.DMA((2,))],
+        far=1,
     )
     pair_a = both_ways(payload)
     force_lo = along(upper, 1)

time: 74.1 us -> 73.9 us (level)
  waiting for transfers between devices: 19.3 us -> 18.2 us
  Pallas kernels: 24.9 us -> 25.8 us
    ppermute x3, waiting for transfers between devices: 8.06 us -> 6.81 us  [both_ways(): return lax.ppermute(value, ('load', 'brick'), pairs)]
    pallas_call x13 -> x14, Pallas kernels: 24.9 us -> 25.8 us  [on_core(): pl.pallas_call(kernel, out_shape=[pltpu.HBM(shape, jnp.float32) if i < fa...]
  transfers between devices with their start and end apart: 15 -> 15, of which waited for: 7 -> 7; matrix products, arithmetic and copies ran while one was open for 0% -> 0% of each run, Pallas kernels for 12% -> 14%
where the time goes in v7:
time: 73.9 us; the launch traced here: 73 us
  starting transfers between devices  26.5 us (36%)
  Pallas kernels  25.8 us (35%)
  waiting for transfers between devices  18.2 us (25%)
  local copies, waits for them, and re-layouts  1.4 us (2%)
  between operations  1.12 us (2%)
    pallas_call x14, Pallas kernels, on_core(): pl.pallas_call(kernel, out_shape=[pltpu.HBM(shape, jnp.float32) if i < fa...  25.8 us
    ppermute x3, starting transfers between devices, both_ways(): return lax.ppermute(value, ('load', 'brick'), pairs)  12.8 us
    all_to_all x2, waiting for transfers between devices, meet(): total = totals(lax.all_to_all(tiles, ('load', 'brick'), 0, 0, tiled=True))  8.11 us
    all_to_all x2, starting transfers between devices, meet(): total = totals(lax.all_to_all(tiles, ('load', 'brick'), 0, 0, tiled=True))  6.83 us
    ppermute x3, waiting for transfers between devices, both_ways(): return lax.ppermute(value, ('load', 'brick'), pairs)  6.81 us
    ppermute x2, starting transfers between devices, along(): return lax.ppermute(value, 'brick', pairs)  4.69 us
    ppermute x8, waiting for transfers between devices, swap(): return lax.ppermute(value, axis, [(i, i ^ bit) for i in range(count)])  2.58 us
    ppermute x8, starting transfers between devices, swap(): return lax.ppermute(value, axis, [(i, i ^ bit) for i in range(count)])  2.2 us
  transfers between devices with their start and end apart: 15, of which 7 were waited for; matrix products, arithmetic and copies ran while one was open for 0% of the time, Pallas kernels for 14%

profile of v7, /device:TPU:0, one launch (start us, length us, event | category | flops | bytes accessed | tf_op | source)
XLA Modules:
  0.0 73.0 jit_solution(6493234789010939712)
XLA Ops:
  0.7 1.3 %shard_map.94 = f32[11,64,128]{2,1,0:T(8,128)S(1)} custom-call(f32[12,64,128]{2,1,0:T(8,128)} %density.3, s32[12,64,128]{2,1,0:T(8,128)} %passive_far.1, s32[12,64,128]{2,1,0:T(8,128)} %support.3), custom_call_target="tpu_custom_call" | custom-call | tf_op jit(solution)/shard_map/pallas_call | solution.py:580
  2.0 4.9 %collective-permute-start.2 = (f32[11,64,128]{2,1,0:T(8,128)S(1)}, f32[11,64,128]{2,1,0:T(8,128)S(1)}, u32[]{:S(2)}, u32[]{:S(2)}) collective-permute-start(f32[11,64,128]{2,1,0:T(8,128)S(1)} %shard_map.94), channel_id=1, source_target_pairs={{0,1},{1,2},{2,3},{3,4},{4,5},{5,6},{6,7},{7,8},{8,9},{9,10},{10,1... | collective-permute-start | bytes 1081352 | tf_op jit(solution)/shard_map/ppermute | solution.py:615
  6.9 1.1 %shard_map.95 = (f32[2,5,64,128]{3,2,1,0:T(8,128)S(1)}, f32[2,5,64,128]{3,2,1,0:T(8,128)S(1)}) custom-call(f32[2,12,64,128]{3,2,1,0:T(8,128)} %force_ref), custom_call_target="tpu_custom_call" | custom-call | tf_op jit(solution)/shard_map/pallas_call | solution.py:580
  8.0 3.4 %collective-permute-start = (f32[2,5,64,128]{3,2,1,0:T(8,128)S(1)}, f32[2,5,64,128]{3,2,1,0:T(8,128)S(1)}, u32[]{:S(2)}, u32[]{:S(2)}) collective-permute-start(f32[2,5,64,128]{3,2,1,0:T(8,128)S(1)} %get-tuple-element.41), channel_id=1, source_target_pairs={{0,1},{1,2},{2,3},{3,4},{4,5},{5,6},{6,7},{7,8},{8,9},{9,10},{10,1... | collective-permute-start | bytes 983048 | tf_op jit(solution)/shard_map/ppermute | solution.py:606
  11.4 1.3 %collective-permute-start.1 = (f32[2,5,64,128]{3,2,1,0:T(8,128)S(1)}, f32[2,5,64,128]{3,2,1,0:T(8,128)S(1)}, u32[]{:S(2)}, u32[]{:S(2)}) collective-permute-start(f32[2,5,64,128]{3,2,1,0:T(8,128)S(1)} %get-tuple-element.42), channel_id=1, source_target_pairs={{1,0},{2,1},{3,2},{4,3},{5,4},{6,5},{7,6},{8,7},{9,8},{10,9},{11,1... | collective-permute-start | bytes 983048 | tf_op jit(solution)/shard_map/ppermute | solution.py:606
  14.1 4.1 %shard_map.96 = (f32[2,22,64,128]{3,2,1,0:T(8,128)}, f32[2,22,64,128]{3,2,1,0:T(8,128)S(1)}) custom-call(s32[2,64]{1,0:T(2,128)S(1)} %copy-done.5, f32[2,64]{1,0:T(2,128)S(1)} %copy-done.6, f32[2,12,64,128]{3,2,1,0:T(8,128)S(1)} %copy-done.1), custom_call_target="tpu_custom_call" | custom-call | flops 1 | bytes 1 | tf_op jit(solution)/shard_map/pallas_call | solution.py:580
  18.2 2.2 %shard_map.97 = (f32[12,64,128]{2,1,0:T(8,128)S(1)}, f32[12,64,128]{2,1,0:T(8,128)S(1)}, f32[6,12,64,128]{3,2,1,0:T(8,128)S(1)}, f32[12,64,128]{2,1,0:T(8,128)S(...) custom-call(f32[2]{0:T(128)S(1)} %copy-done.4, ...), custom_call_target="tpu_custom_call" | custom-call | flops 1 | bytes 1 | tf_op jit(solution)/shard_map/pallas_call | solution.py:580
  20.4 5.2 %collective-permute-done.2.pair_a = f32[11,64,128]{2,1,0:T(8,128)S(1)} collective-permute-done((f32[11,64,128]{2,1,0:T(8,128)S(1)}, f32[11,64,128]{2,1,0:T(8,128)S(1)}, u32[]{:S(2)}, u32[]{:S(2)}) %collective-permute-start.2) | collective-permute-done | bytes 360480 | tf_op jit(solution)/shard_map/ppermute | solution.py:615
  26.3 1.1 %collective-permute-done.4.pair_c = f32[5,64,128]{2,1,0:T(8,128)S(1)} collective-permute-done((f32[5,64,128]{2,1,0:T(8,128)S(1)}, f32[5,64,128]{2,1,0:T(8,128)S(1)}, u32[]{:S(2)}, u32[]{:S(2)}) %collective-permute-start.4) | collective-permute-done | bytes 163872 | tf_op jit(solution)/shard_map/ppermute | solution.py:600
  27.4 1.6 %shard_map.98 = (f32[24,64,128]{2,1,0:T(8,128)S(1)}, f32[6,12,64,128]{3,2,1,0:T(8,128)S(1)}, f32[12,64,128]{2,1,0:T(8,128)S(1)}, f32[2,12,64,128]{3,2,1,0:T(8,12...) custom-call(f32[2]{0:T(128)S(1)} %copy-done.4, ...), custom_call_target="tpu_custom_call" | custom-call | flops 1 | bytes 1 | tf_op jit(solution)/shard_map/pallas_call | solution.py:580
  29.7 4.5 %shard_map.99 = (f32[2,5,64,128]{3,2,1,0:T(8,128)}, f32[2,5,64,128]{3,2,1,0:T(8,128)}, f32[12,64,128]{2,1,0:T(8,128)S(1)}, f32[7,64,128]{2,1,0:T(8,128)S(1)}, f3...) custom-call(f32[2]{0:T(128)S(1)} %copy-done.4, f32[2,5,64,128]{3,2,1,0:T(8,128)S(1)} %collective-permute-done.force_lo, ...), custom_call_target="tpu_custom_call" | custom-call | tf_op jit(solution)/shard_map/pallas_call | solution.py:580
  34.3 1.5 %collective-permute-done.5.outer = f32[7,64,128]{2,1,0:T(8,128)S(1)} collective-permute-done((f32[7,64,128]{2,1,0:T(8,128)S(1)}, f32[7,64,128]{2,1,0:T(8,128)S(1)}, u32[]{:S(2)}, u32[]{:S(2)}) %collective-permute-start.5) | collective-permute-done | bytes 229408 | tf_op jit(solution)/shard_map/ppermute | solution.py:600
  35.9 4.4 %collective-permute-start.7 = (f32[7,64,128]{2,1,0:T(8,128)S(1)}, f32[7,64,128]{2,1,0:T(8,128)S(1)}, u32[]{:S(2)}, u32[]{:S(2)}) collective-permute-start(f32[7,64,128]{2,1,0:T(8,128)S(1)} %shard_map.101.edge), channel_id=1, source_target_pairs={{0,1},{1,2},{2,3},{3,4},{4,5},{5,6},{6,7},{7,8},{8,9},{9,10},{10,1... | collective-permute-start | bytes 688136 | tf_op jit(solution)/shard_map/ppermute | solution.py:615
  40.3 4.3 %all-to-all-start = ((f32[32,1,256]{2,1,0:T(1,128)}), f32[32,1,256]{2,1,0:T(1,128)S(1)}, u32[]{:S(2)}, u32[]{:S(2)}) async-start(f32[32,1,256]{2,1,0:T(1,128)} %get-tuple-element.59.before), calls=%async_computation | async-start | bytes 65536 | tf_op jit(solution)/shard_map/all_to_all | solution.py:633
  44.5 0.9 %collective-permute-start.8 = (f32[7,64,128]{2,1,0:T(8,128)S(1)}, f32[7,64,128]{2,1,0:T(8,128)S(1)}, u32[]{:S(2)}, u32[]{:S(2)}) collective-permute-start(f32[7,64,128]{2,1,0:T(8,128)S(1)} %collective-permute-done.7.pair_a), channel_id=1, source_target_pairs={{0,16},{16,0},{1,17},{17,1},{2,18},{18,2},{3,19},{19,3},{4,20},{20... | collective-permute-start | bytes 688136 | tf_op jit(solution)/shard_map/ppermute | solution.py:600
  45.5 6.1 %all-to-all-done.tile_in = f32[32,1,256]{2,1,0:T(1,128)S(1)} async-done(((f32[32,1,256]{2,1,0:T(1,128)}), f32[32,1,256]{2,1,0:T(1,128)S(1)}, u32[]{:S(2)}, u32[]{:S(2)}) %all-to-all-start) | async-done | bytes 32800 | tf_op jit(solution)/shard_map/all_to_all | solution.py:633
  51.6 0.9 %shard_map.100.step_ref.before = f32[8,128]{1,0:T(8,128)S(1)} custom-call(f32[32,1,256]{2,1,0:T(1,128)S(1)} %all-to-all-done.tile_in, f32[32,1,256]{2,1,0:T(1,128)} %get-tuple-element.59.before), custom_call_target="tpu_custom_call" | custom-call | flops 2000000000 | bytes 2000000000 | tf_op jit(solution)/shard_map/pallas_call | solution.py:580
  53.0 7.3 %shard_map.103 = (f32[2,12,64,128]{3,2,1,0:T(8,128)}, f32[12,64,128]{2,1,0:T(8,128)}, f32[12,64,128]{2,1,0:T(8,128)S(1)}, f32[1,64,128]{2,1,0:T(8,128)S(1)}, f32...) custom-call(f32[2]{0:T(128)S(1)} %copy-done.4, f32[8,128]{1,0:T(8,128)S(1)} %shard_map.100.step_ref.before, ...), custom_call_target="tpu_custom_call" | custom-call | tf_op jit(solution)/shard_map/pallas_call | solution.py:580
  60.8 2.6 %all-to-all-start.1 = ((f32[32,1,256]{2,1,0:T(1,128)}), f32[32,1,256]{2,1,0:T(1,128)S(1)}, u32[]{:S(2)}, u32[]{:S(2)}) async-start(f32[32,1,256]{2,1,0:T(1,128)} %get-tuple-element.66), calls=%async_computation.1 | async-start | bytes 65536 | tf_op jit(solution)/shard_map/all_to_all | solution.py:633
  63.5 3.5 %collective-permute-start.11 = (f32[1,64,128]{2,1,0:T(8,128)S(1)}, f32[1,64,128]{2,1,0:T(8,128)S(1)}, u32[]{:S(2)}, u32[]{:S(2)}) collective-permute-start(f32[1,64,128]{2,1,0:T(8,128)S(1)} %shard_map.105.edge), channel_id=1, source_target_pairs={{0,1},{1,2},{2,3},{3,4},{4,5},{5,6},{6,7},{7,8},{8,9},{9,10},{10,1... | collective-permute-start | bytes 98312 | tf_op jit(solution)/shard_map/ppermute | solution.py:615
  67.0 1.6 %collective-permute-done.11.pair_a = f32[1,64,128]{2,1,0:T(8,128)S(1)} collective-permute-done((f32[1,64,128]{2,1,0:T(8,128)S(1)}, f32[1,64,128]{2,1,0:T(8,128)S(1)}, u32[]{:S(2)}, u32[]{:S(2)}) %collective-permute-start.11) | collective-permute-done | bytes 32800 | tf_op jit(solution)/shard_map/ppermute | solution.py:615
  68.6 2.0 %all-to-all-done.1.tile_in = f32[32,1,256]{2,1,0:T(1,128)S(1)} async-done(((f32[32,1,256]{2,1,0:T(1,128)}), f32[32,1,256]{2,1,0:T(1,128)S(1)}, u32[]{:S(2)}, u32[]{:S(2)}) %all-to-all-start.1) | async-done | bytes 32800 | tf_op jit(solution)/shard_map/all_to_all | solution.py:633
  70.9 1.2 %shard_map.106 = (f32[12,32,128]{2,1,0:T(8,128)}, f32[12,32,128]{2,1,0:T(8,128)S(1)}, f32[12,32,128]{2,1,0:T(8,128)S(1)}, f32[12,32,128]{2,1,0:T(8,128)S(1)}, f32[12,32,128]{2,1,0:T(8,128)S(1)}) custom-call(f32[12,64,128]{2,1,0:T(8,128)S(1)} %get-tuple-element.67.sense, f32[1,64,128]{2,1,0:T(8,128)S(1)} %shard_map.105.edge, ...), custom_call_target="tpu_custom_call" | custom-call | tf_op jit(solution)/shard_map/pallas_call | solution.py:580
  72.1 0.7 %shard_map.107 = f32[12,32,128]{2,1,0:T(8,128)} custom-call(f32[8,128]{1,0:T(8,128)S(1)} %shard_map.104.step_ref, f32[12,32,128]{2,1,0:T(8,128)S(1)} %get-tuple-element.71.momentum_ref, f32[12,32,128]{2,1,0:T(8,128)S(1)} %get-tuple-element.72.before_ref, f32[12,32,128]{2,1,0:T(8,128)S(1)} %get-tuple-element.73.least_ref, ...), custom_call_target="tpu_custom_call" | custom-call | tf_op jit(solution)/shard_map/pallas_call | solution.py:580
  (36 shorter events, 4.1 us)
Async XLA Ops:
  0.6 17.5 %copy-start = (s32[12,64,128]{2,1,0:T(8,128)S(1)}, s32[12,64,128]{2,1,0:T(8,128)}, u32[]{:S(2)}) copy-start(s32[12,64,128]{2,1,0:T(8,128)} %passive_far.1) | copy-start | bytes 1179652
  0.6 17.5 %copy-start.3 = (s32[12,64,128]{2,1,0:T(8,128)S(1)}, s32[12,64,128]{2,1,0:T(8,128)}, u32[]{:S(2)}) copy-start(s32[12,64,128]{2,1,0:T(8,128)} %support.3) | copy-start | bytes 1179652
  0.7 17.5 %copy-start.2 = (f32[12,64,128]{2,1,0:T(8,128)S(1)}, f32[12,64,128]{2,1,0:T(8,128)}, u32[]{:S(2)}) copy-start(f32[12,64,128]{2,1,0:T(8,128)} %density.3) | copy-start | bytes 1179652
  0.7 12.0 %copy-start.1 = (f32[2,12,64,128]{3,2,1,0:T(8,128)S(1)}, f32[2,12,64,128]{3,2,1,0:T(8,128)}, u32[]{:S(2)}) copy-start(f32[2,12,64,128]{3,2,1,0:T(8,128)} %force_ref) | copy-start | bytes 2359300
  0.7 17.5 %copy-start.4 = (f32[2]{0:T(128)S(1)}, f32[2]{0:T(128)}, u32[]{:S(2)}) copy-start(f32[2]{0:T(128)} %self_weight.7) | copy-start | bytes 28
  2.0 23.6 %collective-permute-start.2 = (f32[11,64,128]{2,1,0:T(8,128)S(1)}, f32[11,64,128]{2,1,0:T(8,128)S(1)}, u32[]{:S(2)}, u32[]{:S(2)}) collective-permute-start(f32[11,64,128]{2,1,0:T(8,128)S(1)} %shard_map.94), channel_id=1, source_target_pairs={{0,1},{1,2},{2,3},{3,4},{4,5},{5,6},{6,7},{7,8},{8,9},{9,10},{10,1... | collective-permute-start | bytes 1081352 | tf_op jit(solution)/shard_map/ppermute | solution.py:615
  8.0 21.7 %collective-permute-start = (f32[2,5,64,128]{3,2,1,0:T(8,128)S(1)}, f32[2,5,64,128]{3,2,1,0:T(8,128)S(1)}, u32[]{:S(2)}, u32[]{:S(2)}) collective-permute-start(f32[2,5,64,128]{3,2,1,0:T(8,128)S(1)} %get-tuple-element.41), channel_id=1, source_target_pairs={{0,1},{1,2},{2,3},{3,4},{4,5},{5,6},{6,7},{7,8},{8,9},{9,10},{10,1... | collective-permute-start | bytes 983048 | tf_op jit(solution)/shard_map/ppermute | solution.py:606
  11.4 18.3 %collective-permute-start.1 = (f32[2,5,64,128]{3,2,1,0:T(8,128)S(1)}, f32[2,5,64,128]{3,2,1,0:T(8,128)S(1)}, u32[]{:S(2)}, u32[]{:S(2)}) collective-permute-start(f32[2,5,64,128]{3,2,1,0:T(8,128)S(1)} %get-tuple-element.42), channel_id=1, source_target_pairs={{1,0},{2,1},{3,2},{4,3},{5,4},{6,5},{7,6},{8,7},{9,8},{10,9},{11,1... | collective-permute-start | bytes 983048 | tf_op jit(solution)/shard_map/ppermute | solution.py:606
  12.7 0.7 copy-start.5
  13.4 0.7 copy-start.6
  25.7 1.7 %collective-permute-start.3 = (f32[6,64,128]{2,1,0:T(8,128)S(1)}, f32[6,64,128]{2,1,0:T(8,128)S(1)}, u32[]{:S(2)}, u32[]{:S(2)}) collective-permute-start(f32[6,64,128]{2,1,0:T(8,128)S(1)} %slice.6), channel_id=1, source_target_pairs={{0,16},{16,0},{1,17},{17,1},{2,18},{18,2},{3,19},{19,3},{4,20},{20... | collective-permute-start | bytes 589832 | tf_op jit(solution)/shard_map/ppermute | solution.py:600
  25.8 1.6 %collective-permute-start.4 = (f32[5,64,128]{2,1,0:T(8,128)S(1)}, f32[5,64,128]{2,1,0:T(8,128)S(1)}, u32[]{:S(2)}, u32[]{:S(2)}) collective-permute-start(f32[5,64,128]{2,1,0:T(8,128)S(1)} %slice.7), channel_id=1, source_target_pairs={{0,16},{16,0},{1,17},{17,1},{2,18},{18,2},{3,19},{19,3},{4,20},{20... | collective-permute-start | bytes 491528 | tf_op jit(solution)/shard_map/ppermute | solution.py:600
  34.3 1.6 %collective-permute-start.5 = (f32[7,64,128]{2,1,0:T(8,128)S(1)}, f32[7,64,128]{2,1,0:T(8,128)S(1)}, u32[]{:S(2)}, u32[]{:S(2)}) collective-permute-start(f32[7,64,128]{2,1,0:T(8,128)S(1)} %get-tuple-element.61), channel_id=1, source_target_pairs={{0,16},{16,0},{1,17},{17,1},{2,18},{18,2},{3,19},{19,3},{4,20},{20... | collective-permute-start | bytes 688136 | tf_op jit(solution)/shard_map/ppermute | solution.py:600
  35.9 8.7 %collective-permute-start.7 = (f32[7,64,128]{2,1,0:T(8,128)S(1)}, f32[7,64,128]{2,1,0:T(8,128)S(1)}, u32[]{:S(2)}, u32[]{:S(2)}) collective-permute-start(f32[7,64,128]{2,1,0:T(8,128)S(1)} %shard_map.101.edge), channel_id=1, source_target_pairs={{0,1},{1,2},{2,3},{3,4},{4,5},{5,6},{6,7},{7,8},{8,9},{9,10},{10,1... | collective-permute-start | bytes 688136 | tf_op jit(solution)/shard_map/ppermute | solution.py:615
  40.3 11.3 %all-to-all-start = ((f32[32,1,256]{2,1,0:T(1,128)}), f32[32,1,256]{2,1,0:T(1,128)S(1)}, u32[]{:S(2)}, u32[]{:S(2)}) async-start(f32[32,1,256]{2,1,0:T(1,128)} %get-tuple-element.59.before), calls=%async_computation | async-start | bytes 65536 | tf_op jit(solution)/shard_map/all_to_all | solution.py:633
  44.5 8.0 %collective-permute-start.8 = (f32[7,64,128]{2,1,0:T(8,128)S(1)}, f32[7,64,128]{2,1,0:T(8,128)S(1)}, u32[]{:S(2)}, u32[]{:S(2)}) collective-permute-start(f32[7,64,128]{2,1,0:T(8,128)S(1)} %collective-permute-done.7.pair_a), channel_id=1, source_target_pairs={{0,16},{16,0},{1,17},{17,1},{2,18},{18,2},{3,19},{19,3},{4,20},{20... | collective-permute-start | bytes 688136 | tf_op jit(solution)/shard_map/ppermute | solution.py:600
  45.5 7.0 %collective-permute-start.6 = (f32[5,64,128]{2,1,0:T(8,128)S(1)}, f32[5,64,128]{2,1,0:T(8,128)S(1)}, u32[]{:S(2)}, u32[]{:S(2)}) collective-permute-start(f32[5,64,128]{2,1,0:T(8,128)S(1)} %get-tuple-element.62), channel_id=1, source_target_pairs={{0,16},{16,0},{1,17},{17,1},{2,18},{18,2},{3,19},{19,3},{4,20},{20... | collective-permute-start | bytes 491528 | tf_op jit(solution)/shard_map/ppermute | solution.py:600
  60.3 10.6 %collective-permute-start.10 = (f32[11,64,128]{2,1,0:T(8,128)S(1)}, f32[11,64,128]{2,1,0:T(8,128)S(1)}, u32[]{:S(2)}, u32[]{:S(2)}) collective-permute-start(f32[11,64,128]{2,1,0:T(8,128)S(1)} %get-tuple-element.69), channel_id=1, source_target_pairs={{0,16},{16,0},{1,17},{17,1},{2,18},{18,2},{3,19},{19,3},{4,20},{20... | collective-permute-start | bytes 1081352 | tf_op jit(solution)/shard_map/ppermute | solution.py:600
  60.3 3.1 %collective-permute-start.9 = (f32[1,64,128]{2,1,0:T(8,128)S(1)}, f32[1,64,128]{2,1,0:T(8,128)S(1)}, u32[]{:S(2)}, u32[]{:S(2)}) collective-permute-start(f32[1,64,128]{2,1,0:T(8,128)S(1)} %get-tuple-element.68), channel_id=1, source_target_pairs={{0,16},{16,0},{1,17},{17,1},{2,18},{18,2},{3,19},{19,3},{4,20},{20... | collective-permute-start | bytes 98312 | tf_op jit(solution)/shard_map/ppermute | solution.py:600
  60.8 9.8 %all-to-all-start.1 = ((f32[32,1,256]{2,1,0:T(1,128)}), f32[32,1,256]{2,1,0:T(1,128)S(1)}, u32[]{:S(2)}, u32[]{:S(2)}) async-start(f32[32,1,256]{2,1,0:T(1,128)} %get-tuple-element.66), calls=%async_computation.1 | async-start | bytes 65536 | tf_op jit(solution)/shard_map/all_to_all | solution.py:633
  63.5 5.1 %collective-permute-start.11 = (f32[1,64,128]{2,1,0:T(8,128)S(1)}, f32[1,64,128]{2,1,0:T(8,128)S(1)}, u32[]{:S(2)}, u32[]{:S(2)}) collective-permute-start(f32[1,64,128]{2,1,0:T(8,128)S(1)} %shard_map.105.edge), channel_id=1, source_target_pairs={{0,1},{1,2},{2,3},{3,4},{4,5},{5,6},{6,7},{7,8},{8,9},{9,10},{10,1... | collective-permute-start | bytes 98312 | tf_op jit(solution)/shard_map/ppermute | solution.py:615
  68.6 2.2 %collective-permute-start.12 = (f32[1,64,128]{2,1,0:T(8,128)S(1)}, f32[1,64,128]{2,1,0:T(8,128)S(1)}, u32[]{:S(2)}, u32[]{:S(2)}) collective-permute-start(f32[1,64,128]{2,1,0:T(8,128)S(1)} %collective-permute-done.11.pair_a), channel_id=1, source_target_pairs={{0,16},{16,0},{1,17},{17,1},{2,18},{18,2},{3,19},{19,3},{4,20},{20... | collective-permute-start | bytes 98312 | tf_op jit(solution)/shard_map/ppermute | solution.py:600
